TPU v7x, 256 devices: a whole 4x4x8 slice. The times are simulated.
256 devices in a mesh: ctx: 32 (over z, x_lo, core), head: 8 (over y, x_hi).
Axes of the slice: x: 4 (x_hi: 2, x_lo: 2; x = x_hi * 2 + x_lo), y: 4, z: 8, core: 2. Of those that a mesh axis runs over, the one named last changes fastest.
Arguments:
- queries: bfloat16 [8192, 8192], P('ctx', 'head'), may hold values from -6.5 to 6.5
- keys: bfloat16 [8192, 1024], P('ctx', 'head'), may hold values from -6.5 to 6.5
- values: bfloat16 [8192, 1024], P('ctx', 'head'), may hold values from -6 to 6
- doc_lengths: int32 [8], replicated, may hold values from 1 to 4096, 8192 in all
- out_weight: bfloat16 [8192, 4096], P(None, 'head'), may hold values from -0.0625 to 0.0625
Outputs:
- projected: bfloat16 [8192, 4096], P('ctx', 'head')
Inputs may be any that keep to these rules, and one draw needn't show every extreme that they name: `doc_lengths`: the lengths sum to 8192; the longest document has exactly 4096 tokens.
All inputs are finite; a program needn't handle non-finite values.
Results may differ from a plain program's by a relative error of at most 0.009.
Values may be sent and summed in bfloat16 or wider, within the bound.
No kernel may reach another device: no remote copies, remote signals or barrier semaphores. Data moves between devices by JAX's collectives and lax.ppermute only.
A program may use at most 64 MiB of HBM per device.

v0:
```python
import math

import jax
import jax.numpy as jnp
from jax import lax
from jax.sharding import PartitionSpec as P

HEAD_DIM = 128
GROUP = 8


LOW_SCORE = -1e30


def passed_along(value, axis, steps):
    count = lax.axis_size(axis)
    leading, last = (max(0, -steps), min(count, count - steps))
    return lax.ppermute(value, axis, [(source, source + steps) for source in range(leading, last)])


def doc_numbers(doc_ends, positions):
    return jnp.sum((doc_ends[None, :] <= positions[:, None]).astype(jnp.int32), axis=1)


def local(queries, keys, values, doc_lengths, out_weight):
    tok_rows = queries.shape[0]
    groups = keys.shape[1] // HEAD_DIM
    cycle_size = lax.axis_size("ctx")
    my_index = lax.axis_index("ctx")
    score_scale = 1.0 / math.sqrt(HEAD_DIM)
    folded = (
        queries.reshape(tok_rows, groups, GROUP, HEAD_DIM)
        .transpose(1, 2, 0, 3)
        .reshape(groups, GROUP * tok_rows, HEAD_DIM)
    )
    doc_ends = jnp.cumsum(doc_lengths)
    first_row = my_index * tok_rows
    query_pos = first_row + jnp.arange(tok_rows, dtype=jnp.int32)
    query_doc = doc_numbers(doc_ends, query_pos)
    paired = jnp.stack([keys, values])
    initial = (
        jnp.full((groups, GROUP * tok_rows), LOW_SCORE, jnp.float32),
        jnp.zeros((groups, GROUP * tok_rows), jnp.float32),
        jnp.zeros((groups, GROUP * tok_rows, HEAD_DIM), jnp.float32),
    )

    def attend(softmax_state, kv_block, begin_at):
        key_count = kv_block.shape[1]
        key_pos = begin_at + jnp.arange(key_count, dtype=jnp.int32)
        key_doc = doc_numbers(doc_ends, key_pos)
        allowed = (key_pos[None, :] <= query_pos[:, None]) & (
            key_doc[None, :] == query_doc[:, None]
        )
        allowed = jnp.tile(allowed, (GROUP, 1))
        key_tile = kv_block[0].reshape(key_count, groups, HEAD_DIM)
        value_tile = kv_block[1].reshape(key_count, groups, HEAD_DIM)
        scores = (
            jnp.einsum("gqd,kgd->gqk", folded, key_tile, preferred_element_type=jnp.float32)
            * score_scale
        )
        scores = jnp.where(allowed[None], scores, LOW_SCORE)
        row_max, row_sums, weighted = softmax_state
        new_max = jnp.maximum(row_max, jnp.max(scores, axis=-1))
        exp_scores = jnp.where(allowed[None], jnp.exp(scores - new_max[..., None]), 0.0)
        shrink = jnp.exp(row_max - new_max)
        row_sums = row_sums * shrink + jnp.sum(exp_scores, axis=-1)
        weighted = weighted * shrink[..., None] + jnp.einsum(
            "gqk,kgd->gqd",
            exp_scores.astype(jnp.bfloat16),
            value_tile,
            preferred_element_type=jnp.float32,
        )
        return (new_max, row_sums, weighted)

    def visit_block(softmax_state, kv_block, begin_at):
        masked_out = begin_at > first_row + tok_rows - 1
        return lax.cond(
            masked_out,
            lambda current: current,
            lambda current: attend(current, kv_block, begin_at),
            softmax_state,
        )

    def hop_step(hop_index, running):
        softmax_state, kv_block = running
        source = (my_index - hop_index) % cycle_size
        softmax_state = visit_block(softmax_state, kv_block, source * tok_rows)
        kv_block = passed_along(kv_block, "ctx", 1)
        return (softmax_state, kv_block)

    softmax_state, kv_block = lax.fori_loop(0, cycle_size - 1, hop_step, (initial, paired))
    last_source = (my_index - (cycle_size - 1)) % cycle_size
    softmax_state = visit_block(softmax_state, kv_block, last_source * tok_rows)
    row_max, row_sums, weighted = softmax_state
    head_outs = (weighted / row_sums[..., None]).reshape(groups, GROUP, tok_rows, HEAD_DIM)
    head_outs = (
        head_outs.transpose(2, 0, 1, 3)
        .reshape(tok_rows, groups * GROUP * HEAD_DIM)
        .astype(jnp.bfloat16)
    )
    projected = jnp.dot(
        lax.all_gather(head_outs, "head", axis=1, tiled=True),
        out_weight,
        preferred_element_type=jnp.float32,
    )
    return projected.astype(jnp.bfloat16)


def solution(mesh):
    placed = (P("ctx", "head"), P("ctx", "head"), P("ctx", "head"), P(), P(None, "head"))
    return jax.shard_map(
        local, mesh=mesh, in_specs=placed, out_specs=P("ctx", "head"), check_vma=False
    )
```

profile of v0, /device:TPU:98, one launch (start us, length us, event | category | flops | bytes accessed | tf_op | source)
XLA Modules:
  0.0 389.1 jit_solution(2568431028546470253)
XLA Ops:
  8.9 280.0 %while.22 = (s32[]{:T(128)}, f32[1,2048]{1,0:T(1,128)S(1)}, f32[1,2048]{1,0:T(1,128)S(1)}, f32[1,2048,128]{2,1,0:T(8,128)S(1)}, bf16[2,256,128]{2,1,0:T(8,128)(2...) while((s32[]{:T(128)}, f32[1,2048]{1,0:T(1,128)S(1)}, ...), condition=%wide.region_8.9_spmd.clone, body=%wide.region_2.8_spmd.clone.sunk | while | flops 273885440 | bytes 13249016 | solution.py:91
  9.5 1.9 collective-permute-start
  11.5 4.6 %conditional.5 = (f32[1,2048]{1,0:T(1,128)S(1)}, f32[1,2048]{1,0:T(1,128)S(1)}, f32[1,2048,128]{2,1,0:T(8,128)S(1)}) conditional(s32[]{:T(128)} %convert_element_type.63, (s32[]{:T(128)}, s32[]{:T(128)}, s32[8]{0:T(128)S(1)}, s32[256]{0:T(256)S(1)}, bf16[1,2048,128]{2,1,0:T(8,128)(2,1)S(1)}, /*index=5*/bf16[2,256,128]{2,1,0:T(8,128)(2,1)}, ...), branch_computations={%region_3.6_spmd, %region_7.7_spmd} | conditional | flops 273885440 | bytes 12444736 | solution.py:77
  14.2 1.8 fusion.3
  16.8 5.1 %collective-permute-start = (bf16[2,256,128]{2,1,0:T(8,128)(2,1)}, bf16[2,256,128]{2,1,0:T(8,128)(2,1)S(1)}, u32[]{:S(2)}, u32[]{:S(2)}) collective-permute-start(bf16[2,256,128]{2,1,0:T(8,128)(2,1)} %copy.30), channel_id=1, source_target_pairs={{0,8},{8,16},{16,24},{24,32},{32,40},{40,48},{48,56},{56,64},{64,7... | collective-permute-start | bytes 393224 | tf_op jit(solution)/shard_map/while/body/eval_jaxpr/ppermute | solution.py:18
  21.9 4.6 %conditional.5 = (f32[1,2048]{1,0:T(1,128)S(1)}, f32[1,2048]{1,0:T(1,128)S(1)}, f32[1,2048,128]{2,1,0:T(8,128)S(1)}) conditional(s32[]{:T(128)} %convert_element_type.63, (s32[]{:T(128)}, s32[]{:T(128)}, s32[8]{0:T(128)S(1)}, s32[256]{0:T(256)S(1)}, bf16[1,2048,128]{2,1,0:T(8,128)(2,1)S(1)}, /*index=5*/bf16[2,256,128]{2,1,0:T(8,128)(2,1)}, ...), branch_computations={%region_3.6_spmd, %region_7.7_spmd} | conditional | flops 273885440 | bytes 12444736 | solution.py:77
  24.7 1.8 fusion.3
  27.2 3.9 %collective-permute-start = (bf16[2,256,128]{2,1,0:T(8,128)(2,1)}, bf16[2,256,128]{2,1,0:T(8,128)(2,1)S(1)}, u32[]{:S(2)}, u32[]{:S(2)}) collective-permute-start(bf16[2,256,128]{2,1,0:T(8,128)(2,1)} %copy.30), channel_id=1, source_target_pairs={{0,8},{8,16},{16,24},{24,32},{32,40},{40,48},{48,56},{56,64},{64,7... | collective-permute-start | bytes 393224 | tf_op jit(solution)/shard_map/while/body/eval_jaxpr/ppermute | solution.py:18
  31.2 4.6 %conditional.5 = (f32[1,2048]{1,0:T(1,128)S(1)}, f32[1,2048]{1,0:T(1,128)S(1)}, f32[1,2048,128]{2,1,0:T(8,128)S(1)}) conditional(s32[]{:T(128)} %convert_element_type.63, (s32[]{:T(128)}, s32[]{:T(128)}, s32[8]{0:T(128)S(1)}, s32[256]{0:T(256)S(1)}, bf16[1,2048,128]{2,1,0:T(8,128)(2,1)S(1)}, /*index=5*/bf16[2,256,128]{2,1,0:T(8,128)(2,1)}, ...), branch_computations={%region_3.6_spmd, %region_7.7_spmd} | conditional | flops 273885440 | bytes 12444736 | solution.py:77
  33.9 1.8 fusion.3
  36.5 3.9 %collective-permute-start = (bf16[2,256,128]{2,1,0:T(8,128)(2,1)}, bf16[2,256,128]{2,1,0:T(8,128)(2,1)S(1)}, u32[]{:S(2)}, u32[]{:S(2)}) collective-permute-start(bf16[2,256,128]{2,1,0:T(8,128)(2,1)} %copy.30), channel_id=1, source_target_pairs={{0,8},{8,16},{16,24},{24,32},{32,40},{40,48},{48,56},{56,64},{64,7... | collective-permute-start | bytes 393224 | tf_op jit(solution)/shard_map/while/body/eval_jaxpr/ppermute | solution.py:18
  40.4 4.6 %conditional.5 = (f32[1,2048]{1,0:T(1,128)S(1)}, f32[1,2048]{1,0:T(1,128)S(1)}, f32[1,2048,128]{2,1,0:T(8,128)S(1)}) conditional(s32[]{:T(128)} %convert_element_type.63, (s32[]{:T(128)}, s32[]{:T(128)}, s32[8]{0:T(128)S(1)}, s32[256]{0:T(256)S(1)}, bf16[1,2048,128]{2,1,0:T(8,128)(2,1)S(1)}, /*index=5*/bf16[2,256,128]{2,1,0:T(8,128)(2,1)}, ...), branch_computations={%region_3.6_spmd, %region_7.7_spmd} | conditional | flops 273885440 | bytes 12444736 | solution.py:77
  43.2 1.8 fusion.3
  45.7 3.9 %collective-permute-start = (bf16[2,256,128]{2,1,0:T(8,128)(2,1)}, bf16[2,256,128]{2,1,0:T(8,128)(2,1)S(1)}, u32[]{:S(2)}, u32[]{:S(2)}) collective-permute-start(bf16[2,256,128]{2,1,0:T(8,128)(2,1)} %copy.30), channel_id=1, source_target_pairs={{0,8},{8,16},{16,24},{24,32},{32,40},{40,48},{48,56},{56,64},{64,7... | collective-permute-start | bytes 393224 | tf_op jit(solution)/shard_map/while/body/eval_jaxpr/ppermute | solution.py:18
  49.7 4.6 %conditional.5 = (f32[1,2048]{1,0:T(1,128)S(1)}, f32[1,2048]{1,0:T(1,128)S(1)}, f32[1,2048,128]{2,1,0:T(8,128)S(1)}) conditional(s32[]{:T(128)} %convert_element_type.63, (s32[]{:T(128)}, s32[]{:T(128)}, s32[8]{0:T(128)S(1)}, s32[256]{0:T(256)S(1)}, bf16[1,2048,128]{2,1,0:T(8,128)(2,1)S(1)}, /*index=5*/bf16[2,256,128]{2,1,0:T(8,128)(2,1)}, ...), branch_computations={%region_3.6_spmd, %region_7.7_spmd} | conditional | flops 273885440 | bytes 12444736 | solution.py:77
  52.4 1.8 fusion.3
  55.0 3.9 %collective-permute-start = (bf16[2,256,128]{2,1,0:T(8,128)(2,1)}, bf16[2,256,128]{2,1,0:T(8,128)(2,1)S(1)}, u32[]{:S(2)}, u32[]{:S(2)}) collective-permute-start(bf16[2,256,128]{2,1,0:T(8,128)(2,1)} %copy.30), channel_id=1, source_target_pairs={{0,8},{8,16},{16,24},{24,32},{32,40},{40,48},{48,56},{56,64},{64,7... | collective-permute-start | bytes 393224 | tf_op jit(solution)/shard_map/while/body/eval_jaxpr/ppermute | solution.py:18
  58.9 4.6 %conditional.5 = (f32[1,2048]{1,0:T(1,128)S(1)}, f32[1,2048]{1,0:T(1,128)S(1)}, f32[1,2048,128]{2,1,0:T(8,128)S(1)}) conditional(s32[]{:T(128)} %convert_element_type.63, (s32[]{:T(128)}, s32[]{:T(128)}, s32[8]{0:T(128)S(1)}, s32[256]{0:T(256)S(1)}, bf16[1,2048,128]{2,1,0:T(8,128)(2,1)S(1)}, /*index=5*/bf16[2,256,128]{2,1,0:T(8,128)(2,1)}, ...), branch_computations={%region_3.6_spmd, %region_7.7_spmd} | conditional | flops 273885440 | bytes 12444736 | solution.py:77
  61.7 1.8 fusion.3
  64.2 3.9 %collective-permute-start = (bf16[2,256,128]{2,1,0:T(8,128)(2,1)}, bf16[2,256,128]{2,1,0:T(8,128)(2,1)S(1)}, u32[]{:S(2)}, u32[]{:S(2)}) collective-permute-start(bf16[2,256,128]{2,1,0:T(8,128)(2,1)} %copy.30), channel_id=1, source_target_pairs={{0,8},{8,16},{16,24},{24,32},{32,40},{40,48},{48,56},{56,64},{64,7... | collective-permute-start | bytes 393224 | tf_op jit(solution)/shard_map/while/body/eval_jaxpr/ppermute | solution.py:18
  68.2 4.6 %conditional.5 = (f32[1,2048]{1,0:T(1,128)S(1)}, f32[1,2048]{1,0:T(1,128)S(1)}, f32[1,2048,128]{2,1,0:T(8,128)S(1)}) conditional(s32[]{:T(128)} %convert_element_type.63, (s32[]{:T(128)}, s32[]{:T(128)}, s32[8]{0:T(128)S(1)}, s32[256]{0:T(256)S(1)}, bf16[1,2048,128]{2,1,0:T(8,128)(2,1)S(1)}, /*index=5*/bf16[2,256,128]{2,1,0:T(8,128)(2,1)}, ...), branch_computations={%region_3.6_spmd, %region_7.7_spmd} | conditional | flops 273885440 | bytes 12444736 | solution.py:77
  70.9 1.8 fusion.3
  73.5 3.9 %collective-permute-start = (bf16[2,256,128]{2,1,0:T(8,128)(2,1)}, bf16[2,256,128]{2,1,0:T(8,128)(2,1)S(1)}, u32[]{:S(2)}, u32[]{:S(2)}) collective-permute-start(bf16[2,256,128]{2,1,0:T(8,128)(2,1)} %copy.30), channel_id=1, source_target_pairs={{0,8},{8,16},{16,24},{24,32},{32,40},{40,48},{48,56},{56,64},{64,7... | collective-permute-start | bytes 393224 | tf_op jit(solution)/shard_map/while/body/eval_jaxpr/ppermute | solution.py:18
  77.4 4.6 %conditional.5 = (f32[1,2048]{1,0:T(1,128)S(1)}, f32[1,2048]{1,0:T(1,128)S(1)}, f32[1,2048,128]{2,1,0:T(8,128)S(1)}) conditional(s32[]{:T(128)} %convert_element_type.63, (s32[]{:T(128)}, s32[]{:T(128)}, s32[8]{0:T(128)S(1)}, s32[256]{0:T(256)S(1)}, bf16[1,2048,128]{2,1,0:T(8,128)(2,1)S(1)}, /*index=5*/bf16[2,256,128]{2,1,0:T(8,128)(2,1)}, ...), branch_computations={%region_3.6_spmd, %region_7.7_spmd} | conditional | flops 273885440 | bytes 12444736 | solution.py:77
  80.2 1.8 fusion.3
  82.7 3.9 %collective-permute-start = (bf16[2,256,128]{2,1,0:T(8,128)(2,1)}, bf16[2,256,128]{2,1,0:T(8,128)(2,1)S(1)}, u32[]{:S(2)}, u32[]{:S(2)}) collective-permute-start(bf16[2,256,128]{2,1,0:T(8,128)(2,1)} %copy.30), channel_id=1, source_target_pairs={{0,8},{8,16},{16,24},{24,32},{32,40},{40,48},{48,56},{56,64},{64,7... | collective-permute-start | bytes 393224 | tf_op jit(solution)/shard_map/while/body/eval_jaxpr/ppermute | solution.py:18
  86.7 4.6 %conditional.5 = (f32[1,2048]{1,0:T(1,128)S(1)}, f32[1,2048]{1,0:T(1,128)S(1)}, f32[1,2048,128]{2,1,0:T(8,128)S(1)}) conditional(s32[]{:T(128)} %convert_element_type.63, (s32[]{:T(128)}, s32[]{:T(128)}, s32[8]{0:T(128)S(1)}, s32[256]{0:T(256)S(1)}, bf16[1,2048,128]{2,1,0:T(8,128)(2,1)S(1)}, /*index=5*/bf16[2,256,128]{2,1,0:T(8,128)(2,1)}, ...), branch_computations={%region_3.6_spmd, %region_7.7_spmd} | conditional | flops 273885440 | bytes 12444736 | solution.py:77
  89.4 1.8 fusion.3
  92.0 3.9 %collective-permute-start = (bf16[2,256,128]{2,1,0:T(8,128)(2,1)}, bf16[2,256,128]{2,1,0:T(8,128)(2,1)S(1)}, u32[]{:S(2)}, u32[]{:S(2)}) collective-permute-start(bf16[2,256,128]{2,1,0:T(8,128)(2,1)} %copy.30), channel_id=1, source_target_pairs={{0,8},{8,16},{16,24},{24,32},{32,40},{40,48},{48,56},{56,64},{64,7... | collective-permute-start | bytes 393224 | tf_op jit(solution)/shard_map/while/body/eval_jaxpr/ppermute | solution.py:18
  95.9 4.6 %conditional.5 = (f32[1,2048]{1,0:T(1,128)S(1)}, f32[1,2048]{1,0:T(1,128)S(1)}, f32[1,2048,128]{2,1,0:T(8,128)S(1)}) conditional(s32[]{:T(128)} %convert_element_type.63, (s32[]{:T(128)}, s32[]{:T(128)}, s32[8]{0:T(128)S(1)}, s32[256]{0:T(256)S(1)}, bf16[1,2048,128]{2,1,0:T(8,128)(2,1)S(1)}, /*index=5*/bf16[2,256,128]{2,1,0:T(8,128)(2,1)}, ...), branch_computations={%region_3.6_spmd, %region_7.7_spmd} | conditional | flops 273885440 | bytes 12444736 | solution.py:77
  98.7 1.8 fusion.3
  101.2 3.9 %collective-permute-start = (bf16[2,256,128]{2,1,0:T(8,128)(2,1)}, bf16[2,256,128]{2,1,0:T(8,128)(2,1)S(1)}, u32[]{:S(2)}, u32[]{:S(2)}) collective-permute-start(bf16[2,256,128]{2,1,0:T(8,128)(2,1)} %copy.30), channel_id=1, source_target_pairs={{0,8},{8,16},{16,24},{24,32},{32,40},{40,48},{48,56},{56,64},{64,7... | collective-permute-start | bytes 393224 | tf_op jit(solution)/shard_map/while/body/eval_jaxpr/ppermute | solution.py:18
  105.2 4.6 %conditional.5 = (f32[1,2048]{1,0:T(1,128)S(1)}, f32[1,2048]{1,0:T(1,128)S(1)}, f32[1,2048,128]{2,1,0:T(8,128)S(1)}) conditional(s32[]{:T(128)} %convert_element_type.63, (s32[]{:T(128)}, s32[]{:T(128)}, s32[8]{0:T(128)S(1)}, s32[256]{0:T(256)S(1)}, bf16[1,2048,128]{2,1,0:T(8,128)(2,1)S(1)}, /*index=5*/bf16[2,256,128]{2,1,0:T(8,128)(2,1)}, ...), branch_computations={%region_3.6_spmd, %region_7.7_spmd} | conditional | flops 273885440 | bytes 12444736 | solution.py:77
  107.9 1.8 fusion.3
  110.5 3.9 %collective-permute-start = (bf16[2,256,128]{2,1,0:T(8,128)(2,1)}, bf16[2,256,128]{2,1,0:T(8,128)(2,1)S(1)}, u32[]{:S(2)}, u32[]{:S(2)}) collective-permute-start(bf16[2,256,128]{2,1,0:T(8,128)(2,1)} %copy.30), channel_id=1, source_target_pairs={{0,8},{8,16},{16,24},{24,32},{32,40},{40,48},{48,56},{56,64},{64,7... | collective-permute-start | bytes 393224 | tf_op jit(solution)/shard_map/while/body/eval_jaxpr/ppermute | solution.py:18
  114.4 4.6 %conditional.5 = (f32[1,2048]{1,0:T(1,128)S(1)}, f32[1,2048]{1,0:T(1,128)S(1)}, f32[1,2048,128]{2,1,0:T(8,128)S(1)}) conditional(s32[]{:T(128)} %convert_element_type.63, (s32[]{:T(128)}, s32[]{:T(128)}, s32[8]{0:T(128)S(1)}, s32[256]{0:T(256)S(1)}, bf16[1,2048,128]{2,1,0:T(8,128)(2,1)S(1)}, /*index=5*/bf16[2,256,128]{2,1,0:T(8,128)(2,1)}, ...), branch_computations={%region_3.6_spmd, %region_7.7_spmd} | conditional | flops 273885440 | bytes 12444736 | solution.py:77
  117.2 1.8 fusion.3
  119.7 3.9 %collective-permute-start = (bf16[2,256,128]{2,1,0:T(8,128)(2,1)}, bf16[2,256,128]{2,1,0:T(8,128)(2,1)S(1)}, u32[]{:S(2)}, u32[]{:S(2)}) collective-permute-start(bf16[2,256,128]{2,1,0:T(8,128)(2,1)} %copy.30), channel_id=1, source_target_pairs={{0,8},{8,16},{16,24},{24,32},{32,40},{40,48},{48,56},{56,64},{64,7... | collective-permute-start | bytes 393224 | tf_op jit(solution)/shard_map/while/body/eval_jaxpr/ppermute | solution.py:18
  123.7 4.6 %conditional.5 = (f32[1,2048]{1,0:T(1,128)S(1)}, f32[1,2048]{1,0:T(1,128)S(1)}, f32[1,2048,128]{2,1,0:T(8,128)S(1)}) conditional(s32[]{:T(128)} %convert_element_type.63, (s32[]{:T(128)}, s32[]{:T(128)}, s32[8]{0:T(128)S(1)}, s32[256]{0:T(256)S(1)}, bf16[1,2048,128]{2,1,0:T(8,128)(2,1)S(1)}, /*index=5*/bf16[2,256,128]{2,1,0:T(8,128)(2,1)}, ...), branch_computations={%region_3.6_spmd, %region_7.7_spmd} | conditional | flops 273885440 | bytes 12444736 | solution.py:77
  126.4 1.8 fusion.3
  129.0 3.9 %collective-permute-start = (bf16[2,256,128]{2,1,0:T(8,128)(2,1)}, bf16[2,256,128]{2,1,0:T(8,128)(2,1)S(1)}, u32[]{:S(2)}, u32[]{:S(2)}) collective-permute-start(bf16[2,256,128]{2,1,0:T(8,128)(2,1)} %copy.30), channel_id=1, source_target_pairs={{0,8},{8,16},{16,24},{24,32},{32,40},{40,48},{48,56},{56,64},{64,7... | collective-permute-start | bytes 393224 | tf_op jit(solution)/shard_map/while/body/eval_jaxpr/ppermute | solution.py:18
  132.9 4.6 %conditional.5 = (f32[1,2048]{1,0:T(1,128)S(1)}, f32[1,2048]{1,0:T(1,128)S(1)}, f32[1,2048,128]{2,1,0:T(8,128)S(1)}) conditional(s32[]{:T(128)} %convert_element_type.63, (s32[]{:T(128)}, s32[]{:T(128)}, s32[8]{0:T(128)S(1)}, s32[256]{0:T(256)S(1)}, bf16[1,2048,128]{2,1,0:T(8,128)(2,1)S(1)}, /*index=5*/bf16[2,256,128]{2,1,0:T(8,128)(2,1)}, ...), branch_computations={%region_3.6_spmd, %region_7.7_spmd} | conditional | flops 273885440 | bytes 12444736 | solution.py:77
  135.7 1.8 fusion.3
  138.2 3.9 %collective-permute-start = (bf16[2,256,128]{2,1,0:T(8,128)(2,1)}, bf16[2,256,128]{2,1,0:T(8,128)(2,1)S(1)}, u32[]{:S(2)}, u32[]{:S(2)}) collective-permute-start(bf16[2,256,128]{2,1,0:T(8,128)(2,1)} %copy.30), channel_id=1, source_target_pairs={{0,8},{8,16},{16,24},{24,32},{32,40},{40,48},{48,56},{56,64},{64,7... | collective-permute-start | bytes 393224 | tf_op jit(solution)/shard_map/while/body/eval_jaxpr/ppermute | solution.py:18
  142.2 4.6 %conditional.5 = (f32[1,2048]{1,0:T(1,128)S(1)}, f32[1,2048]{1,0:T(1,128)S(1)}, f32[1,2048,128]{2,1,0:T(8,128)S(1)}) conditional(s32[]{:T(128)} %convert_element_type.63, (s32[]{:T(128)}, s32[]{:T(128)}, s32[8]{0:T(128)S(1)}, s32[256]{0:T(256)S(1)}, bf16[1,2048,128]{2,1,0:T(8,128)(2,1)S(1)}, /*index=5*/bf16[2,256,128]{2,1,0:T(8,128)(2,1)}, ...), branch_computations={%region_3.6_spmd, %region_7.7_spmd} | conditional | flops 273885440 | bytes 12444736 | solution.py:77
  147.5 3.9 %collective-permute-start = (bf16[2,256,128]{2,1,0:T(8,128)(2,1)}, bf16[2,256,128]{2,1,0:T(8,128)(2,1)S(1)}, u32[]{:S(2)}, u32[]{:S(2)}) collective-permute-start(bf16[2,256,128]{2,1,0:T(8,128)(2,1)} %copy.30), channel_id=1, source_target_pairs={{0,8},{8,16},{16,24},{24,32},{32,40},{40,48},{48,56},{56,64},{64,7... | collective-permute-start | bytes 393224 | tf_op jit(solution)/shard_map/while/body/eval_jaxpr/ppermute | solution.py:18
  151.5 2.5 collective-permute-done
  154.6 6.0 %collective-permute-start = (bf16[2,256,128]{2,1,0:T(8,128)(2,1)}, bf16[2,256,128]{2,1,0:T(8,128)(2,1)S(1)}, u32[]{:S(2)}, u32[]{:S(2)}) collective-permute-start(bf16[2,256,128]{2,1,0:T(8,128)(2,1)} %copy.30), channel_id=1, source_target_pairs={{0,8},{8,16},{16,24},{24,32},{32,40},{40,48},{48,56},{56,64},{64,7... | collective-permute-start | bytes 393224 | tf_op jit(solution)/shard_map/while/body/eval_jaxpr/ppermute | solution.py:18
  162.5 5.0 %collective-permute-start = (bf16[2,256,128]{2,1,0:T(8,128)(2,1)}, bf16[2,256,128]{2,1,0:T(8,128)(2,1)S(1)}, u32[]{:S(2)}, u32[]{:S(2)}) collective-permute-start(bf16[2,256,128]{2,1,0:T(8,128)(2,1)} %copy.30), channel_id=1, source_target_pairs={{0,8},{8,16},{16,24},{24,32},{32,40},{40,48},{48,56},{56,64},{64,7... | collective-permute-start | bytes 393224 | tf_op jit(solution)/shard_map/while/body/eval_jaxpr/ppermute | solution.py:18
  169.6 7.1 %collective-permute-start = (bf16[2,256,128]{2,1,0:T(8,128)(2,1)}, bf16[2,256,128]{2,1,0:T(8,128)(2,1)S(1)}, u32[]{:S(2)}, u32[]{:S(2)}) collective-permute-start(bf16[2,256,128]{2,1,0:T(8,128)(2,1)} %copy.30), channel_id=1, source_target_pairs={{0,8},{8,16},{16,24},{24,32},{32,40},{40,48},{48,56},{56,64},{64,7... | collective-permute-start | bytes 393224 | tf_op jit(solution)/shard_map/while/body/eval_jaxpr/ppermute | solution.py:18
  178.5 7.4 %collective-permute-start = (bf16[2,256,128]{2,1,0:T(8,128)(2,1)}, bf16[2,256,128]{2,1,0:T(8,128)(2,1)S(1)}, u32[]{:S(2)}, u32[]{:S(2)}) collective-permute-start(bf16[2,256,128]{2,1,0:T(8,128)(2,1)} %copy.30), channel_id=1, source_target_pairs={{0,8},{8,16},{16,24},{24,32},{32,40},{40,48},{48,56},{56,64},{64,7... | collective-permute-start | bytes 393224 | tf_op jit(solution)/shard_map/while/body/eval_jaxpr/ppermute | solution.py:18
  187.8 7.4 %collective-permute-start = (bf16[2,256,128]{2,1,0:T(8,128)(2,1)}, bf16[2,256,128]{2,1,0:T(8,128)(2,1)S(1)}, u32[]{:S(2)}, u32[]{:S(2)}) collective-permute-start(bf16[2,256,128]{2,1,0:T(8,128)(2,1)} %copy.30), channel_id=1, source_target_pairs={{0,8},{8,16},{16,24},{24,32},{32,40},{40,48},{48,56},{56,64},{64,7... | collective-permute-start | bytes 393224 | tf_op jit(solution)/shard_map/while/body/eval_jaxpr/ppermute | solution.py:18
  197.0 7.4 %collective-permute-start = (bf16[2,256,128]{2,1,0:T(8,128)(2,1)}, bf16[2,256,128]{2,1,0:T(8,128)(2,1)S(1)}, u32[]{:S(2)}, u32[]{:S(2)}) collective-permute-start(bf16[2,256,128]{2,1,0:T(8,128)(2,1)} %copy.30), channel_id=1, source_target_pairs={{0,8},{8,16},{16,24},{24,32},{32,40},{40,48},{48,56},{56,64},{64,7... | collective-permute-start | bytes 393224 | tf_op jit(solution)/shard_map/while/body/eval_jaxpr/ppermute | solution.py:18
  206.3 7.4 %collective-permute-start = (bf16[2,256,128]{2,1,0:T(8,128)(2,1)}, bf16[2,256,128]{2,1,0:T(8,128)(2,1)S(1)}, u32[]{:S(2)}, u32[]{:S(2)}) collective-permute-start(bf16[2,256,128]{2,1,0:T(8,128)(2,1)} %copy.30), channel_id=1, source_target_pairs={{0,8},{8,16},{16,24},{24,32},{32,40},{40,48},{48,56},{56,64},{64,7... | collective-permute-start | bytes 393224 | tf_op jit(solution)/shard_map/while/body/eval_jaxpr/ppermute | solution.py:18
  215.5 7.4 %collective-permute-start = (bf16[2,256,128]{2,1,0:T(8,128)(2,1)}, bf16[2,256,128]{2,1,0:T(8,128)(2,1)S(1)}, u32[]{:S(2)}, u32[]{:S(2)}) collective-permute-start(bf16[2,256,128]{2,1,0:T(8,128)(2,1)} %copy.30), channel_id=1, source_target_pairs={{0,8},{8,16},{16,24},{24,32},{32,40},{40,48},{48,56},{56,64},{64,7... | collective-permute-start | bytes 393224 | tf_op jit(solution)/shard_map/while/body/eval_jaxpr/ppermute | solution.py:18
  224.8 7.4 %collective-permute-start = (bf16[2,256,128]{2,1,0:T(8,128)(2,1)}, bf16[2,256,128]{2,1,0:T(8,128)(2,1)S(1)}, u32[]{:S(2)}, u32[]{:S(2)}) collective-permute-start(bf16[2,256,128]{2,1,0:T(8,128)(2,1)} %copy.30), channel_id=1, source_target_pairs={{0,8},{8,16},{16,24},{24,32},{32,40},{40,48},{48,56},{56,64},{64,7... | collective-permute-start | bytes 393224 | tf_op jit(solution)/shard_map/while/body/eval_jaxpr/ppermute | solution.py:18
  234.0 7.4 %collective-permute-start = (bf16[2,256,128]{2,1,0:T(8,128)(2,1)}, bf16[2,256,128]{2,1,0:T(8,128)(2,1)S(1)}, u32[]{:S(2)}, u32[]{:S(2)}) collective-permute-start(bf16[2,256,128]{2,1,0:T(8,128)(2,1)} %copy.30), channel_id=1, source_target_pairs={{0,8},{8,16},{16,24},{24,32},{32,40},{40,48},{48,56},{56,64},{64,7... | collective-permute-start | bytes 393224 | tf_op jit(solution)/shard_map/while/body/eval_jaxpr/ppermute | solution.py:18
  243.3 7.4 %collective-permute-start = (bf16[2,256,128]{2,1,0:T(8,128)(2,1)}, bf16[2,256,128]{2,1,0:T(8,128)(2,1)S(1)}, u32[]{:S(2)}, u32[]{:S(2)}) collective-permute-start(bf16[2,256,128]{2,1,0:T(8,128)(2,1)} %copy.30), channel_id=1, source_target_pairs={{0,8},{8,16},{16,24},{24,32},{32,40},{40,48},{48,56},{56,64},{64,7... | collective-permute-start | bytes 393224 | tf_op jit(solution)/shard_map/while/body/eval_jaxpr/ppermute | solution.py:18
  252.5 7.4 %collective-permute-start = (bf16[2,256,128]{2,1,0:T(8,128)(2,1)}, bf16[2,256,128]{2,1,0:T(8,128)(2,1)S(1)}, u32[]{:S(2)}, u32[]{:S(2)}) collective-permute-start(bf16[2,256,128]{2,1,0:T(8,128)(2,1)} %copy.30), channel_id=1, source_target_pairs={{0,8},{8,16},{16,24},{24,32},{32,40},{40,48},{48,56},{56,64},{64,7... | collective-permute-start | bytes 393224 | tf_op jit(solution)/shard_map/while/body/eval_jaxpr/ppermute | solution.py:18
  261.8 7.4 %collective-permute-start = (bf16[2,256,128]{2,1,0:T(8,128)(2,1)}, bf16[2,256,128]{2,1,0:T(8,128)(2,1)S(1)}, u32[]{:S(2)}, u32[]{:S(2)}) collective-permute-start(bf16[2,256,128]{2,1,0:T(8,128)(2,1)} %copy.30), channel_id=1, source_target_pairs={{0,8},{8,16},{16,24},{24,32},{32,40},{40,48},{48,56},{56,64},{64,7... | collective-permute-start | bytes 393224 | tf_op jit(solution)/shard_map/while/body/eval_jaxpr/ppermute | solution.py:18
  271.0 7.4 %collective-permute-start = (bf16[2,256,128]{2,1,0:T(8,128)(2,1)}, bf16[2,256,128]{2,1,0:T(8,128)(2,1)S(1)}, u32[]{:S(2)}, u32[]{:S(2)}) collective-permute-start(bf16[2,256,128]{2,1,0:T(8,128)(2,1)} %copy.30), channel_id=1, source_target_pairs={{0,8},{8,16},{16,24},{24,32},{32,40},{40,48},{48,56},{56,64},{64,7... | collective-permute-start | bytes 393224 | tf_op jit(solution)/shard_map/while/body/eval_jaxpr/ppermute | solution.py:18
  280.3 7.4 %collective-permute-start = (bf16[2,256,128]{2,1,0:T(8,128)(2,1)}, bf16[2,256,128]{2,1,0:T(8,128)(2,1)S(1)}, u32[]{:S(2)}, u32[]{:S(2)}) collective-permute-start(bf16[2,256,128]{2,1,0:T(8,128)(2,1)} %copy.30), channel_id=1, source_target_pairs={{0,8},{8,16},{16,24},{24,32},{32,40},{40,48},{48,56},{56,64},{64,7... | collective-permute-start | bytes 393224 | tf_op jit(solution)/shard_map/while/body/eval_jaxpr/ppermute | solution.py:18
  290.3 84.3 %all-gather.2.cloned.1.call-done = bf16[256,8192]{0,1:T(8,128)(2,1)} async-done(((bf16[256,1024]{0,1:T(8,128)(2,1)}), bf16[256,8192]{0,1:T(8,128)(2,1)}) %all-gather.2.cloned.1.call-update) | async-done | bytes 4194320 | tf_op jit(solution)/shard_map/all_gather | solution.py:102
  374.6 7.7 %convolution_convert_fusion = bf16[256,512]{1,0:T(8,128)(2,1)} fusion(bf16[256,8192]{0,1:T(8,128)(2,1)} %all-gather.2.cloned.1.call-done, bf16[8192,512]{1,0:T(8,128)(2,1)} %param.15), kind=kOutput, calls=%fused_computation.42 | convolution fusion | flops 2147614720 | bytes 12845056 | tf_op jit(solution)/shard_map/dot_general | solution.py:101
  (309 shorter events, 83.5 us)
Async XLA Ops:
  6.5 2.2 copy-start.1
  6.5 2.2 copy-start
  6.5 368.0 %all-gather.2.cloned.1.call-start = ((), (), s32[]{:S(2)}) async-start(), calls=%async_computation | async-start | bytes 4718592 | tf_op jit(solution)/shard_map/all_gather | solution.py:102
  9.5 6.6 %collective-permute-start = (bf16[2,256,128]{2,1,0:T(8,128)(2,1)}, bf16[2,256,128]{2,1,0:T(8,128)(2,1)S(1)}, u32[]{:S(2)}, u32[]{:S(2)}) collective-permute-start(bf16[2,256,128]{2,1,0:T(8,128)(2,1)} %copy.30), channel_id=1, source_target_pairs={{0,8},{8,16},{16,24},{24,32},{32,40},{40,48},{48,56},{56,64},{64,7... | collective-permute-start | bytes 393224 | tf_op jit(solution)/shard_map/while/body/eval_jaxpr/ppermute | solution.py:18
  16.8 9.8 %collective-permute-start = (bf16[2,256,128]{2,1,0:T(8,128)(2,1)}, bf16[2,256,128]{2,1,0:T(8,128)(2,1)S(1)}, u32[]{:S(2)}, u32[]{:S(2)}) collective-permute-start(bf16[2,256,128]{2,1,0:T(8,128)(2,1)} %copy.30), channel_id=1, source_target_pairs={{0,8},{8,16},{16,24},{24,32},{32,40},{40,48},{48,56},{56,64},{64,7... | collective-permute-start | bytes 393224 | tf_op jit(solution)/shard_map/while/body/eval_jaxpr/ppermute | solution.py:18
  27.2 8.6 %collective-permute-start = (bf16[2,256,128]{2,1,0:T(8,128)(2,1)}, bf16[2,256,128]{2,1,0:T(8,128)(2,1)S(1)}, u32[]{:S(2)}, u32[]{:S(2)}) collective-permute-start(bf16[2,256,128]{2,1,0:T(8,128)(2,1)} %copy.30), channel_id=1, source_target_pairs={{0,8},{8,16},{16,24},{24,32},{32,40},{40,48},{48,56},{56,64},{64,7... | collective-permute-start | bytes 393224 | tf_op jit(solution)/shard_map/while/body/eval_jaxpr/ppermute | solution.py:18
  36.5 8.6 %collective-permute-start = (bf16[2,256,128]{2,1,0:T(8,128)(2,1)}, bf16[2,256,128]{2,1,0:T(8,128)(2,1)S(1)}, u32[]{:S(2)}, u32[]{:S(2)}) collective-permute-start(bf16[2,256,128]{2,1,0:T(8,128)(2,1)} %copy.30), channel_id=1, source_target_pairs={{0,8},{8,16},{16,24},{24,32},{32,40},{40,48},{48,56},{56,64},{64,7... | collective-permute-start | bytes 393224 | tf_op jit(solution)/shard_map/while/body/eval_jaxpr/ppermute | solution.py:18
  45.7 8.6 %collective-permute-start = (bf16[2,256,128]{2,1,0:T(8,128)(2,1)}, bf16[2,256,128]{2,1,0:T(8,128)(2,1)S(1)}, u32[]{:S(2)}, u32[]{:S(2)}) collective-permute-start(bf16[2,256,128]{2,1,0:T(8,128)(2,1)} %copy.30), channel_id=1, source_target_pairs={{0,8},{8,16},{16,24},{24,32},{32,40},{40,48},{48,56},{56,64},{64,7... | collective-permute-start | bytes 393224 | tf_op jit(solution)/shard_map/while/body/eval_jaxpr/ppermute | solution.py:18
  55.0 8.6 %collective-permute-start = (bf16[2,256,128]{2,1,0:T(8,128)(2,1)}, bf16[2,256,128]{2,1,0:T(8,128)(2,1)S(1)}, u32[]{:S(2)}, u32[]{:S(2)}) collective-permute-start(bf16[2,256,128]{2,1,0:T(8,128)(2,1)} %copy.30), channel_id=1, source_target_pairs={{0,8},{8,16},{16,24},{24,32},{32,40},{40,48},{48,56},{56,64},{64,7... | collective-permute-start | bytes 393224 | tf_op jit(solution)/shard_map/while/body/eval_jaxpr/ppermute | solution.py:18
  64.2 8.6 %collective-permute-start = (bf16[2,256,128]{2,1,0:T(8,128)(2,1)}, bf16[2,256,128]{2,1,0:T(8,128)(2,1)S(1)}, u32[]{:S(2)}, u32[]{:S(2)}) collective-permute-start(bf16[2,256,128]{2,1,0:T(8,128)(2,1)} %copy.30), channel_id=1, source_target_pairs={{0,8},{8,16},{16,24},{24,32},{32,40},{40,48},{48,56},{56,64},{64,7... | collective-permute-start | bytes 393224 | tf_op jit(solution)/shard_map/while/body/eval_jaxpr/ppermute | solution.py:18
  73.5 8.6 %collective-permute-start = (bf16[2,256,128]{2,1,0:T(8,128)(2,1)}, bf16[2,256,128]{2,1,0:T(8,128)(2,1)S(1)}, u32[]{:S(2)}, u32[]{:S(2)}) collective-permute-start(bf16[2,256,128]{2,1,0:T(8,128)(2,1)} %copy.30), channel_id=1, source_target_pairs={{0,8},{8,16},{16,24},{24,32},{32,40},{40,48},{48,56},{56,64},{64,7... | collective-permute-start | bytes 393224 | tf_op jit(solution)/shard_map/while/body/eval_jaxpr/ppermute | solution.py:18
  82.7 8.6 %collective-permute-start = (bf16[2,256,128]{2,1,0:T(8,128)(2,1)}, bf16[2,256,128]{2,1,0:T(8,128)(2,1)S(1)}, u32[]{:S(2)}, u32[]{:S(2)}) collective-permute-start(bf16[2,256,128]{2,1,0:T(8,128)(2,1)} %copy.30), channel_id=1, source_target_pairs={{0,8},{8,16},{16,24},{24,32},{32,40},{40,48},{48,56},{56,64},{64,7... | collective-permute-start | bytes 393224 | tf_op jit(solution)/shard_map/while/body/eval_jaxpr/ppermute | solution.py:18
  92.0 8.6 %collective-permute-start = (bf16[2,256,128]{2,1,0:T(8,128)(2,1)}, bf16[2,256,128]{2,1,0:T(8,128)(2,1)S(1)}, u32[]{:S(2)}, u32[]{:S(2)}) collective-permute-start(bf16[2,256,128]{2,1,0:T(8,128)(2,1)} %copy.30), channel_id=1, source_target_pairs={{0,8},{8,16},{16,24},{24,32},{32,40},{40,48},{48,56},{56,64},{64,7... | collective-permute-start | bytes 393224 | tf_op jit(solution)/shard_map/while/body/eval_jaxpr/ppermute | solution.py:18
  101.2 8.6 %collective-permute-start = (bf16[2,256,128]{2,1,0:T(8,128)(2,1)}, bf16[2,256,128]{2,1,0:T(8,128)(2,1)S(1)}, u32[]{:S(2)}, u32[]{:S(2)}) collective-permute-start(bf16[2,256,128]{2,1,0:T(8,128)(2,1)} %copy.30), channel_id=1, source_target_pairs={{0,8},{8,16},{16,24},{24,32},{32,40},{40,48},{48,56},{56,64},{64,7... | collective-permute-start | bytes 393224 | tf_op jit(solution)/shard_map/while/body/eval_jaxpr/ppermute | solution.py:18
  110.5 8.6 %collective-permute-start = (bf16[2,256,128]{2,1,0:T(8,128)(2,1)}, bf16[2,256,128]{2,1,0:T(8,128)(2,1)S(1)}, u32[]{:S(2)}, u32[]{:S(2)}) collective-permute-start(bf16[2,256,128]{2,1,0:T(8,128)(2,1)} %copy.30), channel_id=1, source_target_pairs={{0,8},{8,16},{16,24},{24,32},{32,40},{40,48},{48,56},{56,64},{64,7... | collective-permute-start | bytes 393224 | tf_op jit(solution)/shard_map/while/body/eval_jaxpr/ppermute | solution.py:18
  119.7 8.6 %collective-permute-start = (bf16[2,256,128]{2,1,0:T(8,128)(2,1)}, bf16[2,256,128]{2,1,0:T(8,128)(2,1)S(1)}, u32[]{:S(2)}, u32[]{:S(2)}) collective-permute-start(bf16[2,256,128]{2,1,0:T(8,128)(2,1)} %copy.30), channel_id=1, source_target_pairs={{0,8},{8,16},{16,24},{24,32},{32,40},{40,48},{48,56},{56,64},{64,7... | collective-permute-start | bytes 393224 | tf_op jit(solution)/shard_map/while/body/eval_jaxpr/ppermute | solution.py:18
  129.0 8.6 %collective-permute-start = (bf16[2,256,128]{2,1,0:T(8,128)(2,1)}, bf16[2,256,128]{2,1,0:T(8,128)(2,1)S(1)}, u32[]{:S(2)}, u32[]{:S(2)}) collective-permute-start(bf16[2,256,128]{2,1,0:T(8,128)(2,1)} %copy.30), channel_id=1, source_target_pairs={{0,8},{8,16},{16,24},{24,32},{32,40},{40,48},{48,56},{56,64},{64,7... | collective-permute-start | bytes 393224 | tf_op jit(solution)/shard_map/while/body/eval_jaxpr/ppermute | solution.py:18
  138.2 8.6 %collective-permute-start = (bf16[2,256,128]{2,1,0:T(8,128)(2,1)}, bf16[2,256,128]{2,1,0:T(8,128)(2,1)S(1)}, u32[]{:S(2)}, u32[]{:S(2)}) collective-permute-start(bf16[2,256,128]{2,1,0:T(8,128)(2,1)} %copy.30), channel_id=1, source_target_pairs={{0,8},{8,16},{16,24},{24,32},{32,40},{40,48},{48,56},{56,64},{64,7... | collective-permute-start | bytes 393224 | tf_op jit(solution)/shard_map/while/body/eval_jaxpr/ppermute | solution.py:18
  147.5 6.5 %collective-permute-start = (bf16[2,256,128]{2,1,0:T(8,128)(2,1)}, bf16[2,256,128]{2,1,0:T(8,128)(2,1)S(1)}, u32[]{:S(2)}, u32[]{:S(2)}) collective-permute-start(bf16[2,256,128]{2,1,0:T(8,128)(2,1)} %copy.30), channel_id=1, source_target_pairs={{0,8},{8,16},{16,24},{24,32},{32,40},{40,48},{48,56},{56,64},{64,7... | collective-permute-start | bytes 393224 | tf_op jit(solution)/shard_map/while/body/eval_jaxpr/ppermute | solution.py:18
  154.6 7.2 %collective-permute-start = (bf16[2,256,128]{2,1,0:T(8,128)(2,1)}, bf16[2,256,128]{2,1,0:T(8,128)(2,1)S(1)}, u32[]{:S(2)}, u32[]{:S(2)}) collective-permute-start(bf16[2,256,128]{2,1,0:T(8,128)(2,1)} %copy.30), channel_id=1, source_target_pairs={{0,8},{8,16},{16,24},{24,32},{32,40},{40,48},{48,56},{56,64},{64,7... | collective-permute-start | bytes 393224 | tf_op jit(solution)/shard_map/while/body/eval_jaxpr/ppermute | solution.py:18
  162.5 6.5 %collective-permute-start = (bf16[2,256,128]{2,1,0:T(8,128)(2,1)}, bf16[2,256,128]{2,1,0:T(8,128)(2,1)S(1)}, u32[]{:S(2)}, u32[]{:S(2)}) collective-permute-start(bf16[2,256,128]{2,1,0:T(8,128)(2,1)} %copy.30), channel_id=1, source_target_pairs={{0,8},{8,16},{16,24},{24,32},{32,40},{40,48},{48,56},{56,64},{64,7... | collective-permute-start | bytes 393224 | tf_op jit(solution)/shard_map/while/body/eval_jaxpr/ppermute | solution.py:18
  169.6 8.3 %collective-permute-start = (bf16[2,256,128]{2,1,0:T(8,128)(2,1)}, bf16[2,256,128]{2,1,0:T(8,128)(2,1)S(1)}, u32[]{:S(2)}, u32[]{:S(2)}) collective-permute-start(bf16[2,256,128]{2,1,0:T(8,128)(2,1)} %copy.30), channel_id=1, source_target_pairs={{0,8},{8,16},{16,24},{24,32},{32,40},{40,48},{48,56},{56,64},{64,7... | collective-permute-start | bytes 393224 | tf_op jit(solution)/shard_map/while/body/eval_jaxpr/ppermute | solution.py:18
  178.5 8.6 %collective-permute-start = (bf16[2,256,128]{2,1,0:T(8,128)(2,1)}, bf16[2,256,128]{2,1,0:T(8,128)(2,1)S(1)}, u32[]{:S(2)}, u32[]{:S(2)}) collective-permute-start(bf16[2,256,128]{2,1,0:T(8,128)(2,1)} %copy.30), channel_id=1, source_target_pairs={{0,8},{8,16},{16,24},{24,32},{32,40},{40,48},{48,56},{56,64},{64,7... | collective-permute-start | bytes 393224 | tf_op jit(solution)/shard_map/while/body/eval_jaxpr/ppermute | solution.py:18
  187.8 8.6 %collective-permute-start = (bf16[2,256,128]{2,1,0:T(8,128)(2,1)}, bf16[2,256,128]{2,1,0:T(8,128)(2,1)S(1)}, u32[]{:S(2)}, u32[]{:S(2)}) collective-permute-start(bf16[2,256,128]{2,1,0:T(8,128)(2,1)} %copy.30), channel_id=1, source_target_pairs={{0,8},{8,16},{16,24},{24,32},{32,40},{40,48},{48,56},{56,64},{64,7... | collective-permute-start | bytes 393224 | tf_op jit(solution)/shard_map/while/body/eval_jaxpr/ppermute | solution.py:18
  197.0 8.6 %collective-permute-start = (bf16[2,256,128]{2,1,0:T(8,128)(2,1)}, bf16[2,256,128]{2,1,0:T(8,128)(2,1)S(1)}, u32[]{:S(2)}, u32[]{:S(2)}) collective-permute-start(bf16[2,256,128]{2,1,0:T(8,128)(2,1)} %copy.30), channel_id=1, source_target_pairs={{0,8},{8,16},{16,24},{24,32},{32,40},{40,48},{48,56},{56,64},{64,7... | collective-permute-start | bytes 393224 | tf_op jit(solution)/shard_map/while/body/eval_jaxpr/ppermute | solution.py:18
  206.3 8.6 %collective-permute-start = (bf16[2,256,128]{2,1,0:T(8,128)(2,1)}, bf16[2,256,128]{2,1,0:T(8,128)(2,1)S(1)}, u32[]{:S(2)}, u32[]{:S(2)}) collective-permute-start(bf16[2,256,128]{2,1,0:T(8,128)(2,1)} %copy.30), channel_id=1, source_target_pairs={{0,8},{8,16},{16,24},{24,32},{32,40},{40,48},{48,56},{56,64},{64,7... | collective-permute-start | bytes 393224 | tf_op jit(solution)/shard_map/while/body/eval_jaxpr/ppermute | solution.py:18
  215.5 8.6 %collective-permute-start = (bf16[2,256,128]{2,1,0:T(8,128)(2,1)}, bf16[2,256,128]{2,1,0:T(8,128)(2,1)S(1)}, u32[]{:S(2)}, u32[]{:S(2)}) collective-permute-start(bf16[2,256,128]{2,1,0:T(8,128)(2,1)} %copy.30), channel_id=1, source_target_pairs={{0,8},{8,16},{16,24},{24,32},{32,40},{40,48},{48,56},{56,64},{64,7... | collective-permute-start | bytes 393224 | tf_op jit(solution)/shard_map/while/body/eval_jaxpr/ppermute | solution.py:18
  224.8 8.6 %collective-permute-start = (bf16[2,256,128]{2,1,0:T(8,128)(2,1)}, bf16[2,256,128]{2,1,0:T(8,128)(2,1)S(1)}, u32[]{:S(2)}, u32[]{:S(2)}) collective-permute-start(bf16[2,256,128]{2,1,0:T(8,128)(2,1)} %copy.30), channel_id=1, source_target_pairs={{0,8},{8,16},{16,24},{24,32},{32,40},{40,48},{48,56},{56,64},{64,7... | collective-permute-start | bytes 393224 | tf_op jit(solution)/shard_map/while/body/eval_jaxpr/ppermute | solution.py:18
  234.0 8.6 %collective-permute-start = (bf16[2,256,128]{2,1,0:T(8,128)(2,1)}, bf16[2,256,128]{2,1,0:T(8,128)(2,1)S(1)}, u32[]{:S(2)}, u32[]{:S(2)}) collective-permute-start(bf16[2,256,128]{2,1,0:T(8,128)(2,1)} %copy.30), channel_id=1, source_target_pairs={{0,8},{8,16},{16,24},{24,32},{32,40},{40,48},{48,56},{56,64},{64,7... | collective-permute-start | bytes 393224 | tf_op jit(solution)/shard_map/while/body/eval_jaxpr/ppermute | solution.py:18
  243.3 8.6 %collective-permute-start = (bf16[2,256,128]{2,1,0:T(8,128)(2,1)}, bf16[2,256,128]{2,1,0:T(8,128)(2,1)S(1)}, u32[]{:S(2)}, u32[]{:S(2)}) collective-permute-start(bf16[2,256,128]{2,1,0:T(8,128)(2,1)} %copy.30), channel_id=1, source_target_pairs={{0,8},{8,16},{16,24},{24,32},{32,40},{40,48},{48,56},{56,64},{64,7... | collective-permute-start | bytes 393224 | tf_op jit(solution)/shard_map/while/body/eval_jaxpr/ppermute | solution.py:18
  252.5 8.6 %collective-permute-start = (bf16[2,256,128]{2,1,0:T(8,128)(2,1)}, bf16[2,256,128]{2,1,0:T(8,128)(2,1)S(1)}, u32[]{:S(2)}, u32[]{:S(2)}) collective-permute-start(bf16[2,256,128]{2,1,0:T(8,128)(2,1)} %copy.30), channel_id=1, source_target_pairs={{0,8},{8,16},{16,24},{24,32},{32,40},{40,48},{48,56},{56,64},{64,7... | collective-permute-start | bytes 393224 | tf_op jit(solution)/shard_map/while/body/eval_jaxpr/ppermute | solution.py:18
  261.8 8.6 %collective-permute-start = (bf16[2,256,128]{2,1,0:T(8,128)(2,1)}, bf16[2,256,128]{2,1,0:T(8,128)(2,1)S(1)}, u32[]{:S(2)}, u32[]{:S(2)}) collective-permute-start(bf16[2,256,128]{2,1,0:T(8,128)(2,1)} %copy.30), channel_id=1, source_target_pairs={{0,8},{8,16},{16,24},{24,32},{32,40},{40,48},{48,56},{56,64},{64,7... | collective-permute-start | bytes 393224 | tf_op jit(solution)/shard_map/while/body/eval_jaxpr/ppermute | solution.py:18
  271.0 8.6 %collective-permute-start = (bf16[2,256,128]{2,1,0:T(8,128)(2,1)}, bf16[2,256,128]{2,1,0:T(8,128)(2,1)S(1)}, u32[]{:S(2)}, u32[]{:S(2)}) collective-permute-start(bf16[2,256,128]{2,1,0:T(8,128)(2,1)} %copy.30), channel_id=1, source_target_pairs={{0,8},{8,16},{16,24},{24,32},{32,40},{40,48},{48,56},{56,64},{64,7... | collective-permute-start | bytes 393224 | tf_op jit(solution)/shard_map/while/body/eval_jaxpr/ppermute | solution.py:18
  280.3 8.6 %collective-permute-start = (bf16[2,256,128]{2,1,0:T(8,128)(2,1)}, bf16[2,256,128]{2,1,0:T(8,128)(2,1)S(1)}, u32[]{:S(2)}, u32[]{:S(2)}) collective-permute-start(bf16[2,256,128]{2,1,0:T(8,128)(2,1)} %copy.30), channel_id=1, source_target_pairs={{0,8},{8,16},{16,24},{24,32},{32,40},{40,48},{48,56},{56,64},{64,7... | collective-permute-start | bytes 393224 | tf_op jit(solution)/shard_map/while/body/eval_jaxpr/ppermute | solution.py:18
Sparse Core Ops, SparseCore 0:
  290.4 84.1 all-gather.1
where the time goes:
time: 395 us; the launch traced here: 389 us
  starting transfers between devices  169 us (43%)
  waiting for transfers between devices  103 us (26%)
  matrix products  55.6 us (14%)
  local copies, waits for them, and re-layouts  31.1 us (8%)
  between operations  13.5 us (3%)
  other arithmetic  12.9 us (3%)
    ppermute x31, starting transfers between devices, passed_along(): lax.ppermute(value, axis, [(source, source + steps) for source in range(l...  169 us
    all_gather x1, waiting for transfers between devices, local(): lax.all_gather(head_outs, 'head', axis=1, tiled=True)  84.3 us
    dot_general x15, matrix products, attend(): jnp.einsum('gqk,kgd->gqd', exp_scores.astype(jnp.bfloat16), value_tile, p...  27.4 us
    dot_general x15, matrix products, attend(): jnp.einsum('gqd,kgd->gqk', folded, key_tile, preferred_element_type=jnp.f...  20.5 us
    while x62, local copies, waits for them, and re-layouts  20.4 us
    ppermute x31, waiting for transfers between devices, passed_along(): lax.ppermute(value, axis, [(source, source + steps) for source in range(l...  19.1 us
  transfers between devices with their start and end apart: 32, of which 17 were waited for; matrix products, arithmetic and copies ran while one was open for 17% of the time, Pallas kernels for 0%

commit v1 on v0

v1 whole, which is shorter than its diff:
```python
import math

import jax
import jax.numpy as jnp
from jax import lax
from jax.experimental import pallas as pl
from jax.experimental.pallas import tpu as pltpu
from jax.sharding import PartitionSpec as P

HEAD_DIM = 128
GROUP = 8
LOW_SCORE = -1e30
FLOOR = -1e20
LANES = 4
LEVELS = 5
CHUNK = 512


def attention_kernel(ctx_ref, docs_ref, q_ref, *refs):
    count = LEVELS * LANES
    pieces, (out_ref, key_buf, value_buf, max_buf, sum_buf, sem) = refs[:count], refs[count:]
    rows = q_ref.shape[0]
    ctx = ctx_ref[0]
    lane = lax.rem(ctx, LANES)
    window = (ctx - lane - (LEVELS - 1) * LANES) * rows
    copies = []
    for index, piece in enumerate(pieces):
        back, flip = index // LANES, index % LANES
        slot = (LEVELS - 1 - back) * LANES + lax.bitwise_xor(lane, flip)
        at = pl.ds(pl.multiple_of(slot * rows, rows), rows)
        copies.append(pltpu.make_async_copy(piece.at[:, :HEAD_DIM], key_buf.at[at], sem.at[2 * index]))
        copies.append(pltpu.make_async_copy(piece.at[:, HEAD_DIM:], value_buf.at[at, :HEAD_DIM], sem.at[2 * index + 1]))
    for copy in copies:
        copy.start()
    first_row = ctx * rows
    row_pos = first_row + lax.broadcasted_iota(jnp.int32, (rows, 1), 0)
    row_low = jnp.zeros((rows, 1), jnp.int32)
    first_low, last_low, end = jnp.int32(0), jnp.int32(0), jnp.int32(0)
    for doc in range(docs_ref.shape[0]):
        end = end + docs_ref[doc]
        row_low = jnp.where(end <= row_pos, end, row_low)
        first_low = jnp.where(end <= first_row, end, first_low)
        last_low = jnp.where(end <= first_row + rows - 1, end, last_low)
    value_buf[:, HEAD_DIM:] = jnp.ones((value_buf.shape[0], HEAD_DIM), jnp.bfloat16)
    max_buf[...] = jnp.full(max_buf.shape, FLOOR, jnp.float32)
    sum_buf[...] = jnp.zeros(sum_buf.shape, jnp.float32)
    for copy in copies:
        copy.wait()
    log_scale = math.log2(math.e) / math.sqrt(HEAD_DIM)

    def one_head(head, begin, key_pos_begin, masked):
        columns = pl.ds(pl.multiple_of(head * HEAD_DIM, HEAD_DIM), HEAD_DIM)
        scores = lax.dot_general(
            q_ref[:, columns],
            key_buf[pl.ds(begin, CHUNK), :],
            (((1,), (1,)), ((), ())),
            preferred_element_type=jnp.float32,
        )
        scores = scores * log_scale
        if masked:
            key_pos = key_pos_begin + lax.broadcasted_iota(jnp.int32, (1, CHUNK), 1)
            allowed = (key_pos <= row_pos) & (key_pos >= row_low)
            scores = jnp.where(allowed, scores, LOW_SCORE)
        old_max = max_buf[head]
        new_max = jnp.maximum(old_max, jnp.max(scores, axis=1, keepdims=True))
        probs = jnp.exp2(scores - new_max[:, :1]).astype(jnp.bfloat16)
        shrink = jnp.exp2(old_max - new_max)
        added = jnp.dot(probs, value_buf[pl.ds(begin, CHUNK), :], preferred_element_type=jnp.float32)
        sum_buf[head] = sum_buf[head] * jnp.concatenate([shrink, shrink], axis=1) + added
        max_buf[head] = new_max

    def one_chunk(chunk, carry):
        begin = pl.multiple_of(chunk * CHUNK, CHUNK)
        key_pos_begin = window + begin
        free = (key_pos_begin >= last_low) & (key_pos_begin + CHUNK - 1 <= first_row)

        @pl.when(free)
        def _():
            for head in range(GROUP):
                one_head(head, begin, key_pos_begin, False)

        @pl.when(jnp.logical_not(free))
        def _():
            for head in range(GROUP):
                one_head(head, begin, key_pos_begin, True)

        return carry

    lax.fori_loop((first_low - window) // CHUNK, (first_row + rows - 1 - window) // CHUNK + 1, one_chunk, 0)
    for head in range(GROUP):
        total = sum_buf[head]
        out_ref[:, head * HEAD_DIM : (head + 1) * HEAD_DIM] = (
            total[:, :HEAD_DIM] / total[:, HEAD_DIM:]
        ).astype(jnp.bfloat16)


def attention(ctx, doc_lengths, queries, pieces):
    rows = queries.shape[0]
    held = LEVELS * LANES * rows
    smem, vmem, anywhere = (
        pl.BlockSpec(memory_space=pltpu.SMEM),
        pl.BlockSpec(memory_space=pltpu.VMEM),
        pl.BlockSpec(memory_space=pl.ANY),
    )
    return pl.pallas_call(
        attention_kernel,
        out_shape=jax.ShapeDtypeStruct(queries.shape, jnp.bfloat16),
        in_specs=[smem, smem, vmem] + [anywhere] * len(pieces),
        out_specs=vmem,
        scratch_shapes=[
            pltpu.VMEM((held, HEAD_DIM), jnp.bfloat16),
            pltpu.VMEM((held, 2 * HEAD_DIM), jnp.bfloat16),
            pltpu.VMEM((GROUP, rows, HEAD_DIM), jnp.float32),
            pltpu.VMEM((GROUP, rows, 2 * HEAD_DIM), jnp.float32),
            pltpu.SemaphoreType.DMA((2 * len(pieces),)),
        ],
        compiler_params=pltpu.CompilerParams(vmem_limit_bytes=40 * 1024 * 1024),
        cost_estimate=pl.CostEstimate(flops=5 * 10**9, bytes_accessed=4 * 10**6, transcendentals=8 * 10**6),
        name="attention",
    )(ctx, doc_lengths, queries, *pieces)


def turned(value, axis, steps):
    size = lax.axis_size(axis)
    return lax.ppermute(value, axis, [(source, (source + steps) % size) for source in range(size)])


def swapped(value, axis, flip):
    return lax.ppermute(value, axis, [(source, source ^ flip) for source in range(lax.axis_size(axis))])


def local(queries, keys, values, doc_lengths, out_weight):
    rows = queries.shape[0]
    ctx = lax.axis_index("ctx")
    me = lax.axis_index("head")
    own = jnp.concatenate([keys, values], axis=1)
    one_back = turned(own, "ctx", LANES)
    two_ahead = turned(own, "ctx", -2 * LANES)
    two_back = turned(one_back, "ctx", LANES)
    four_back = turned(two_ahead, "ctx", -2 * LANES)
    three_back = turned(two_back, "ctx", LANES)
    pieces = []
    for level in (own, one_back, two_back, three_back, four_back):
        across = swapped(level, "ctx", 2)
        pieces += [level, swapped(level, "ctx", 1), across, swapped(across, "ctx", 1)]
    attended = attention(ctx.reshape(1), doc_lengths, queries, pieces)
    below = turned(attended, "head", 2)
    above = turned(attended, "head", -2)
    beside = swapped(attended, "head", 1)
    half = rows // 2
    far_top = turned(below[:half], "head", 2)
    far_bottom = turned(above[half:], "head", -2)
    below_beside = turned(beside, "head", 2)
    above_beside = turned(beside, "head", -2)
    far_beside_top = swapped(far_top, "head", 1)
    far_beside_bottom = swapped(far_bottom, "head", 1)
    depth = queries.shape[1]
    count = lax.axis_size("head")

    def term(piece, steps, flip):
        source = lax.bitwise_xor((me + 2 * steps) % count, flip)
        return jnp.dot(
            piece,
            lax.dynamic_slice_in_dim(out_weight, source * depth, depth, 0),
            preferred_element_type=jnp.float32,
        )

    total = term(attended, 0, 0) + term(below, -1, 0) + term(above, 1, 0) + term(beside, 0, 1)
    total = total + term(jnp.concatenate([far_top, far_bottom]), 2, 0)
    total = total + term(below_beside, -1, 1) + term(above_beside, 1, 1)
    total = total + term(jnp.concatenate([far_beside_top, far_beside_bottom]), 2, 1)
    return total.astype(jnp.bfloat16)


def solution(mesh):
    placed = (P("ctx", "head"), P("ctx", "head"), P("ctx", "head"), P(), P(None, "head"))
    return jax.shard_map(
        local, mesh=mesh, in_specs=placed, out_specs=P("ctx", "head"), check_vma=False
    )
```

time: 395 us -> 95.6 us (0.24); the launches traced: 389 us -> 97.1 us
  starting transfers between devices: 169 us -> 29.2 us
  waiting for transfers between devices: 103 us -> 34.5 us
  matrix products: 55.6 us -> 9.1 us
  local copies, waits for them, and re-layouts: 31.1 us -> 3.45 us
  Pallas kernels: 0 us -> 20.6 us
  between operations: 13.5 us -> 0.17 us
  other arithmetic: 12.9 us -> 0 us
    ppermute x31 -> x29, starting transfers between devices: 169 us -> 29.2 us  [the longest x11 18.4 us: turned(): lax.ppermute(value, axis, [(source, (source + steps) % size) for source i...]
    all_gather x1 -> x0, waiting for transfers between devices: 84.3 us -> none  [local(): lax.all_gather(head_outs, 'head', axis=1, tiled=True)]
    dot_general x31 -> x8, matrix products: 55.6 us -> 9.1 us  [term(): jnp.dot(piece, lax.dynamic_slice_in_dim(out_weight, source * depth, depth...]
    pallas_call x0 -> x1, Pallas kernels: none -> 20.6 us  [attention(): pl.pallas_call(attention_kernel, out_shape=jax.ShapeDtypeStruct(queries.s...]
    while x62 -> x0, local copies, waits for them, and re-layouts: 20.4 us -> none
    ppermute x31 -> x29, waiting for transfers between devices: 19.1 us -> 34.5 us  [the longest x11 19.7 us: turned(): lax.ppermute(value, axis, [(source, (source + steps) % size) for source i...]
    reduce_sum x31 -> x0, other arithmetic: 8.8 us -> none  [the longest x15 7.44 us: attend(): row_sums = row_sums * shrink + jnp.sum(exp_scores, axis=-1)]
    cond x31 -> x0, local copies, waits for them, and re-layouts: 4.7 us -> none
  transfers between devices with their start and end apart: 32 -> 29, of which waited for: 17 -> 10; matrix products, arithmetic and copies ran while one was open for 17% -> 8% of each run, Pallas kernels for 0% -> 0%
where the time goes in v1:
time: 95.6 us; the launch traced here: 97.1 us
  waiting for transfers between devices  34.5 us (36%)
  starting transfers between devices  29.2 us (31%)
  Pallas kernels  20.6 us (22%)
  matrix products  9.1 us (10%)
  local copies, waits for them, and re-layouts  3.45 us (4%)
    pallas_call x1, Pallas kernels, attention(): pl.pallas_call(attention_kernel, out_shape=jax.ShapeDtypeStruct(queries.s...  20.6 us
    ppermute x11, waiting for transfers between devices, turned(): lax.ppermute(value, axis, [(source, (source + steps) % size) for source i...  19.7 us
    ppermute x11, starting transfers between devices, turned(): lax.ppermute(value, axis, [(source, (source + steps) % size) for source i...  18.4 us
    ppermute x18, waiting for transfers between devices, swapped(): lax.ppermute(value, axis, [(source, source ^ flip) for source in range(la...  14.9 us
    ppermute x18, starting transfers between devices, swapped(): lax.ppermute(value, axis, [(source, source ^ flip) for source in range(la...  10.8 us
    dot_general x8, matrix products, term(): jnp.dot(piece, lax.dynamic_slice_in_dim(out_weight, source * depth, depth...  9.1 us
    unnamed x7, local copies, waits for them, and re-layouts  2.55 us
  transfers between devices with their start and end apart: 29, of which 10 were waited for; matrix products, arithmetic and copies ran while one was open for 8% of the time, Pallas kernels for 0%

profile of v1, /device:TPU:98, one launch (start us, length us, event | category | flops | bytes accessed | tf_op | source)
XLA Modules:
  0.0 97.1 jit_solution(14858784478288727647)
XLA Ops:
  0.0 0.9 constant_dynamic-update-slice_fusion.1
  0.9 0.9 constant_dynamic-update-slice_fusion.refs_0_
  1.7 3.2 %collective-permute-start.3 = (bf16[256,256]{1,0:T(8,128)(2,1)S(1)}, bf16[256,256]{1,0:T(8,128)(2,1)S(1)}, u32[]{:S(2)}, u32[]{:S(2)}) collective-permute-start(bf16[256,256]{1,0:T(8,128)(2,1)S(1)} %constant_dynamic-update-slice_fusion.refs_0_), channel_id=1, source_target_pairs={{0,32},{8,40},{16,48},{24,56},{32,64},{40,72},{48,80},{56,88},{64,... | collective-permute-start | bytes 393224 | tf_op jit(solution)/shard_map/ppermute | solution.py:125
  4.9 0.0 collective-permute-start.15
  4.9 0.5 collective-permute-start.1
  5.5 0.0 collective-permute-start
  5.5 2.2 %collective-permute-done.3.refs_4_ = bf16[256,256]{1,0:T(8,128)(2,1)S(1)} collective-permute-done((bf16[256,256]{1,0:T(8,128)(2,1)S(1)}, bf16[256,256]{1,0:T(8,128)(2,1)S(1)}, u32[]{:S(2)}, u32[]{:S(2)}) %collective-permute-start.3) | collective-permute-done | bytes 131104 | tf_op jit(solution)/shard_map/ppermute | solution.py:125
  7.7 3.7 %collective-permute-start.7 = (bf16[256,256]{1,0:T(8,128)(2,1)S(1)}, bf16[256,256]{1,0:T(8,128)(2,1)S(1)}, u32[]{:S(2)}, u32[]{:S(2)}) collective-permute-start(bf16[256,256]{1,0:T(8,128)(2,1)S(1)} %collective-permute-done.3.refs_4_), channel_id=1, source_target_pairs={{0,32},{8,40},{16,48},{24,56},{32,64},{40,72},{48,80},{56,88},{64,... | collective-permute-start | bytes 393224 | tf_op jit(solution)/shard_map/ppermute | solution.py:125
  11.4 0.5 collective-permute-start.5
  11.9 2.4 %collective-permute-done.15 = bf16[256,256]{1,0:T(8,128)(2,1)S(1)} collective-permute-done((bf16[256,256]{1,0:T(8,128)(2,1)S(1)}, bf16[256,256]{1,0:T(8,128)(2,1)S(1)}, u32[]{:S(2)}, u32[]{:S(2)}) %collective-permute-start.15) | collective-permute-done | bytes 131104 | tf_op jit(solution)/shard_map/ppermute | solution.py:125
  14.3 0.0 collective-permute-start.16
  14.3 0.0 collective-permute-done.1.refs_2_
  14.3 0.0 collective-permute-start.4
  14.3 0.0 collective-permute-done.refs_1_
  14.3 0.5 collective-permute-start.2
  14.8 0.0 collective-permute-done.7.refs_8_
  14.8 2.7 %collective-permute-start.11 = (bf16[256,256]{1,0:T(8,128)(2,1)S(1)}, bf16[256,256]{1,0:T(8,128)(2,1)S(1)}, u32[]{:S(2)}, u32[]{:S(2)}) collective-permute-start(bf16[256,256]{1,0:T(8,128)(2,1)S(1)} %collective-permute-done.7.refs_8_), channel_id=1, source_target_pairs={{0,32},{8,40},{16,48},{24,56},{32,64},{40,72},{48,80},{56,88},{64,... | collective-permute-start | bytes 393224 | tf_op jit(solution)/shard_map/ppermute | solution.py:125
  17.6 0.0 collective-permute-done.5.refs_6_
  17.6 0.5 collective-permute-start.9
  18.1 5.1 %collective-permute-done.16.refs_16_ = bf16[256,256]{1,0:T(8,128)(2,1)S(1)} collective-permute-done((bf16[256,256]{1,0:T(8,128)(2,1)S(1)}, bf16[256,256]{1,0:T(8,128)(2,1)S(1)}, u32[]{:S(2)}, u32[]{:S(2)}) %collective-permute-start.16) | collective-permute-done | bytes 131104 | tf_op jit(solution)/shard_map/ppermute | solution.py:125
  23.2 0.0 collective-permute-start.8
  23.2 0.0 collective-permute-done.4.refs_5_
  23.2 0.5 collective-permute-start.6
  23.7 0.0 collective-permute-done.2.refs_3_
  23.7 0.5 collective-permute-start.18
  24.2 0.0 collective-permute-done.11.refs_12_
  24.2 1.5 %collective-permute-start.13 = (bf16[256,256]{1,0:T(8,128)(2,1)S(1)}, bf16[256,256]{1,0:T(8,128)(2,1)S(1)}, u32[]{:S(2)}, u32[]{:S(2)}) collective-permute-start(bf16[256,256]{1,0:T(8,128)(2,1)S(1)} %collective-permute-done.11.refs_12_), channel_id=1, source_target_pairs={{0,16},{8,24},{16,0},{24,8},{32,48},{40,56},{48,32},{56,40},{64,80... | collective-permute-start | bytes 393224 | tf_op jit(solution)/shard_map/ppermute | solution.py:129
  25.7 0.0 collective-permute-done.9.refs_10_
  25.7 0.0 collective-permute-start.17
  25.7 0.5 collective-permute-start.12
  26.2 0.1 collective-permute-start.10
  26.3 3.7 %collective-permute-done.18.refs_18_ = bf16[256,256]{1,0:T(8,128)(2,1)S(1)} collective-permute-done((bf16[256,256]{1,0:T(8,128)(2,1)S(1)}, bf16[256,256]{1,0:T(8,128)(2,1)S(1)}, u32[]{:S(2)}, u32[]{:S(2)}) %collective-permute-start.18) | collective-permute-done | bytes 131104 | tf_op jit(solution)/shard_map/ppermute | solution.py:129
  30.0 0.0 collective-permute-start.19
  30.0 1.9 %collective-permute-done.13.refs_14_ = bf16[256,256]{1,0:T(8,128)(2,1)S(1)} collective-permute-done((bf16[256,256]{1,0:T(8,128)(2,1)S(1)}, bf16[256,256]{1,0:T(8,128)(2,1)S(1)}, u32[]{:S(2)}, u32[]{:S(2)}) %collective-permute-start.13) | collective-permute-done | bytes 131104 | tf_op jit(solution)/shard_map/ppermute | solution.py:129
  32.0 0.0 collective-permute-start.14
  32.0 0.0 collective-permute-done.17.refs_17_
  32.0 0.0 collective-permute-done.19.refs_19_
  32.0 1.3 %collective-permute-done.14.refs_15_ = bf16[256,256]{1,0:T(8,128)(2,1)S(1)} collective-permute-done((bf16[256,256]{1,0:T(8,128)(2,1)S(1)}, bf16[256,256]{1,0:T(8,128)(2,1)S(1)}, u32[]{:S(2)}, u32[]{:S(2)}) %collective-permute-start.14) | collective-permute-done | bytes 131104 | tf_op jit(solution)/shard_map/ppermute | solution.py:129
  33.3 1.0 %copy-done = bf16[256,1024]{1,0:T(8,128)(2,1)S(1)} copy-done((bf16[256,1024]{1,0:T(8,128)(2,1)S(1)}, bf16[256,1024]{1,0:T(8,128)(2,1)}, u32[]{:S(2)}) %copy-start) | copy-done | bytes 524312
  34.4 0.7 copy-done.1
  35.0 20.6 %attention.1 = bf16[256,1024]{1,0:T(8,128)(2,1)S(1)} custom-call(s32[1]{0:T(128)} %bitcast.ctx_ref, s32[8]{0:T(128)S(1)} %copy-done.1, bf16[256,1024]{1,0:T(8,128)(2,1)S(1)} %copy-done, bf16[256,256]{1,0:T(8,128)(2,1)S(1)} %constant_dynamic-update-slice_fusion.refs_0_, bf16[256,256]{1,0:T(8,128)(2,1)S(1)} %collective-permute-done.refs_1_, ...), custom_call_target="tpu_custom_call" | custom-call | flops 5000000000 | bytes 4000000 | tf_op jit(solution)/shard_map/attention/pallas_call | solution.py:105
  55.6 1.6 %collective-permute-start.20 = (bf16[256,1024]{1,0:T(8,128)(2,1)S(1)}, bf16[256,1024]{1,0:T(8,128)(2,1)S(1)}, u32[]{:S(2)}, u32[]{:S(2)}) collective-permute-start(bf16[256,1024]{1,0:T(8,128)(2,1)S(1)} %attention.1), channel_id=1, source_target_pairs={{0,2},{1,3},{2,4},{3,5},{4,6},{5,7},{6,0},{7,1},{8,10},{9,11},{10,... | collective-permute-start | bytes 1572872 | tf_op jit(solution)/shard_map/ppermute | solution.py:125
  57.3 1.7 %collective-permute-start.21 = (bf16[256,1024]{1,0:T(8,128)(2,1)S(1)}, bf16[256,1024]{1,0:T(8,128)(2,1)S(1)}, u32[]{:S(2)}, u32[]{:S(2)}) collective-permute-start(bf16[256,1024]{1,0:T(8,128)(2,1)S(1)} %attention.1), channel_id=1, source_target_pairs={{0,6},{1,7},{2,0},{3,1},{4,2},{5,3},{6,4},{7,5},{8,14},{9,15},{10,... | collective-permute-start | bytes 1572872 | tf_op jit(solution)/shard_map/ppermute | solution.py:125
  59.0 2.1 %collective-permute-start.22 = (bf16[256,1024]{1,0:T(8,128)(2,1)S(1)}, bf16[256,1024]{1,0:T(8,128)(2,1)S(1)}, u32[]{:S(2)}, u32[]{:S(2)}) collective-permute-start(bf16[256,1024]{1,0:T(8,128)(2,1)S(1)} %attention.1), channel_id=1, source_target_pairs={{0,1},{1,0},{2,3},{3,2},{4,5},{5,4},{6,7},{7,6},{8,9},{9,8},{10,11... | collective-permute-start | bytes 1572872 | tf_op jit(solution)/shard_map/ppermute | solution.py:129
  61.0 9.9 %collective-permute-done.20 = bf16[256,1024]{1,0:T(8,128)(2,1)S(1)} collective-permute-done((bf16[256,1024]{1,0:T(8,128)(2,1)S(1)}, bf16[256,1024]{1,0:T(8,128)(2,1)S(1)}, u32[]{:S(2)}, u32[]{:S(2)}) %collective-permute-start.20) | collective-permute-done | bytes 524320 | tf_op jit(solution)/shard_map/ppermute | solution.py:125
  70.9 0.4 collective-permute-start.23
  71.4 3.0 %collective-permute-start.24 = (bf16[128,1024]{1,0:T(8,128)(2,1)S(1)}, bf16[128,1024]{1,0:T(8,128)(2,1)S(1)}, u32[]{:S(2)}, u32[]{:S(2)}) collective-permute-start(bf16[128,1024]{1,0:T(8,128)(2,1)S(1)} %slice.9), channel_id=1, source_target_pairs={{0,6},{1,7},{2,0},{3,1},{4,2},{5,3},{6,4},{7,5},{8,14},{9,15},{10,... | collective-permute-start | bytes 786440 | tf_op jit(solution)/shard_map/ppermute | solution.py:125
  74.4 1.3 %collective-permute-start.26 = (bf16[256,1024]{1,0:T(8,128)(2,1)S(1)}, bf16[256,1024]{1,0:T(8,128)(2,1)S(1)}, u32[]{:S(2)}, u32[]{:S(2)}) collective-permute-start(bf16[256,1024]{1,0:T(8,128)(2,1)S(1)} %collective-permute-done.22), channel_id=1, source_target_pairs={{0,6},{1,7},{2,0},{3,1},{4,2},{5,3},{6,4},{7,5},{8,14},{9,15},{10,... | collective-permute-start | bytes 1572872 | tf_op jit(solution)/shard_map/ppermute | solution.py:125
  75.6 0.8 collective-permute-start.25
  76.4 1.7 %fusion.15 = f32[256,512]{1,0:T(8,128)S(1)} fusion(bf16[256,1024]{1,0:T(8,128)(2,1)S(1)} %collective-permute-done.21, bf16[8192,512]{1,0:T(8,128)(2,1)} %param.9, s32[]{:T(128)S(6)} %select_n.56), kind=kOutput, calls=%fused_computation.17 | convolution fusion | flops 268435456 | bytes 2097156 | tf_op jit(solution)/shard_map/dot_general | solution.py:162
  78.1 1.7 %fusion.17 = f32[256,512]{1,0:T(8,128)S(1)} fusion(bf16[256,1024]{1,0:T(8,128)(2,1)S(1)} %collective-permute-done.20, bf16[8192,512]{1,0:T(8,128)(2,1)} %param.9, s32[]{:T(128)S(6)} %select_n.54), kind=kOutput, calls=%fused_computation.19 | convolution fusion | flops 268435456 | bytes 2097156 | tf_op jit(solution)/shard_map/dot_general | solution.py:162
  79.7 1.7 %fusion.13 = f32[256,512]{1,0:T(8,128)S(1)} fusion(bf16[256,1024]{1,0:T(8,128)(2,1)S(1)} %collective-permute-done.22, bf16[8192,512]{1,0:T(8,128)(2,1)} %param.9, s32[]{:T(128)S(6)} %select_n.57), kind=kOutput, calls=%fused_computation.15 | convolution fusion | flops 268435456 | bytes 2097156 | tf_op jit(solution)/shard_map/dot_general | solution.py:162
  81.4 0.1 collective-permute-done.23
  81.5 2.1 %collective-permute-start.27 = (bf16[128,1024]{1,0:T(8,128)(2,1)S(1)}, bf16[128,1024]{1,0:T(8,128)(2,1)S(1)}, u32[]{:S(2)}, u32[]{:S(2)}) collective-permute-start(bf16[128,1024]{1,0:T(8,128)(2,1)S(1)} %collective-permute-done.23), channel_id=1, source_target_pairs={{0,1},{1,0},{2,3},{3,2},{4,5},{5,4},{6,7},{7,6},{8,9},{9,8},{10,11... | collective-permute-start | bytes 786440 | tf_op jit(solution)/shard_map/ppermute | solution.py:129
  83.6 1.4 %collective-permute-start.28 = (bf16[128,1024]{1,0:T(8,128)(2,1)S(1)}, bf16[128,1024]{1,0:T(8,128)(2,1)S(1)}, u32[]{:S(2)}, u32[]{:S(2)}) collective-permute-start(bf16[128,1024]{1,0:T(8,128)(2,1)S(1)} %collective-permute-done.24), channel_id=1, source_target_pairs={{0,1},{1,0},{2,3},{3,2},{4,5},{5,4},{6,7},{7,6},{8,9},{9,8},{10,11... | collective-permute-start | bytes 786440 | tf_op jit(solution)/shard_map/ppermute | solution.py:129
  85.0 1.7 %fusion.11 = f32[256,512]{1,0:T(8,128)S(1)} fusion(bf16[8192,512]{1,0:T(8,128)(2,1)} %param.9, s32[]{:T(128)S(6)} %select_n.59, bf16[128,1024]{1,0:T(8,128)(2,1)S(1)} %collective-permute-done.24, bf16[128,1024]{1,0:T(8,128)(2,1)S(1)} %collective-permute-done.23), kind=kOutput, calls=%fused_computation.13 | convolution fusion | flops 269484032 | bytes 2097156 | tf_op jit(solution)/shard_map/dot_general | solution.py:162
  86.7 0.5 fusion.4
  87.2 5.1 %collective-permute-done.27 = bf16[128,1024]{1,0:T(8,128)(2,1)S(1)} collective-permute-done((bf16[128,1024]{1,0:T(8,128)(2,1)S(1)}, bf16[128,1024]{1,0:T(8,128)(2,1)S(1)}, u32[]{:S(2)}, u32[]{:S(2)}) %collective-permute-start.27) | collective-permute-done | bytes 262176 | tf_op jit(solution)/shard_map/ppermute | solution.py:129
  92.2 2.8 %collective-permute-done.28 = bf16[128,1024]{1,0:T(8,128)(2,1)S(1)} collective-permute-done((bf16[128,1024]{1,0:T(8,128)(2,1)S(1)}, bf16[128,1024]{1,0:T(8,128)(2,1)S(1)}, u32[]{:S(2)}, u32[]{:S(2)}) %collective-permute-start.28) | collective-permute-done | bytes 262176 | tf_op jit(solution)/shard_map/ppermute | solution.py:129
  95.0 0.4 fusion.6
  95.5 0.0 collective-permute-done.26
  95.5 0.4 fusion.8
  95.9 0.0 collective-permute-done.25
  95.9 1.2 %fusion.5 = bf16[256,512]{1,0:T(8,128)(2,1)} fusion(f32[256,512]{1,0:T(8,128)S(1)} %fusion.6, f32[256,512]{1,0:T(8,128)S(1)} %fusion.8, f32[256,512]{1,0:T(8,128)S(1)} %fusion.4, bf16[256,1024]{1,0:T(8,128)(2,1)S(1)} %collective-permute-done.25, bf16[8192,512]{1,0:T(8,128)(2,1)S(1)} %copy-done.2, s32[]{:T(128)S(6)} %select_n.60), kind=kOutput, calls=%fused_computation.7 | convolution fusion | flops 268959744 | bytes 3407876 | tf_op jit(solution)/shard_map/dot_general | solution.py:162
  (13 shorter events, 0.1 us)
Async XLA Ops:
  1.7 6.0 %collective-permute-start.3 = (bf16[256,256]{1,0:T(8,128)(2,1)S(1)}, bf16[256,256]{1,0:T(8,128)(2,1)S(1)}, u32[]{:S(2)}, u32[]{:S(2)}) collective-permute-start(bf16[256,256]{1,0:T(8,128)(2,1)S(1)} %constant_dynamic-update-slice_fusion.refs_0_), channel_id=1, source_target_pairs={{0,32},{8,40},{16,48},{24,56},{32,64},{40,72},{48,80},{56,88},{64,... | collective-permute-start | bytes 393224 | tf_op jit(solution)/shard_map/ppermute | solution.py:125
  4.9 9.4 %collective-permute-start.15 = (bf16[256,256]{1,0:T(8,128)(2,1)S(1)}, bf16[256,256]{1,0:T(8,128)(2,1)S(1)}, u32[]{:S(2)}, u32[]{:S(2)}) collective-permute-start(bf16[256,256]{1,0:T(8,128)(2,1)S(1)} %constant_dynamic-update-slice_fusion.refs_0_), channel_id=1, source_target_pairs={{0,192},{8,200},{16,208},{24,216},{32,224},{40,232},{48,240},{56,2... | collective-permute-start | bytes 393224 | tf_op jit(solution)/shard_map/ppermute | solution.py:125
  4.9 9.4 %collective-permute-start.1 = (bf16[256,256]{1,0:T(8,128)(2,1)S(1)}, bf16[256,256]{1,0:T(8,128)(2,1)S(1)}, u32[]{:S(2)}, u32[]{:S(2)}) collective-permute-start(bf16[256,256]{1,0:T(8,128)(2,1)S(1)} %constant_dynamic-update-slice_fusion.refs_0_), channel_id=1, source_target_pairs={{0,16},{8,24},{16,0},{24,8},{32,48},{40,56},{48,32},{56,40},{64,80... | collective-permute-start | bytes 393224 | tf_op jit(solution)/shard_map/ppermute | solution.py:129
  5.5 8.8 %collective-permute-start = (bf16[256,256]{1,0:T(8,128)(2,1)S(1)}, bf16[256,256]{1,0:T(8,128)(2,1)S(1)}, u32[]{:S(2)}, u32[]{:S(2)}) collective-permute-start(bf16[256,256]{1,0:T(8,128)(2,1)S(1)} %constant_dynamic-update-slice_fusion.refs_0_), channel_id=1, source_target_pairs={{0,8},{8,0},{16,24},{24,16},{32,40},{40,32},{48,56},{56,48},{64,72... | collective-permute-start | bytes 393224 | tf_op jit(solution)/shard_map/ppermute | solution.py:129
  7.7 7.1 %collective-permute-start.7 = (bf16[256,256]{1,0:T(8,128)(2,1)S(1)}, bf16[256,256]{1,0:T(8,128)(2,1)S(1)}, u32[]{:S(2)}, u32[]{:S(2)}) collective-permute-start(bf16[256,256]{1,0:T(8,128)(2,1)S(1)} %collective-permute-done.3.refs_4_), channel_id=1, source_target_pairs={{0,32},{8,40},{16,48},{24,56},{32,64},{40,72},{48,80},{56,88},{64,... | collective-permute-start | bytes 393224 | tf_op jit(solution)/shard_map/ppermute | solution.py:125
  11.4 6.2 %collective-permute-start.5 = (bf16[256,256]{1,0:T(8,128)(2,1)S(1)}, bf16[256,256]{1,0:T(8,128)(2,1)S(1)}, u32[]{:S(2)}, u32[]{:S(2)}) collective-permute-start(bf16[256,256]{1,0:T(8,128)(2,1)S(1)} %collective-permute-done.3.refs_4_), channel_id=1, source_target_pairs={{0,16},{8,24},{16,0},{24,8},{32,48},{40,56},{48,32},{56,40},{64,80... | collective-permute-start | bytes 393224 | tf_op jit(solution)/shard_map/ppermute | solution.py:129
  14.3 8.9 %collective-permute-start.16 = (bf16[256,256]{1,0:T(8,128)(2,1)S(1)}, bf16[256,256]{1,0:T(8,128)(2,1)S(1)}, u32[]{:S(2)}, u32[]{:S(2)}) collective-permute-start(bf16[256,256]{1,0:T(8,128)(2,1)S(1)} %collective-permute-done.15), channel_id=1, source_target_pairs={{0,192},{8,200},{16,208},{24,216},{32,224},{40,232},{48,240},{56,2... | collective-permute-start | bytes 393224 | tf_op jit(solution)/shard_map/ppermute | solution.py:125
  14.3 8.9 %collective-permute-start.4 = (bf16[256,256]{1,0:T(8,128)(2,1)S(1)}, bf16[256,256]{1,0:T(8,128)(2,1)S(1)}, u32[]{:S(2)}, u32[]{:S(2)}) collective-permute-start(bf16[256,256]{1,0:T(8,128)(2,1)S(1)} %collective-permute-done.3.refs_4_), channel_id=1, source_target_pairs={{0,8},{8,0},{16,24},{24,16},{32,40},{40,32},{48,56},{56,48},{64,72... | collective-permute-start | bytes 393224 | tf_op jit(solution)/shard_map/ppermute | solution.py:129
  14.3 9.4 %collective-permute-start.2 = (bf16[256,256]{1,0:T(8,128)(2,1)S(1)}, bf16[256,256]{1,0:T(8,128)(2,1)S(1)}, u32[]{:S(2)}, u32[]{:S(2)}) collective-permute-start(bf16[256,256]{1,0:T(8,128)(2,1)S(1)} %collective-permute-done.1.refs_2_), channel_id=1, source_target_pairs={{0,8},{8,0},{16,24},{24,16},{32,40},{40,32},{48,56},{56,48},{64,72... | collective-permute-start | bytes 393224 | tf_op jit(solution)/shard_map/ppermute | solution.py:129
  14.8 9.4 %collective-permute-start.11 = (bf16[256,256]{1,0:T(8,128)(2,1)S(1)}, bf16[256,256]{1,0:T(8,128)(2,1)S(1)}, u32[]{:S(2)}, u32[]{:S(2)}) collective-permute-start(bf16[256,256]{1,0:T(8,128)(2,1)S(1)} %collective-permute-done.7.refs_8_), channel_id=1, source_target_pairs={{0,32},{8,40},{16,48},{24,56},{32,64},{40,72},{48,80},{56,88},{64,... | collective-permute-start | bytes 393224 | tf_op jit(solution)/shard_map/ppermute | solution.py:125
  17.6 8.2 %collective-permute-start.9 = (bf16[256,256]{1,0:T(8,128)(2,1)S(1)}, bf16[256,256]{1,0:T(8,128)(2,1)S(1)}, u32[]{:S(2)}, u32[]{:S(2)}) collective-permute-start(bf16[256,256]{1,0:T(8,128)(2,1)S(1)} %collective-permute-done.7.refs_8_), channel_id=1, source_target_pairs={{0,16},{8,24},{16,0},{24,8},{32,48},{40,56},{48,32},{56,40},{64,80... | collective-permute-start | bytes 393224 | tf_op jit(solution)/shard_map/ppermute | solution.py:129
  23.2 2.6 %collective-permute-start.8 = (bf16[256,256]{1,0:T(8,128)(2,1)S(1)}, bf16[256,256]{1,0:T(8,128)(2,1)S(1)}, u32[]{:S(2)}, u32[]{:S(2)}) collective-permute-start(bf16[256,256]{1,0:T(8,128)(2,1)S(1)} %collective-permute-done.7.refs_8_), channel_id=1, source_target_pairs={{0,8},{8,0},{16,24},{24,16},{32,40},{40,32},{48,56},{56,48},{64,72... | collective-permute-start | bytes 393224 | tf_op jit(solution)/shard_map/ppermute | solution.py:129
  23.2 3.1 %collective-permute-start.6 = (bf16[256,256]{1,0:T(8,128)(2,1)S(1)}, bf16[256,256]{1,0:T(8,128)(2,1)S(1)}, u32[]{:S(2)}, u32[]{:S(2)}) collective-permute-start(bf16[256,256]{1,0:T(8,128)(2,1)S(1)} %collective-permute-done.5.refs_6_), channel_id=1, source_target_pairs={{0,8},{8,0},{16,24},{24,16},{32,40},{40,32},{48,56},{56,48},{64,72... | collective-permute-start | bytes 393224 | tf_op jit(solution)/shard_map/ppermute | solution.py:129
  23.7 6.4 %collective-permute-start.18 = (bf16[256,256]{1,0:T(8,128)(2,1)S(1)}, bf16[256,256]{1,0:T(8,128)(2,1)S(1)}, u32[]{:S(2)}, u32[]{:S(2)}) collective-permute-start(bf16[256,256]{1,0:T(8,128)(2,1)S(1)} %collective-permute-done.16.refs_16_), channel_id=1, source_target_pairs={{0,16},{8,24},{16,0},{24,8},{32,48},{40,56},{48,32},{56,40},{64,80... | collective-permute-start | bytes 393224 | tf_op jit(solution)/shard_map/ppermute | solution.py:129
  24.2 7.8 %collective-permute-start.13 = (bf16[256,256]{1,0:T(8,128)(2,1)S(1)}, bf16[256,256]{1,0:T(8,128)(2,1)S(1)}, u32[]{:S(2)}, u32[]{:S(2)}) collective-permute-start(bf16[256,256]{1,0:T(8,128)(2,1)S(1)} %collective-permute-done.11.refs_12_), channel_id=1, source_target_pairs={{0,16},{8,24},{16,0},{24,8},{32,48},{40,56},{48,32},{56,40},{64,80... | collective-permute-start | bytes 393224 | tf_op jit(solution)/shard_map/ppermute | solution.py:129
  25.7 6.3 %collective-permute-start.17 = (bf16[256,256]{1,0:T(8,128)(2,1)S(1)}, bf16[256,256]{1,0:T(8,128)(2,1)S(1)}, u32[]{:S(2)}, u32[]{:S(2)}) collective-permute-start(bf16[256,256]{1,0:T(8,128)(2,1)S(1)} %collective-permute-done.16.refs_16_), channel_id=1, source_target_pairs={{0,8},{8,0},{16,24},{24,16},{32,40},{40,32},{48,56},{56,48},{64,72... | collective-permute-start | bytes 393224 | tf_op jit(solution)/shard_map/ppermute | solution.py:129
  25.7 6.3 %collective-permute-start.12 = (bf16[256,256]{1,0:T(8,128)(2,1)S(1)}, bf16[256,256]{1,0:T(8,128)(2,1)S(1)}, u32[]{:S(2)}, u32[]{:S(2)}) collective-permute-start(bf16[256,256]{1,0:T(8,128)(2,1)S(1)} %collective-permute-done.11.refs_12_), channel_id=1, source_target_pairs={{0,8},{8,0},{16,24},{24,16},{32,40},{40,32},{48,56},{56,48},{64,72... | collective-permute-start | bytes 393224 | tf_op jit(solution)/shard_map/ppermute | solution.py:129
  26.2 5.8 %collective-permute-start.10 = (bf16[256,256]{1,0:T(8,128)(2,1)S(1)}, bf16[256,256]{1,0:T(8,128)(2,1)S(1)}, u32[]{:S(2)}, u32[]{:S(2)}) collective-permute-start(bf16[256,256]{1,0:T(8,128)(2,1)S(1)} %collective-permute-done.9.refs_10_), channel_id=1, source_target_pairs={{0,8},{8,0},{16,24},{24,16},{32,40},{40,32},{48,56},{56,48},{64,72... | collective-permute-start | bytes 393224 | tf_op jit(solution)/shard_map/ppermute | solution.py:129
  30.0 2.0 %collective-permute-start.19 = (bf16[256,256]{1,0:T(8,128)(2,1)S(1)}, bf16[256,256]{1,0:T(8,128)(2,1)S(1)}, u32[]{:S(2)}, u32[]{:S(2)}) collective-permute-start(bf16[256,256]{1,0:T(8,128)(2,1)S(1)} %collective-permute-done.18.refs_18_), channel_id=1, source_target_pairs={{0,8},{8,0},{16,24},{24,16},{32,40},{40,32},{48,56},{56,48},{64,72... | collective-permute-start | bytes 393224 | tf_op jit(solution)/shard_map/ppermute | solution.py:129
  32.0 1.3 %collective-permute-start.14 = (bf16[256,256]{1,0:T(8,128)(2,1)S(1)}, bf16[256,256]{1,0:T(8,128)(2,1)S(1)}, u32[]{:S(2)}, u32[]{:S(2)}) collective-permute-start(bf16[256,256]{1,0:T(8,128)(2,1)S(1)} %collective-permute-done.13.refs_14_), channel_id=1, source_target_pairs={{0,8},{8,0},{16,24},{24,16},{32,40},{40,32},{48,56},{56,48},{64,72... | collective-permute-start | bytes 393224 | tf_op jit(solution)/shard_map/ppermute | solution.py:129
  33.3 1.0 %copy-start = (bf16[256,1024]{1,0:T(8,128)(2,1)S(1)}, bf16[256,1024]{1,0:T(8,128)(2,1)}, u32[]{:S(2)}) copy-start(bf16[256,1024]{1,0:T(8,128)(2,1)} %q_ref.1) | copy-start | bytes 1572868
  34.4 0.7 copy-start.1
  55.6 15.3 %collective-permute-start.20 = (bf16[256,1024]{1,0:T(8,128)(2,1)S(1)}, bf16[256,1024]{1,0:T(8,128)(2,1)S(1)}, u32[]{:S(2)}, u32[]{:S(2)}) collective-permute-start(bf16[256,1024]{1,0:T(8,128)(2,1)S(1)} %attention.1), channel_id=1, source_target_pairs={{0,2},{1,3},{2,4},{3,5},{4,6},{5,7},{6,0},{7,1},{8,10},{9,11},{10,... | collective-permute-start | bytes 1572872 | tf_op jit(solution)/shard_map/ppermute | solution.py:125
  57.3 14.1 %collective-permute-start.21 = (bf16[256,1024]{1,0:T(8,128)(2,1)S(1)}, bf16[256,1024]{1,0:T(8,128)(2,1)S(1)}, u32[]{:S(2)}, u32[]{:S(2)}) collective-permute-start(bf16[256,1024]{1,0:T(8,128)(2,1)S(1)} %attention.1), channel_id=1, source_target_pairs={{0,6},{1,7},{2,0},{3,1},{4,2},{5,3},{6,4},{7,5},{8,14},{9,15},{10,... | collective-permute-start | bytes 1572872 | tf_op jit(solution)/shard_map/ppermute | solution.py:125
  59.0 15.4 %collective-permute-start.22 = (bf16[256,1024]{1,0:T(8,128)(2,1)S(1)}, bf16[256,1024]{1,0:T(8,128)(2,1)S(1)}, u32[]{:S(2)}, u32[]{:S(2)}) collective-permute-start(bf16[256,1024]{1,0:T(8,128)(2,1)S(1)} %attention.1), channel_id=1, source_target_pairs={{0,1},{1,0},{2,3},{3,2},{4,5},{5,4},{6,7},{7,6},{8,9},{9,8},{10,11... | collective-permute-start | bytes 1572872 | tf_op jit(solution)/shard_map/ppermute | solution.py:129
  61.0 25.7 %copy-start.2 = (bf16[8192,512]{1,0:T(8,128)(2,1)S(1)}, bf16[8192,512]{1,0:T(8,128)(2,1)}, u32[]{:S(2)}) copy-start(bf16[8192,512]{1,0:T(8,128)(2,1)} %param.9) | copy-start | bytes 25165828
  70.9 10.5 %collective-permute-start.23 = (bf16[128,1024]{1,0:T(8,128)(2,1)S(1)}, bf16[128,1024]{1,0:T(8,128)(2,1)S(1)}, u32[]{:S(2)}, u32[]{:S(2)}) collective-permute-start(bf16[128,1024]{1,0:T(8,128)(2,1)S(1)} %slice.8), channel_id=1, source_target_pairs={{0,2},{1,3},{2,4},{3,5},{4,6},{5,7},{6,0},{7,1},{8,10},{9,11},{10,... | collective-permute-start | bytes 786440 | tf_op jit(solution)/shard_map/ppermute | solution.py:125
  71.4 12.2 %collective-permute-start.24 = (bf16[128,1024]{1,0:T(8,128)(2,1)S(1)}, bf16[128,1024]{1,0:T(8,128)(2,1)S(1)}, u32[]{:S(2)}, u32[]{:S(2)}) collective-permute-start(bf16[128,1024]{1,0:T(8,128)(2,1)S(1)} %slice.9), channel_id=1, source_target_pairs={{0,6},{1,7},{2,0},{3,1},{4,2},{5,3},{6,4},{7,5},{8,14},{9,15},{10,... | collective-permute-start | bytes 786440 | tf_op jit(solution)/shard_map/ppermute | solution.py:125
  74.4 21.1 %collective-permute-start.26 = (bf16[256,1024]{1,0:T(8,128)(2,1)S(1)}, bf16[256,1024]{1,0:T(8,128)(2,1)S(1)}, u32[]{:S(2)}, u32[]{:S(2)}) collective-permute-start(bf16[256,1024]{1,0:T(8,128)(2,1)S(1)} %collective-permute-done.22), channel_id=1, source_target_pairs={{0,6},{1,7},{2,0},{3,1},{4,2},{5,3},{6,4},{7,5},{8,14},{9,15},{10,... | collective-permute-start | bytes 1572872 | tf_op jit(solution)/shard_map/ppermute | solution.py:125
  75.6 20.3 %collective-permute-start.25 = (bf16[256,1024]{1,0:T(8,128)(2,1)S(1)}, bf16[256,1024]{1,0:T(8,128)(2,1)S(1)}, u32[]{:S(2)}, u32[]{:S(2)}) collective-permute-start(bf16[256,1024]{1,0:T(8,128)(2,1)S(1)} %collective-permute-done.22), channel_id=1, source_target_pairs={{0,2},{1,3},{2,4},{3,5},{4,6},{5,7},{6,0},{7,1},{8,10},{9,11},{10,... | collective-permute-start | bytes 1572872 | tf_op jit(solution)/shard_map/ppermute | solution.py:125
  81.5 10.7 %collective-permute-start.27 = (bf16[128,1024]{1,0:T(8,128)(2,1)S(1)}, bf16[128,1024]{1,0:T(8,128)(2,1)S(1)}, u32[]{:S(2)}, u32[]{:S(2)}) collective-permute-start(bf16[128,1024]{1,0:T(8,128)(2,1)S(1)} %collective-permute-done.23), channel_id=1, source_target_pairs={{0,1},{1,0},{2,3},{3,2},{4,5},{5,4},{6,7},{7,6},{8,9},{9,8},{10,11... | collective-permute-start | bytes 786440 | tf_op jit(solution)/shard_map/ppermute | solution.py:129
  83.6 11.4 %collective-permute-start.28 = (bf16[128,1024]{1,0:T(8,128)(2,1)S(1)}, bf16[128,1024]{1,0:T(8,128)(2,1)S(1)}, u32[]{:S(2)}, u32[]{:S(2)}) collective-permute-start(bf16[128,1024]{1,0:T(8,128)(2,1)S(1)} %collective-permute-done.24), channel_id=1, source_target_pairs={{0,1},{1,0},{2,3},{3,2},{4,5},{5,4},{6,7},{7,6},{8,9},{9,8},{10,11... | collective-permute-start | bytes 786440 | tf_op jit(solution)/shard_map/ppermute | solution.py:129

commit v2 on v1

--- a/solution.py
+++ b/solution.py
@@ -13,23 +13,26 @@
 FLOOR = -1e20
 LANES = 4
 LEVELS = 5
-CHUNK = 512
+REACH = 16
+STEP = 4
 
 
 def attention_kernel(ctx_ref, docs_ref, q_ref, *refs):
     count = LEVELS * LANES
-    pieces, (out_ref, key_buf, value_buf, max_buf, sum_buf, sem) = refs[:count], refs[count:]
+    pieces, (out_ref, key_buf, value_buf, max_buf, sum_buf, sems) = refs[:count], refs[count:]
     rows = q_ref.shape[0]
     ctx = ctx_ref[0]
     lane = lax.rem(ctx, LANES)
-    window = (ctx - lane - (LEVELS - 1) * LANES) * rows
+    newest = LEVELS * LANES - 1
     copies = []
     for index, piece in enumerate(pieces):
         back, flip = index // LANES, index % LANES
-        slot = (LEVELS - 1 - back) * LANES + lax.bitwise_xor(lane, flip)
-        at = pl.ds(pl.multiple_of(slot * rows, rows), rows)
-        copies.append(pltpu.make_async_copy(piece.at[:, :HEAD_DIM], key_buf.at[at], sem.at[2 * index]))
-        copies.append(pltpu.make_async_copy(piece.at[:, HEAD_DIM:], value_buf.at[at, :HEAD_DIM], sem.at[2 * index + 1]))
+        behind = back * LANES + lane - lax.bitwise_xor(lane, flip)
+        at = pl.ds(pl.multiple_of((newest - behind) * rows, rows), rows)
+        copies.append(pltpu.make_async_copy(piece.at[:, :HEAD_DIM], key_buf.at[at], sems.at[2 * index]))
+        copies.append(
+            pltpu.make_async_copy(piece.at[:, HEAD_DIM:], value_buf.at[at, :HEAD_DIM], sems.at[2 * index + 1])
+        )
     for copy in copies:
         copy.start()
     first_row = ctx * rows
@@ -48,45 +51,49 @@
         copy.wait()
     log_scale = math.log2(math.e) / math.sqrt(HEAD_DIM)
 
-    def one_head(head, begin, key_pos_begin, masked):
-        columns = pl.ds(pl.multiple_of(head * HEAD_DIM, HEAD_DIM), HEAD_DIM)
-        scores = lax.dot_general(
-            q_ref[:, columns],
-            key_buf[pl.ds(begin, CHUNK), :],
-            (((1,), (1,)), ((), ())),
-            preferred_element_type=jnp.float32,
-        )
-        scores = scores * log_scale
-        if masked:
-            key_pos = key_pos_begin + lax.broadcasted_iota(jnp.int32, (1, CHUNK), 1)
-            allowed = (key_pos <= row_pos) & (key_pos >= row_low)
-            scores = jnp.where(allowed, scores, LOW_SCORE)
-        old_max = max_buf[head]
-        new_max = jnp.maximum(old_max, jnp.max(scores, axis=1, keepdims=True))
-        probs = jnp.exp2(scores - new_max[:, :1]).astype(jnp.bfloat16)
-        shrink = jnp.exp2(old_max - new_max)
-        added = jnp.dot(probs, value_buf[pl.ds(begin, CHUNK), :], preferred_element_type=jnp.float32)
-        sum_buf[head] = sum_buf[head] * jnp.concatenate([shrink, shrink], axis=1) + added
-        max_buf[head] = new_max
+    def one_step(begin, size, masked):
+        key_pos = first_row + begin - newest * rows + lax.broadcasted_iota(jnp.int32, (1, size), 1)
+        held = pl.ds(begin, size)
 
-    def one_chunk(chunk, carry):
-        begin = pl.multiple_of(chunk * CHUNK, CHUNK)
-        key_pos_begin = window + begin
-        free = (key_pos_begin >= last_low) & (key_pos_begin + CHUNK - 1 <= first_row)
+        def scores_of(head):
+            scores = lax.dot_general(
+                q_ref[:, head * HEAD_DIM : (head + 1) * HEAD_DIM],
+                key_buf[held, :],
+                (((1,), (1,)), ((), ())),
+                preferred_element_type=jnp.float32,
+            )
+            scores = scores * log_scale
+            if masked:
+                scores = jnp.where((key_pos <= row_pos) & (key_pos >= row_low), scores, LOW_SCORE)
+            return scores
 
-        @pl.when(free)
-        def _():
-            for head in range(GROUP):
-                one_head(head, begin, key_pos_begin, False)
+        scores = scores_of(0)
+        for head in range(GROUP):
+            following = scores_of(head + 1) if head + 1 < GROUP else None
+            old_max = max_buf[head]
+            new_max = jnp.maximum(old_max, jnp.max(scores, axis=1, keepdims=True))
+            probs = jnp.exp2(scores - new_max[:, :1]).astype(jnp.bfloat16)
+            shrink = jnp.exp2(old_max - new_max)
+            added = jnp.dot(probs, value_buf[held, :], preferred_element_type=jnp.float32)
+            sum_buf[head] = sum_buf[head] * jnp.concatenate([shrink, shrink], axis=1) + added
+            max_buf[head] = new_max
+            scores = following
 
-        @pl.when(jnp.logical_not(free))
-        def _():
-            for head in range(GROUP):
-                one_head(head, begin, key_pos_begin, True)
+    step_keys = STEP * rows
+    one_step((newest + 1 - STEP) * rows, step_keys, True)
 
+    def earlier_step(step, carry):
+        begin = pl.multiple_of((newest + 1 - STEP) * rows - step * step_keys, rows)
+        free = first_row + begin - newest * rows >= last_low
+        pl.when(free)(lambda: one_step(begin, step_keys, False))
+        pl.when(jnp.logical_not(free))(lambda: one_step(begin, step_keys, True))
         return carry
 
-    lax.fori_loop((first_low - window) // CHUNK, (first_row + rows - 1 - window) // CHUNK + 1, one_chunk, 0)
+    reach = jnp.maximum(first_row - first_low, 0)
+    own_step = (STEP - 1) * rows
+    steps = jnp.minimum((reach - own_step + step_keys - 1) // step_keys, REACH // STEP - 1)
+    lax.fori_loop(1, steps + 1, earlier_step, 0)
+    pl.when(reach > (REACH - 1) * rows)(lambda: one_step((newest - REACH) * rows, rows, True))
     for head in range(GROUP):
         total = sum_buf[head]
         out_ref[:, head * HEAD_DIM : (head + 1) * HEAD_DIM] = (
@@ -96,7 +103,7 @@
 
 def attention(ctx, doc_lengths, queries, pieces):
     rows = queries.shape[0]
-    held = LEVELS * LANES * rows
+    held = (LEVELS * LANES + LANES - 1) * rows
     smem, vmem, anywhere = (
         pl.BlockSpec(memory_space=pltpu.SMEM),
         pl.BlockSpec(memory_space=pltpu.VMEM),

time: 95.6 us -> 89.9 us (0.940)
  Pallas kernels: 20.6 us -> 14.7 us
    pallas_call x1, Pallas kernels: 20.6 us -> 14.7 us  [attention(): pl.pallas_call(attention_kernel, out_shape=jax.ShapeDtypeStruct(queries.s...]
  transfers between devices with their start and end apart: 29 -> 29, of which waited for: 10 -> 9; matrix products, arithmetic and copies ran while one was open for 8% -> 9% of each run, Pallas kernels for 0% -> 0%
where the time goes in v2:
time: 89.9 us; the launch traced here: 90.5 us
  waiting for transfers between devices  33.7 us (37%)
  starting transfers between devices  29.4 us (33%)
  Pallas kernels  14.7 us (16%)
  matrix products  9.11 us (10%)
  local copies, waits for them, and re-layouts  3.45 us (4%)
    ppermute x11, waiting for transfers between devices, turned(): lax.ppermute(value, axis, [(source, (source + steps) % size) for source i...  19.2 us
    ppermute x11, starting transfers between devices, turned(): lax.ppermute(value, axis, [(source, (source + steps) % size) for source i...  18.4 us
    pallas_call x1, Pallas kernels, attention(): pl.pallas_call(attention_kernel, out_shape=jax.ShapeDtypeStruct(queries.s...  14.7 us
    ppermute x18, waiting for transfers between devices, swapped(): lax.ppermute(value, axis, [(source, source ^ flip) for source in range(la...  14.5 us
    ppermute x18, starting transfers between devices, swapped(): lax.ppermute(value, axis, [(source, source ^ flip) for source in range(la...  11 us
    dot_general x8, matrix products, term(): jnp.dot(piece, lax.dynamic_slice_in_dim(out_weight, source * depth, depth...  9.11 us
    unnamed x7, local copies, waits for them, and re-layouts  2.55 us
  transfers between devices with their start and end apart: 29, of which 9 were waited for; matrix products, arithmetic and copies ran while one was open for 9% of the time, Pallas kernels for 0%

profile of v2, /device:TPU:98, one launch (start us, length us, event | category | flops | bytes accessed | tf_op | source)
XLA Modules:
  0.0 90.5 jit_solution(11875946865884976058)
XLA Ops:
  0.0 0.9 constant_dynamic-update-slice_fusion.1
  0.9 0.9 constant_dynamic-update-slice_fusion.refs_0_
  1.7 3.2 %collective-permute-start.3 = (bf16[256,256]{1,0:T(8,128)(2,1)S(1)}, bf16[256,256]{1,0:T(8,128)(2,1)S(1)}, u32[]{:S(2)}, u32[]{:S(2)}) collective-permute-start(bf16[256,256]{1,0:T(8,128)(2,1)S(1)} %constant_dynamic-update-slice_fusion.refs_0_), channel_id=1, source_target_pairs={{0,32},{8,40},{16,48},{24,56},{32,64},{40,72},{48,80},{56,88},{64,... | collective-permute-start | bytes 393224 | tf_op jit(solution)/shard_map/ppermute | solution.py:132
  4.9 0.0 collective-permute-start.15
  4.9 0.5 collective-permute-start.1
  5.5 0.0 collective-permute-start
  5.5 2.2 %collective-permute-done.3.refs_4_ = bf16[256,256]{1,0:T(8,128)(2,1)S(1)} collective-permute-done((bf16[256,256]{1,0:T(8,128)(2,1)S(1)}, bf16[256,256]{1,0:T(8,128)(2,1)S(1)}, u32[]{:S(2)}, u32[]{:S(2)}) %collective-permute-start.3) | collective-permute-done | bytes 131104 | tf_op jit(solution)/shard_map/ppermute | solution.py:132
  7.7 3.7 %collective-permute-start.7 = (bf16[256,256]{1,0:T(8,128)(2,1)S(1)}, bf16[256,256]{1,0:T(8,128)(2,1)S(1)}, u32[]{:S(2)}, u32[]{:S(2)}) collective-permute-start(bf16[256,256]{1,0:T(8,128)(2,1)S(1)} %collective-permute-done.3.refs_4_), channel_id=1, source_target_pairs={{0,32},{8,40},{16,48},{24,56},{32,64},{40,72},{48,80},{56,88},{64,... | collective-permute-start | bytes 393224 | tf_op jit(solution)/shard_map/ppermute | solution.py:132
  11.4 0.5 collective-permute-start.5
  11.9 2.4 %collective-permute-done.15 = bf16[256,256]{1,0:T(8,128)(2,1)S(1)} collective-permute-done((bf16[256,256]{1,0:T(8,128)(2,1)S(1)}, bf16[256,256]{1,0:T(8,128)(2,1)S(1)}, u32[]{:S(2)}, u32[]{:S(2)}) %collective-permute-start.15) | collective-permute-done | bytes 131104 | tf_op jit(solution)/shard_map/ppermute | solution.py:132
  14.3 0.0 collective-permute-start.16
  14.3 0.0 collective-permute-done.1.refs_2_
  14.3 0.0 collective-permute-start.4
  14.3 0.0 collective-permute-done.refs_1_
  14.3 0.5 collective-permute-start.2
  14.8 2.7 %collective-permute-start.11 = (bf16[256,256]{1,0:T(8,128)(2,1)S(1)}, bf16[256,256]{1,0:T(8,128)(2,1)S(1)}, u32[]{:S(2)}, u32[]{:S(2)}) collective-permute-start(bf16[256,256]{1,0:T(8,128)(2,1)S(1)} %collective-permute-done.7.refs_8_), channel_id=1, source_target_pairs={{0,32},{8,40},{16,48},{24,56},{32,64},{40,72},{48,80},{56,88},{64,... | collective-permute-start | bytes 393224 | tf_op jit(solution)/shard_map/ppermute | solution.py:132
  17.6 0.0 collective-permute-done.5.refs_6_
  17.6 0.5 collective-permute-start.9
  18.1 5.1 %collective-permute-done.16.refs_16_ = bf16[256,256]{1,0:T(8,128)(2,1)S(1)} collective-permute-done((bf16[256,256]{1,0:T(8,128)(2,1)S(1)}, bf16[256,256]{1,0:T(8,128)(2,1)S(1)}, u32[]{:S(2)}, u32[]{:S(2)}) %collective-permute-start.16) | collective-permute-done | bytes 131104 | tf_op jit(solution)/shard_map/ppermute | solution.py:132
  23.2 0.0 collective-permute-start.8
  23.2 0.5 collective-permute-start.6
  23.7 0.5 collective-permute-start.18
  24.2 0.0 collective-permute-done.11.refs_12_
  24.2 1.5 %collective-permute-start.13 = (bf16[256,256]{1,0:T(8,128)(2,1)S(1)}, bf16[256,256]{1,0:T(8,128)(2,1)S(1)}, u32[]{:S(2)}, u32[]{:S(2)}) collective-permute-start(bf16[256,256]{1,0:T(8,128)(2,1)S(1)} %collective-permute-done.11.refs_12_), channel_id=1, source_target_pairs={{0,16},{8,24},{16,0},{24,8},{32,48},{40,56},{48,32},{56,40},{64,80... | collective-permute-start | bytes 393224 | tf_op jit(solution)/shard_map/ppermute | solution.py:136
  25.7 0.0 collective-permute-done.9.refs_10_
  25.7 0.0 collective-permute-start.17
  25.7 0.0 collective-permute-done.8.refs_9_
  25.7 0.5 collective-permute-start.12
  26.2 0.0 collective-permute-done.6.refs_7_
  26.2 0.1 collective-permute-start.10
  26.3 3.7 %collective-permute-done.18.refs_18_ = bf16[256,256]{1,0:T(8,128)(2,1)S(1)} collective-permute-done((bf16[256,256]{1,0:T(8,128)(2,1)S(1)}, bf16[256,256]{1,0:T(8,128)(2,1)S(1)}, u32[]{:S(2)}, u32[]{:S(2)}) %collective-permute-start.18) | collective-permute-done | bytes 131104 | tf_op jit(solution)/shard_map/ppermute | solution.py:136
  30.0 1.9 %collective-permute-done.13.refs_14_ = bf16[256,256]{1,0:T(8,128)(2,1)S(1)} collective-permute-done((bf16[256,256]{1,0:T(8,128)(2,1)S(1)}, bf16[256,256]{1,0:T(8,128)(2,1)S(1)}, u32[]{:S(2)}, u32[]{:S(2)}) %collective-permute-start.13) | collective-permute-done | bytes 131104 | tf_op jit(solution)/shard_map/ppermute | solution.py:136
  32.0 0.0 collective-permute-start.14
  32.0 0.0 collective-permute-done.17.refs_17_
  32.0 0.0 collective-permute-done.12.refs_13_
  32.0 0.0 collective-permute-done.10.refs_11_
  32.0 0.0 collective-permute-done.19.refs_19_
  32.0 1.3 %collective-permute-done.14.refs_15_ = bf16[256,256]{1,0:T(8,128)(2,1)S(1)} collective-permute-done((bf16[256,256]{1,0:T(8,128)(2,1)S(1)}, bf16[256,256]{1,0:T(8,128)(2,1)S(1)}, u32[]{:S(2)}, u32[]{:S(2)}) %collective-permute-start.14) | collective-permute-done | bytes 131104 | tf_op jit(solution)/shard_map/ppermute | solution.py:136
  33.3 1.0 %copy-done = bf16[256,1024]{1,0:T(8,128)(2,1)S(1)} copy-done((bf16[256,1024]{1,0:T(8,128)(2,1)S(1)}, bf16[256,1024]{1,0:T(8,128)(2,1)}, u32[]{:S(2)}) %copy-start) | copy-done | bytes 524312
  34.4 0.7 copy-done.1
  35.0 14.7 %attention.1 = bf16[256,1024]{1,0:T(8,128)(2,1)S(1)} custom-call(s32[1]{0:T(128)} %bitcast.ctx_ref, s32[8]{0:T(128)S(1)} %copy-done.1, bf16[256,1024]{1,0:T(8,128)(2,1)S(1)} %copy-done, bf16[256,256]{1,0:T(8,128)(2,1)S(1)} %constant_dynamic-update-slice_fusion.refs_0_, bf16[256,256]{1,0:T(8,128)(2,1)S(1)} %collective-permute-done.refs_1_, ...), custom_call_target="tpu_custom_call" | custom-call | flops 5000000000 | bytes 4000000 | tf_op jit(solution)/shard_map/attention/pallas_call | solution.py:112
  49.8 1.6 %collective-permute-start.20 = (bf16[256,1024]{1,0:T(8,128)(2,1)S(1)}, bf16[256,1024]{1,0:T(8,128)(2,1)S(1)}, u32[]{:S(2)}, u32[]{:S(2)}) collective-permute-start(bf16[256,1024]{1,0:T(8,128)(2,1)S(1)} %attention.1), channel_id=1, source_target_pairs={{0,2},{1,3},{2,4},{3,5},{4,6},{5,7},{6,0},{7,1},{8,10},{9,11},{10,... | collective-permute-start | bytes 1572872 | tf_op jit(solution)/shard_map/ppermute | solution.py:132
  51.4 1.7 %collective-permute-start.21 = (bf16[256,1024]{1,0:T(8,128)(2,1)S(1)}, bf16[256,1024]{1,0:T(8,128)(2,1)S(1)}, u32[]{:S(2)}, u32[]{:S(2)}) collective-permute-start(bf16[256,1024]{1,0:T(8,128)(2,1)S(1)} %attention.1), channel_id=1, source_target_pairs={{0,6},{1,7},{2,0},{3,1},{4,2},{5,3},{6,4},{7,5},{8,14},{9,15},{10,... | collective-permute-start | bytes 1572872 | tf_op jit(solution)/shard_map/ppermute | solution.py:132
  53.1 2.1 %collective-permute-start.22 = (bf16[256,1024]{1,0:T(8,128)(2,1)S(1)}, bf16[256,1024]{1,0:T(8,128)(2,1)S(1)}, u32[]{:S(2)}, u32[]{:S(2)}) collective-permute-start(bf16[256,1024]{1,0:T(8,128)(2,1)S(1)} %attention.1), channel_id=1, source_target_pairs={{0,1},{1,0},{2,3},{3,2},{4,5},{5,4},{6,7},{7,6},{8,9},{9,8},{10,11... | collective-permute-start | bytes 1572872 | tf_op jit(solution)/shard_map/ppermute | solution.py:136
  55.2 9.5 %collective-permute-done.20 = bf16[256,1024]{1,0:T(8,128)(2,1)S(1)} collective-permute-done((bf16[256,1024]{1,0:T(8,128)(2,1)S(1)}, bf16[256,1024]{1,0:T(8,128)(2,1)S(1)}, u32[]{:S(2)}, u32[]{:S(2)}) %collective-permute-start.20) | collective-permute-done | bytes 524320 | tf_op jit(solution)/shard_map/ppermute | solution.py:132
  64.7 0.4 collective-permute-start.23
  65.1 3.0 %collective-permute-start.24 = (bf16[128,1024]{1,0:T(8,128)(2,1)S(1)}, bf16[128,1024]{1,0:T(8,128)(2,1)S(1)}, u32[]{:S(2)}, u32[]{:S(2)}) collective-permute-start(bf16[128,1024]{1,0:T(8,128)(2,1)S(1)} %slice.9), channel_id=1, source_target_pairs={{0,6},{1,7},{2,0},{3,1},{4,2},{5,3},{6,4},{7,5},{8,14},{9,15},{10,... | collective-permute-start | bytes 786440 | tf_op jit(solution)/shard_map/ppermute | solution.py:132
  68.1 0.0 collective-permute-done.22
  68.1 1.3 %collective-permute-start.26 = (bf16[256,1024]{1,0:T(8,128)(2,1)S(1)}, bf16[256,1024]{1,0:T(8,128)(2,1)S(1)}, u32[]{:S(2)}, u32[]{:S(2)}) collective-permute-start(bf16[256,1024]{1,0:T(8,128)(2,1)S(1)} %collective-permute-done.22), channel_id=1, source_target_pairs={{0,6},{1,7},{2,0},{3,1},{4,2},{5,3},{6,4},{7,5},{8,14},{9,15},{10,... | collective-permute-start | bytes 1572872 | tf_op jit(solution)/shard_map/ppermute | solution.py:132
  69.4 0.8 collective-permute-start.25
  70.2 1.7 %fusion.15 = f32[256,512]{1,0:T(8,128)S(1)} fusion(bf16[256,1024]{1,0:T(8,128)(2,1)S(1)} %collective-permute-done.21, bf16[8192,512]{1,0:T(8,128)(2,1)} %param.9, s32[]{:T(128)S(6)} %select_n.56), kind=kOutput, calls=%fused_computation.17 | convolution fusion | flops 268435456 | bytes 2097156 | tf_op jit(solution)/shard_map/dot_general | solution.py:169
  71.8 1.7 %fusion.17 = f32[256,512]{1,0:T(8,128)S(1)} fusion(bf16[256,1024]{1,0:T(8,128)(2,1)S(1)} %collective-permute-done.20, bf16[8192,512]{1,0:T(8,128)(2,1)} %param.9, s32[]{:T(128)S(6)} %select_n.54), kind=kOutput, calls=%fused_computation.19 | convolution fusion | flops 268435456 | bytes 2097156 | tf_op jit(solution)/shard_map/dot_general | solution.py:169
  73.5 1.7 %fusion.13 = f32[256,512]{1,0:T(8,128)S(1)} fusion(bf16[256,1024]{1,0:T(8,128)(2,1)S(1)} %collective-permute-done.22, bf16[8192,512]{1,0:T(8,128)(2,1)} %param.9, s32[]{:T(128)S(6)} %select_n.57), kind=kOutput, calls=%fused_computation.15 | convolution fusion | flops 268435456 | bytes 2097156 | tf_op jit(solution)/shard_map/dot_general | solution.py:169
  75.2 2.2 %collective-permute-start.27 = (bf16[128,1024]{1,0:T(8,128)(2,1)S(1)}, bf16[128,1024]{1,0:T(8,128)(2,1)S(1)}, u32[]{:S(2)}, u32[]{:S(2)}) collective-permute-start(bf16[128,1024]{1,0:T(8,128)(2,1)S(1)} %collective-permute-done.23), channel_id=1, source_target_pairs={{0,1},{1,0},{2,3},{3,2},{4,5},{5,4},{6,7},{7,6},{8,9},{9,8},{10,11... | collective-permute-start | bytes 786440 | tf_op jit(solution)/shard_map/ppermute | solution.py:136
  77.4 0.0 collective-permute-done.24
  77.4 1.4 %collective-permute-start.28 = (bf16[128,1024]{1,0:T(8,128)(2,1)S(1)}, bf16[128,1024]{1,0:T(8,128)(2,1)S(1)}, u32[]{:S(2)}, u32[]{:S(2)}) collective-permute-start(bf16[128,1024]{1,0:T(8,128)(2,1)S(1)} %collective-permute-done.24), channel_id=1, source_target_pairs={{0,1},{1,0},{2,3},{3,2},{4,5},{5,4},{6,7},{7,6},{8,9},{9,8},{10,11... | collective-permute-start | bytes 786440 | tf_op jit(solution)/shard_map/ppermute | solution.py:136
  78.8 1.7 %fusion.11 = f32[256,512]{1,0:T(8,128)S(1)} fusion(bf16[8192,512]{1,0:T(8,128)(2,1)} %param.9, s32[]{:T(128)S(6)} %select_n.59, bf16[128,1024]{1,0:T(8,128)(2,1)S(1)} %collective-permute-done.24, bf16[128,1024]{1,0:T(8,128)(2,1)S(1)} %collective-permute-done.23), kind=kOutput, calls=%fused_computation.13 | convolution fusion | flops 269484032 | bytes 2097156 | tf_op jit(solution)/shard_map/dot_general | solution.py:169
  80.5 0.5 fusion.4
  80.9 4.7 %collective-permute-done.27 = bf16[128,1024]{1,0:T(8,128)(2,1)S(1)} collective-permute-done((bf16[128,1024]{1,0:T(8,128)(2,1)S(1)}, bf16[128,1024]{1,0:T(8,128)(2,1)S(1)}, u32[]{:S(2)}, u32[]{:S(2)}) %collective-permute-start.27) | collective-permute-done | bytes 262176 | tf_op jit(solution)/shard_map/ppermute | solution.py:136
  85.6 2.8 %collective-permute-done.28 = bf16[128,1024]{1,0:T(8,128)(2,1)S(1)} collective-permute-done((bf16[128,1024]{1,0:T(8,128)(2,1)S(1)}, bf16[128,1024]{1,0:T(8,128)(2,1)S(1)}, u32[]{:S(2)}, u32[]{:S(2)}) %collective-permute-start.28) | collective-permute-done | bytes 262176 | tf_op jit(solution)/shard_map/ppermute | solution.py:136
  88.4 0.4 fusion.6
  88.8 0.0 collective-permute-done.26
  88.9 0.4 fusion.8
  89.3 1.2 %fusion.5 = bf16[256,512]{1,0:T(8,128)(2,1)} fusion(f32[256,512]{1,0:T(8,128)S(1)} %fusion.6, f32[256,512]{1,0:T(8,128)S(1)} %fusion.8, f32[256,512]{1,0:T(8,128)S(1)} %fusion.4, bf16[256,1024]{1,0:T(8,128)(2,1)S(1)} %collective-permute-done.25, bf16[8192,512]{1,0:T(8,128)(2,1)S(1)} %copy-done.2, s32[]{:T(128)S(6)} %select_n.60), kind=kOutput, calls=%fused_computation.7 | convolution fusion | flops 268959744 | bytes 3407876 | tf_op jit(solution)/shard_map/dot_general | solution.py:169
  (13 shorter events, 0.1 us)
Async XLA Ops:
  1.7 6.0 %collective-permute-start.3 = (bf16[256,256]{1,0:T(8,128)(2,1)S(1)}, bf16[256,256]{1,0:T(8,128)(2,1)S(1)}, u32[]{:S(2)}, u32[]{:S(2)}) collective-permute-start(bf16[256,256]{1,0:T(8,128)(2,1)S(1)} %constant_dynamic-update-slice_fusion.refs_0_), channel_id=1, source_target_pairs={{0,32},{8,40},{16,48},{24,56},{32,64},{40,72},{48,80},{56,88},{64,... | collective-permute-start | bytes 393224 | tf_op jit(solution)/shard_map/ppermute | solution.py:132
  4.9 9.4 %collective-permute-start.15 = (bf16[256,256]{1,0:T(8,128)(2,1)S(1)}, bf16[256,256]{1,0:T(8,128)(2,1)S(1)}, u32[]{:S(2)}, u32[]{:S(2)}) collective-permute-start(bf16[256,256]{1,0:T(8,128)(2,1)S(1)} %constant_dynamic-update-slice_fusion.refs_0_), channel_id=1, source_target_pairs={{0,192},{8,200},{16,208},{24,216},{32,224},{40,232},{48,240},{56,2... | collective-permute-start | bytes 393224 | tf_op jit(solution)/shard_map/ppermute | solution.py:132
  4.9 9.4 %collective-permute-start.1 = (bf16[256,256]{1,0:T(8,128)(2,1)S(1)}, bf16[256,256]{1,0:T(8,128)(2,1)S(1)}, u32[]{:S(2)}, u32[]{:S(2)}) collective-permute-start(bf16[256,256]{1,0:T(8,128)(2,1)S(1)} %constant_dynamic-update-slice_fusion.refs_0_), channel_id=1, source_target_pairs={{0,16},{8,24},{16,0},{24,8},{32,48},{40,56},{48,32},{56,40},{64,80... | collective-permute-start | bytes 393224 | tf_op jit(solution)/shard_map/ppermute | solution.py:136
  5.5 8.8 %collective-permute-start = (bf16[256,256]{1,0:T(8,128)(2,1)S(1)}, bf16[256,256]{1,0:T(8,128)(2,1)S(1)}, u32[]{:S(2)}, u32[]{:S(2)}) collective-permute-start(bf16[256,256]{1,0:T(8,128)(2,1)S(1)} %constant_dynamic-update-slice_fusion.refs_0_), channel_id=1, source_target_pairs={{0,8},{8,0},{16,24},{24,16},{32,40},{40,32},{48,56},{56,48},{64,72... | collective-permute-start | bytes 393224 | tf_op jit(solution)/shard_map/ppermute | solution.py:136
  7.7 7.1 %collective-permute-start.7 = (bf16[256,256]{1,0:T(8,128)(2,1)S(1)}, bf16[256,256]{1,0:T(8,128)(2,1)S(1)}, u32[]{:S(2)}, u32[]{:S(2)}) collective-permute-start(bf16[256,256]{1,0:T(8,128)(2,1)S(1)} %collective-permute-done.3.refs_4_), channel_id=1, source_target_pairs={{0,32},{8,40},{16,48},{24,56},{32,64},{40,72},{48,80},{56,88},{64,... | collective-permute-start | bytes 393224 | tf_op jit(solution)/shard_map/ppermute | solution.py:132
  11.4 6.2 %collective-permute-start.5 = (bf16[256,256]{1,0:T(8,128)(2,1)S(1)}, bf16[256,256]{1,0:T(8,128)(2,1)S(1)}, u32[]{:S(2)}, u32[]{:S(2)}) collective-permute-start(bf16[256,256]{1,0:T(8,128)(2,1)S(1)} %collective-permute-done.3.refs_4_), channel_id=1, source_target_pairs={{0,16},{8,24},{16,0},{24,8},{32,48},{40,56},{48,32},{56,40},{64,80... | collective-permute-start | bytes 393224 | tf_op jit(solution)/shard_map/ppermute | solution.py:136
  14.3 8.9 %collective-permute-start.16 = (bf16[256,256]{1,0:T(8,128)(2,1)S(1)}, bf16[256,256]{1,0:T(8,128)(2,1)S(1)}, u32[]{:S(2)}, u32[]{:S(2)}) collective-permute-start(bf16[256,256]{1,0:T(8,128)(2,1)S(1)} %collective-permute-done.15), channel_id=1, source_target_pairs={{0,192},{8,200},{16,208},{24,216},{32,224},{40,232},{48,240},{56,2... | collective-permute-start | bytes 393224 | tf_op jit(solution)/shard_map/ppermute | solution.py:132
  14.3 8.9 %collective-permute-start.4 = (bf16[256,256]{1,0:T(8,128)(2,1)S(1)}, bf16[256,256]{1,0:T(8,128)(2,1)S(1)}, u32[]{:S(2)}, u32[]{:S(2)}) collective-permute-start(bf16[256,256]{1,0:T(8,128)(2,1)S(1)} %collective-permute-done.3.refs_4_), channel_id=1, source_target_pairs={{0,8},{8,0},{16,24},{24,16},{32,40},{40,32},{48,56},{56,48},{64,72... | collective-permute-start | bytes 393224 | tf_op jit(solution)/shard_map/ppermute | solution.py:136
  14.3 9.4 %collective-permute-start.2 = (bf16[256,256]{1,0:T(8,128)(2,1)S(1)}, bf16[256,256]{1,0:T(8,128)(2,1)S(1)}, u32[]{:S(2)}, u32[]{:S(2)}) collective-permute-start(bf16[256,256]{1,0:T(8,128)(2,1)S(1)} %collective-permute-done.1.refs_2_), channel_id=1, source_target_pairs={{0,8},{8,0},{16,24},{24,16},{32,40},{40,32},{48,56},{56,48},{64,72... | collective-permute-start | bytes 393224 | tf_op jit(solution)/shard_map/ppermute | solution.py:136
  14.8 9.4 %collective-permute-start.11 = (bf16[256,256]{1,0:T(8,128)(2,1)S(1)}, bf16[256,256]{1,0:T(8,128)(2,1)S(1)}, u32[]{:S(2)}, u32[]{:S(2)}) collective-permute-start(bf16[256,256]{1,0:T(8,128)(2,1)S(1)} %collective-permute-done.7.refs_8_), channel_id=1, source_target_pairs={{0,32},{8,40},{16,48},{24,56},{32,64},{40,72},{48,80},{56,88},{64,... | collective-permute-start | bytes 393224 | tf_op jit(solution)/shard_map/ppermute | solution.py:132
  17.6 8.2 %collective-permute-start.9 = (bf16[256,256]{1,0:T(8,128)(2,1)S(1)}, bf16[256,256]{1,0:T(8,128)(2,1)S(1)}, u32[]{:S(2)}, u32[]{:S(2)}) collective-permute-start(bf16[256,256]{1,0:T(8,128)(2,1)S(1)} %collective-permute-done.7.refs_8_), channel_id=1, source_target_pairs={{0,16},{8,24},{16,0},{24,8},{32,48},{40,56},{48,32},{56,40},{64,80... | collective-permute-start | bytes 393224 | tf_op jit(solution)/shard_map/ppermute | solution.py:136
  23.2 2.6 %collective-permute-start.8 = (bf16[256,256]{1,0:T(8,128)(2,1)S(1)}, bf16[256,256]{1,0:T(8,128)(2,1)S(1)}, u32[]{:S(2)}, u32[]{:S(2)}) collective-permute-start(bf16[256,256]{1,0:T(8,128)(2,1)S(1)} %collective-permute-done.7.refs_8_), channel_id=1, source_target_pairs={{0,8},{8,0},{16,24},{24,16},{32,40},{40,32},{48,56},{56,48},{64,72... | collective-permute-start | bytes 393224 | tf_op jit(solution)/shard_map/ppermute | solution.py:136
  23.2 3.1 %collective-permute-start.6 = (bf16[256,256]{1,0:T(8,128)(2,1)S(1)}, bf16[256,256]{1,0:T(8,128)(2,1)S(1)}, u32[]{:S(2)}, u32[]{:S(2)}) collective-permute-start(bf16[256,256]{1,0:T(8,128)(2,1)S(1)} %collective-permute-done.5.refs_6_), channel_id=1, source_target_pairs={{0,8},{8,0},{16,24},{24,16},{32,40},{40,32},{48,56},{56,48},{64,72... | collective-permute-start | bytes 393224 | tf_op jit(solution)/shard_map/ppermute | solution.py:136
  23.7 6.4 %collective-permute-start.18 = (bf16[256,256]{1,0:T(8,128)(2,1)S(1)}, bf16[256,256]{1,0:T(8,128)(2,1)S(1)}, u32[]{:S(2)}, u32[]{:S(2)}) collective-permute-start(bf16[256,256]{1,0:T(8,128)(2,1)S(1)} %collective-permute-done.16.refs_16_), channel_id=1, source_target_pairs={{0,16},{8,24},{16,0},{24,8},{32,48},{40,56},{48,32},{56,40},{64,80... | collective-permute-start | bytes 393224 | tf_op jit(solution)/shard_map/ppermute | solution.py:136
  24.2 7.8 %collective-permute-start.13 = (bf16[256,256]{1,0:T(8,128)(2,1)S(1)}, bf16[256,256]{1,0:T(8,128)(2,1)S(1)}, u32[]{:S(2)}, u32[]{:S(2)}) collective-permute-start(bf16[256,256]{1,0:T(8,128)(2,1)S(1)} %collective-permute-done.11.refs_12_), channel_id=1, source_target_pairs={{0,16},{8,24},{16,0},{24,8},{32,48},{40,56},{48,32},{56,40},{64,80... | collective-permute-start | bytes 393224 | tf_op jit(solution)/shard_map/ppermute | solution.py:136
  25.7 6.3 %collective-permute-start.17 = (bf16[256,256]{1,0:T(8,128)(2,1)S(1)}, bf16[256,256]{1,0:T(8,128)(2,1)S(1)}, u32[]{:S(2)}, u32[]{:S(2)}) collective-permute-start(bf16[256,256]{1,0:T(8,128)(2,1)S(1)} %collective-permute-done.16.refs_16_), channel_id=1, source_target_pairs={{0,8},{8,0},{16,24},{24,16},{32,40},{40,32},{48,56},{56,48},{64,72... | collective-permute-start | bytes 393224 | tf_op jit(solution)/shard_map/ppermute | solution.py:136
  25.7 6.3 %collective-permute-start.12 = (bf16[256,256]{1,0:T(8,128)(2,1)S(1)}, bf16[256,256]{1,0:T(8,128)(2,1)S(1)}, u32[]{:S(2)}, u32[]{:S(2)}) collective-permute-start(bf16[256,256]{1,0:T(8,128)(2,1)S(1)} %collective-permute-done.11.refs_12_), channel_id=1, source_target_pairs={{0,8},{8,0},{16,24},{24,16},{32,40},{40,32},{48,56},{56,48},{64,72... | collective-permute-start | bytes 393224 | tf_op jit(solution)/shard_map/ppermute | solution.py:136
  26.2 5.8 %collective-permute-start.10 = (bf16[256,256]{1,0:T(8,128)(2,1)S(1)}, bf16[256,256]{1,0:T(8,128)(2,1)S(1)}, u32[]{:S(2)}, u32[]{:S(2)}) collective-permute-start(bf16[256,256]{1,0:T(8,128)(2,1)S(1)} %collective-permute-done.9.refs_10_), channel_id=1, source_target_pairs={{0,8},{8,0},{16,24},{24,16},{32,40},{40,32},{48,56},{56,48},{64,72... | collective-permute-start | bytes 393224 | tf_op jit(solution)/shard_map/ppermute | solution.py:136
  30.0 2.0 %collective-permute-start.19 = (bf16[256,256]{1,0:T(8,128)(2,1)S(1)}, bf16[256,256]{1,0:T(8,128)(2,1)S(1)}, u32[]{:S(2)}, u32[]{:S(2)}) collective-permute-start(bf16[256,256]{1,0:T(8,128)(2,1)S(1)} %collective-permute-done.18.refs_18_), channel_id=1, source_target_pairs={{0,8},{8,0},{16,24},{24,16},{32,40},{40,32},{48,56},{56,48},{64,72... | collective-permute-start | bytes 393224 | tf_op jit(solution)/shard_map/ppermute | solution.py:136
  32.0 1.3 %collective-permute-start.14 = (bf16[256,256]{1,0:T(8,128)(2,1)S(1)}, bf16[256,256]{1,0:T(8,128)(2,1)S(1)}, u32[]{:S(2)}, u32[]{:S(2)}) collective-permute-start(bf16[256,256]{1,0:T(8,128)(2,1)S(1)} %collective-permute-done.13.refs_14_), channel_id=1, source_target_pairs={{0,8},{8,0},{16,24},{24,16},{32,40},{40,32},{48,56},{56,48},{64,72... | collective-permute-start | bytes 393224 | tf_op jit(solution)/shard_map/ppermute | solution.py:136
  33.3 1.0 %copy-start = (bf16[256,1024]{1,0:T(8,128)(2,1)S(1)}, bf16[256,1024]{1,0:T(8,128)(2,1)}, u32[]{:S(2)}) copy-start(bf16[256,1024]{1,0:T(8,128)(2,1)} %q_ref.1) | copy-start | bytes 1572868
  34.4 0.7 copy-start.1
  49.8 14.9 %collective-permute-start.20 = (bf16[256,1024]{1,0:T(8,128)(2,1)S(1)}, bf16[256,1024]{1,0:T(8,128)(2,1)S(1)}, u32[]{:S(2)}, u32[]{:S(2)}) collective-permute-start(bf16[256,1024]{1,0:T(8,128)(2,1)S(1)} %attention.1), channel_id=1, source_target_pairs={{0,2},{1,3},{2,4},{3,5},{4,6},{5,7},{6,0},{7,1},{8,10},{9,11},{10,... | collective-permute-start | bytes 1572872 | tf_op jit(solution)/shard_map/ppermute | solution.py:132
  51.4 13.7 %collective-permute-start.21 = (bf16[256,1024]{1,0:T(8,128)(2,1)S(1)}, bf16[256,1024]{1,0:T(8,128)(2,1)S(1)}, u32[]{:S(2)}, u32[]{:S(2)}) collective-permute-start(bf16[256,1024]{1,0:T(8,128)(2,1)S(1)} %attention.1), channel_id=1, source_target_pairs={{0,6},{1,7},{2,0},{3,1},{4,2},{5,3},{6,4},{7,5},{8,14},{9,15},{10,... | collective-permute-start | bytes 1572872 | tf_op jit(solution)/shard_map/ppermute | solution.py:132
  53.1 15.1 %collective-permute-start.22 = (bf16[256,1024]{1,0:T(8,128)(2,1)S(1)}, bf16[256,1024]{1,0:T(8,128)(2,1)S(1)}, u32[]{:S(2)}, u32[]{:S(2)}) collective-permute-start(bf16[256,1024]{1,0:T(8,128)(2,1)S(1)} %attention.1), channel_id=1, source_target_pairs={{0,1},{1,0},{2,3},{3,2},{4,5},{5,4},{6,7},{7,6},{8,9},{9,8},{10,11... | collective-permute-start | bytes 1572872 | tf_op jit(solution)/shard_map/ppermute | solution.py:136
  55.2 25.2 %copy-start.2 = (bf16[8192,512]{1,0:T(8,128)(2,1)S(1)}, bf16[8192,512]{1,0:T(8,128)(2,1)}, u32[]{:S(2)}) copy-start(bf16[8192,512]{1,0:T(8,128)(2,1)} %param.9) | copy-start | bytes 25165828
  64.7 10.4 %collective-permute-start.23 = (bf16[128,1024]{1,0:T(8,128)(2,1)S(1)}, bf16[128,1024]{1,0:T(8,128)(2,1)S(1)}, u32[]{:S(2)}, u32[]{:S(2)}) collective-permute-start(bf16[128,1024]{1,0:T(8,128)(2,1)S(1)} %slice.8), channel_id=1, source_target_pairs={{0,2},{1,3},{2,4},{3,5},{4,6},{5,7},{6,0},{7,1},{8,10},{9,11},{10,... | collective-permute-start | bytes 786440 | tf_op jit(solution)/shard_map/ppermute | solution.py:132
  65.1 12.3 %collective-permute-start.24 = (bf16[128,1024]{1,0:T(8,128)(2,1)S(1)}, bf16[128,1024]{1,0:T(8,128)(2,1)S(1)}, u32[]{:S(2)}, u32[]{:S(2)}) collective-permute-start(bf16[128,1024]{1,0:T(8,128)(2,1)S(1)} %slice.9), channel_id=1, source_target_pairs={{0,6},{1,7},{2,0},{3,1},{4,2},{5,3},{6,4},{7,5},{8,14},{9,15},{10,... | collective-permute-start | bytes 786440 | tf_op jit(solution)/shard_map/ppermute | solution.py:132
  68.1 20.7 %collective-permute-start.26 = (bf16[256,1024]{1,0:T(8,128)(2,1)S(1)}, bf16[256,1024]{1,0:T(8,128)(2,1)S(1)}, u32[]{:S(2)}, u32[]{:S(2)}) collective-permute-start(bf16[256,1024]{1,0:T(8,128)(2,1)S(1)} %collective-permute-done.22), channel_id=1, source_target_pairs={{0,6},{1,7},{2,0},{3,1},{4,2},{5,3},{6,4},{7,5},{8,14},{9,15},{10,... | collective-permute-start | bytes 1572872 | tf_op jit(solution)/shard_map/ppermute | solution.py:132
  69.4 19.9 %collective-permute-start.25 = (bf16[256,1024]{1,0:T(8,128)(2,1)S(1)}, bf16[256,1024]{1,0:T(8,128)(2,1)S(1)}, u32[]{:S(2)}, u32[]{:S(2)}) collective-permute-start(bf16[256,1024]{1,0:T(8,128)(2,1)S(1)} %collective-permute-done.22), channel_id=1, source_target_pairs={{0,2},{1,3},{2,4},{3,5},{4,6},{5,7},{6,0},{7,1},{8,10},{9,11},{10,... | collective-permute-start | bytes 1572872 | tf_op jit(solution)/shard_map/ppermute | solution.py:132
  75.2 10.4 %collective-permute-start.27 = (bf16[128,1024]{1,0:T(8,128)(2,1)S(1)}, bf16[128,1024]{1,0:T(8,128)(2,1)S(1)}, u32[]{:S(2)}, u32[]{:S(2)}) collective-permute-start(bf16[128,1024]{1,0:T(8,128)(2,1)S(1)} %collective-permute-done.23), channel_id=1, source_target_pairs={{0,1},{1,0},{2,3},{3,2},{4,5},{5,4},{6,7},{7,6},{8,9},{9,8},{10,11... | collective-permute-start | bytes 786440 | tf_op jit(solution)/shard_map/ppermute | solution.py:136
  77.4 11.0 %collective-permute-start.28 = (bf16[128,1024]{1,0:T(8,128)(2,1)S(1)}, bf16[128,1024]{1,0:T(8,128)(2,1)S(1)}, u32[]{:S(2)}, u32[]{:S(2)}) collective-permute-start(bf16[128,1024]{1,0:T(8,128)(2,1)S(1)} %collective-permute-done.24), channel_id=1, source_target_pairs={{0,1},{1,0},{2,3},{3,2},{4,5},{5,4},{6,7},{7,6},{8,9},{9,8},{10,11... | collective-permute-start | bytes 786440 | tf_op jit(solution)/shard_map/ppermute | solution.py:136

commit v3 on v2

--- a/solution.py
+++ b/solution.py
@@ -17,11 +17,11 @@
 STEP = 4
 
 
-def attention_kernel(ctx_ref, docs_ref, q_ref, *refs):
+def attention_kernel(meta_ref, q_ref, *refs):
     count = LEVELS * LANES
     pieces, (out_ref, key_buf, value_buf, max_buf, sum_buf, sems) = refs[:count], refs[count:]
     rows = q_ref.shape[0]
-    ctx = ctx_ref[0]
+    ctx = meta_ref[0]
     lane = lax.rem(ctx, LANES)
     newest = LEVELS * LANES - 1
     copies = []
@@ -39,8 +39,8 @@
     row_pos = first_row + lax.broadcasted_iota(jnp.int32, (rows, 1), 0)
     row_low = jnp.zeros((rows, 1), jnp.int32)
     first_low, last_low, end = jnp.int32(0), jnp.int32(0), jnp.int32(0)
-    for doc in range(docs_ref.shape[0]):
-        end = end + docs_ref[doc]
+    for entry in range(1, meta_ref.shape[0]):
+        end = end + meta_ref[entry]
         row_low = jnp.where(end <= row_pos, end, row_low)
         first_low = jnp.where(end <= first_row, end, first_low)
         last_low = jnp.where(end <= first_row + rows - 1, end, last_low)
@@ -102,6 +102,7 @@
 
 
 def attention(ctx, doc_lengths, queries, pieces):
+    meta = jnp.concatenate([ctx, doc_lengths])
     rows = queries.shape[0]
     held = (LEVELS * LANES + LANES - 1) * rows
     smem, vmem, anywhere = (
@@ -112,7 +113,7 @@
     return pl.pallas_call(
         attention_kernel,
         out_shape=jax.ShapeDtypeStruct(queries.shape, jnp.bfloat16),
-        in_specs=[smem, smem, vmem] + [anywhere] * len(pieces),
+        in_specs=[smem, vmem] + [anywhere] * len(pieces),
         out_specs=vmem,
         scratch_shapes=[
             pltpu.VMEM((held, HEAD_DIM), jnp.bfloat16),
@@ -124,7 +125,27 @@
         compiler_params=pltpu.CompilerParams(vmem_limit_bytes=40 * 1024 * 1024),
         cost_estimate=pl.CostEstimate(flops=5 * 10**9, bytes_accessed=4 * 10**6, transcendentals=8 * 10**6),
         name="attention",
-    )(ctx, doc_lengths, queries, *pieces)
+    )(meta, queries, *pieces)
+
+
+def join_kernel(top_ref, bottom_ref, joined_ref):
+    half = top_ref.shape[0]
+    joined_ref[:half] = top_ref[...]
+    joined_ref[half:] = bottom_ref[...]
+
+
+def joined(top, bottom):
+    half, depth = top.shape
+    in_vmem = pl.BlockSpec(memory_space=pltpu.VMEM)
+    return pl.pallas_call(
+        join_kernel,
+        out_shape=jax.ShapeDtypeStruct((2 * half, depth), top.dtype),
+        in_specs=[in_vmem, in_vmem],
+        out_specs=in_vmem,
+        compiler_params=pltpu.CompilerParams(vmem_limit_bytes=40 * 1024 * 1024),
+        cost_estimate=pl.CostEstimate(flops=0, bytes_accessed=2**20, transcendentals=0),
+        name="joined",
+    )(top, bottom)
 
 
 def turned(value, axis, steps):
@@ -157,10 +178,10 @@
     half = rows // 2
     far_top = turned(below[:half], "head", 2)
     far_bottom = turned(above[half:], "head", -2)
+    far = joined(far_top, far_bottom)
     below_beside = turned(beside, "head", 2)
     above_beside = turned(beside, "head", -2)
-    far_beside_top = swapped(far_top, "head", 1)
-    far_beside_bottom = swapped(far_bottom, "head", 1)
+    far_beside = swapped(far, "head", 1)
     depth = queries.shape[1]
     count = lax.axis_size("head")
 
@@ -173,9 +194,9 @@
         )
 
     total = term(attended, 0, 0) + term(below, -1, 0) + term(above, 1, 0) + term(beside, 0, 1)
-    total = total + term(jnp.concatenate([far_top, far_bottom]), 2, 0)
+    total = total + term(far, 2, 0)
     total = total + term(below_beside, -1, 1) + term(above_beside, 1, 1)
-    total = total + term(jnp.concatenate([far_beside_top, far_beside_bottom]), 2, 1)
+    total = total + term(far_beside, 2, 1)
     return total.astype(jnp.bfloat16)
 
 

time: 89.9 us -> 88.8 us (0.988)
  the two profiles are of different devices: /device:TPU:98 before, /device:TPU:166 now
where the time goes in v3:
time: 88.8 us; the launch traced here: 88 us
  waiting for transfers between devices  34.9 us (39%)
  starting transfers between devices  26.7 us (30%)
  Pallas kernels  14.9 us (17%)
  matrix products  7.88 us (9%)
  local copies, waits for them, and re-layouts  2.79 us (3%)
    ppermute x11, waiting for transfers between devices, turned(): lax.ppermute(value, axis, [(source, (source + steps) % size) for source i...  21.4 us
    ppermute x11, starting transfers between devices, turned(): lax.ppermute(value, axis, [(source, (source + steps) % size) for source i...  18 us
    pallas_call x1, Pallas kernels, attention(): pl.pallas_call(attention_kernel, out_shape=jax.ShapeDtypeStruct(queries.s...  14.8 us
    ppermute x17, waiting for transfers between devices, swapped(): lax.ppermute(value, axis, [(source, source ^ flip) for source in range(la...  13.4 us
    ppermute x17, starting transfers between devices, swapped(): lax.ppermute(value, axis, [(source, source ^ flip) for source in range(la...  8.74 us
    dot_general x8, matrix products, term(): jnp.dot(piece, lax.dynamic_slice_in_dim(out_weight, source * depth, depth...  7.88 us
    unnamed x5, local copies, waits for them, and re-layouts  1.9 us
  transfers between devices with their start and end apart: 28, of which 12 were waited for; matrix products, arithmetic and copies ran while one was open for 9% of the time, Pallas kernels for 0%

profile of v3, /device:TPU:166, one launch (start us, length us, event | category | flops | bytes accessed | tf_op | source)
XLA Modules:
  0.0 88.0 jit_solution(7751408873009307249)
XLA Ops:
  0.0 0.9 constant_dynamic-update-slice_fusion.1
  0.9 0.9 constant_dynamic-update-slice_fusion.refs_0_
  1.7 1.1 %collective-permute-start.3 = (bf16[256,256]{1,0:T(8,128)(2,1)S(1)}, bf16[256,256]{1,0:T(8,128)(2,1)S(1)}, u32[]{:S(2)}, u32[]{:S(2)}) collective-permute-start(bf16[256,256]{1,0:T(8,128)(2,1)S(1)} %constant_dynamic-update-slice_fusion.refs_0_), channel_id=1, source_target_pairs={{0,32},{8,40},{16,48},{24,56},{32,64},{40,72},{48,80},{56,88},{64,... | collective-permute-start | bytes 393224 | tf_op jit(solution)/shard_map/ppermute | solution.py:153
  2.8 2.7 %collective-permute-start.15 = (bf16[256,256]{1,0:T(8,128)(2,1)S(1)}, bf16[256,256]{1,0:T(8,128)(2,1)S(1)}, u32[]{:S(2)}, u32[]{:S(2)}) collective-permute-start(bf16[256,256]{1,0:T(8,128)(2,1)S(1)} %constant_dynamic-update-slice_fusion.refs_0_), channel_id=1, source_target_pairs={{0,192},{8,200},{16,208},{24,216},{32,224},{40,232},{48,240},{56,2... | collective-permute-start | bytes 393224 | tf_op jit(solution)/shard_map/ppermute | solution.py:153
  5.5 0.8 collective-permute-start.1
  6.3 0.0 collective-permute-start
  6.3 0.7 collective-permute-done.3.refs_4_
  7.0 1.0 %collective-permute-start.7 = (bf16[256,256]{1,0:T(8,128)(2,1)S(1)}, bf16[256,256]{1,0:T(8,128)(2,1)S(1)}, u32[]{:S(2)}, u32[]{:S(2)}) collective-permute-start(bf16[256,256]{1,0:T(8,128)(2,1)S(1)} %collective-permute-done.3.refs_4_), channel_id=1, source_target_pairs={{0,32},{8,40},{16,48},{24,56},{32,64},{40,72},{48,80},{56,88},{64,... | collective-permute-start | bytes 393224 | tf_op jit(solution)/shard_map/ppermute | solution.py:153
  8.1 0.8 collective-permute-start.5
  8.9 1.4 %collective-permute-done.15 = bf16[256,256]{1,0:T(8,128)(2,1)S(1)} collective-permute-done((bf16[256,256]{1,0:T(8,128)(2,1)S(1)}, bf16[256,256]{1,0:T(8,128)(2,1)S(1)}, u32[]{:S(2)}, u32[]{:S(2)}) %collective-permute-start.15) | collective-permute-done | bytes 131104 | tf_op jit(solution)/shard_map/ppermute | solution.py:153
  10.3 4.6 %collective-permute-start.16 = (bf16[256,256]{1,0:T(8,128)(2,1)S(1)}, bf16[256,256]{1,0:T(8,128)(2,1)S(1)}, u32[]{:S(2)}, u32[]{:S(2)}) collective-permute-start(bf16[256,256]{1,0:T(8,128)(2,1)S(1)} %collective-permute-done.15), channel_id=1, source_target_pairs={{0,192},{8,200},{16,208},{24,216},{32,224},{40,232},{48,240},{56,2... | collective-permute-start | bytes 393224 | tf_op jit(solution)/shard_map/ppermute | solution.py:153
  14.8 0.0 collective-permute-done.1.refs_2_
  14.8 0.0 collective-permute-start.4
  14.8 0.0 collective-permute-done.refs_1_
  14.9 0.5 collective-permute-start.2
  15.4 0.0 collective-permute-done.7.refs_8_
  15.4 0.0 collective-permute-start.11
  15.4 0.0 collective-permute-done.5.refs_6_
  15.4 0.9 %collective-permute-start.9 = (bf16[256,256]{1,0:T(8,128)(2,1)S(1)}, bf16[256,256]{1,0:T(8,128)(2,1)S(1)}, u32[]{:S(2)}, u32[]{:S(2)}) collective-permute-start(bf16[256,256]{1,0:T(8,128)(2,1)S(1)} %collective-permute-done.7.refs_8_), channel_id=1, source_target_pairs={{0,16},{8,24},{16,0},{24,8},{32,48},{40,56},{48,32},{56,40},{64,80... | collective-permute-start | bytes 393224 | tf_op jit(solution)/shard_map/ppermute | solution.py:157
  16.3 2.8 %collective-permute-done.16.refs_16_ = bf16[256,256]{1,0:T(8,128)(2,1)S(1)} collective-permute-done((bf16[256,256]{1,0:T(8,128)(2,1)S(1)}, bf16[256,256]{1,0:T(8,128)(2,1)S(1)}, u32[]{:S(2)}, u32[]{:S(2)}) %collective-permute-start.16) | collective-permute-done | bytes 131104 | tf_op jit(solution)/shard_map/ppermute | solution.py:153
  19.1 0.5 collective-permute-start.6
  19.6 0.8 collective-permute-start.18
  20.5 0.4 collective-permute-done.11.refs_12_
  20.9 0.8 collective-permute-start.13
  21.7 0.0 collective-permute-done.9.refs_10_
  21.7 0.0 collective-permute-start.17
  21.7 0.0 collective-permute-done.8.refs_9_
  21.7 0.5 collective-permute-start.12
  22.2 0.0 collective-permute-done.6.refs_7_
  22.2 0.1 collective-permute-start.10
  22.3 3.7 %collective-permute-done.18.refs_18_ = bf16[256,256]{1,0:T(8,128)(2,1)S(1)} collective-permute-done((bf16[256,256]{1,0:T(8,128)(2,1)S(1)}, bf16[256,256]{1,0:T(8,128)(2,1)S(1)}, u32[]{:S(2)}, u32[]{:S(2)}) %collective-permute-start.18) | collective-permute-done | bytes 131104 | tf_op jit(solution)/shard_map/ppermute | solution.py:157
  26.0 1.9 %collective-permute-done.13.refs_14_ = bf16[256,256]{1,0:T(8,128)(2,1)S(1)} collective-permute-done((bf16[256,256]{1,0:T(8,128)(2,1)S(1)}, bf16[256,256]{1,0:T(8,128)(2,1)S(1)}, u32[]{:S(2)}, u32[]{:S(2)}) %collective-permute-start.13) | collective-permute-done | bytes 131104 | tf_op jit(solution)/shard_map/ppermute | solution.py:157
  28.0 0.0 collective-permute-start.14
  28.0 0.7 pad_add_fusion.meta_ref
  28.7 0.0 collective-permute-done.17.refs_17_
  28.7 0.0 collective-permute-done.12.refs_13_
  28.7 0.0 collective-permute-done.10.refs_11_
  28.7 0.6 collective-permute-done.14.refs_15_
  29.3 1.0 %copy-done = bf16[256,1024]{1,0:T(8,128)(2,1)S(1)} copy-done((bf16[256,1024]{1,0:T(8,128)(2,1)S(1)}, bf16[256,1024]{1,0:T(8,128)(2,1)}, u32[]{:S(2)}) %copy-start) | copy-done | bytes 524312
  30.3 14.8 %attention.1 = bf16[256,1024]{1,0:T(8,128)(2,1)S(1)} custom-call(s32[9]{0:T(128)S(1)} %pad_add_fusion.meta_ref, bf16[256,1024]{1,0:T(8,128)(2,1)S(1)} %copy-done, bf16[256,256]{1,0:T(8,128)(2,1)S(1)} %constant_dynamic-update-slice_fusion.refs_0_, bf16[256,256]{1,0:T(8,128)(2,1)S(1)} %collective-permute-done.refs_1_, ...), custom_call_target="tpu_custom_call" | custom-call | flops 5000000000 | bytes 4000000 | tf_op jit(solution)/shard_map/attention/pallas_call | solution.py:113
  45.2 1.7 %collective-permute-start.20 = (bf16[256,1024]{1,0:T(8,128)(2,1)S(1)}, bf16[256,1024]{1,0:T(8,128)(2,1)S(1)}, u32[]{:S(2)}, u32[]{:S(2)}) collective-permute-start(bf16[256,1024]{1,0:T(8,128)(2,1)S(1)} %attention.1), channel_id=1, source_target_pairs={{0,2},{1,3},{2,4},{3,5},{4,6},{5,7},{6,0},{7,1},{8,10},{9,11},{10,... | collective-permute-start | bytes 1572872 | tf_op jit(solution)/shard_map/ppermute | solution.py:153
  46.9 1.7 %collective-permute-start.21 = (bf16[256,1024]{1,0:T(8,128)(2,1)S(1)}, bf16[256,1024]{1,0:T(8,128)(2,1)S(1)}, u32[]{:S(2)}, u32[]{:S(2)}) collective-permute-start(bf16[256,1024]{1,0:T(8,128)(2,1)S(1)} %attention.1), channel_id=1, source_target_pairs={{0,6},{1,7},{2,0},{3,1},{4,2},{5,3},{6,4},{7,5},{8,14},{9,15},{10,... | collective-permute-start | bytes 1572872 | tf_op jit(solution)/shard_map/ppermute | solution.py:153
  48.5 1.4 %collective-permute-start.22 = (bf16[256,1024]{1,0:T(8,128)(2,1)S(1)}, bf16[256,1024]{1,0:T(8,128)(2,1)S(1)}, u32[]{:S(2)}, u32[]{:S(2)}) collective-permute-start(bf16[256,1024]{1,0:T(8,128)(2,1)S(1)} %attention.1), channel_id=1, source_target_pairs={{0,1},{1,0},{2,3},{3,2},{4,5},{5,4},{6,7},{7,6},{8,9},{9,8},{10,11... | collective-permute-start | bytes 1572872 | tf_op jit(solution)/shard_map/ppermute | solution.py:157
  49.9 9.1 %collective-permute-done.20 = bf16[256,1024]{1,0:T(8,128)(2,1)S(1)} collective-permute-done((bf16[256,1024]{1,0:T(8,128)(2,1)S(1)}, bf16[256,1024]{1,0:T(8,128)(2,1)S(1)}, u32[]{:S(2)}, u32[]{:S(2)}) %collective-permute-start.20) | collective-permute-done | bytes 524320 | tf_op jit(solution)/shard_map/ppermute | solution.py:153
  59.1 0.5 collective-permute-start.23
  59.6 0.2 collective-permute-done.21
  59.8 2.8 %collective-permute-start.24 = (bf16[128,1024]{1,0:T(8,128)(2,1)S(1)}, bf16[128,1024]{1,0:T(8,128)(2,1)S(1)}, u32[]{:S(2)}, u32[]{:S(2)}) collective-permute-start(bf16[128,1024]{1,0:T(8,128)(2,1)S(1)} %slice.9), channel_id=1, source_target_pairs={{0,6},{1,7},{2,0},{3,1},{4,2},{5,3},{6,4},{7,5},{8,14},{9,15},{10,... | collective-permute-start | bytes 786440 | tf_op jit(solution)/shard_map/ppermute | solution.py:153
  62.6 0.5 collective-permute-done.22
  63.1 2.0 %collective-permute-start.26 = (bf16[256,1024]{1,0:T(8,128)(2,1)S(1)}, bf16[256,1024]{1,0:T(8,128)(2,1)S(1)}, u32[]{:S(2)}, u32[]{:S(2)}) collective-permute-start(bf16[256,1024]{1,0:T(8,128)(2,1)S(1)} %collective-permute-done.22), channel_id=1, source_target_pairs={{0,6},{1,7},{2,0},{3,1},{4,2},{5,3},{6,4},{7,5},{8,14},{9,15},{10,... | collective-permute-start | bytes 1572872 | tf_op jit(solution)/shard_map/ppermute | solution.py:153
  65.0 0.1 collective-permute-start.25
  65.1 1.7 %fusion.15 = f32[256,512]{1,0:T(8,128)S(1)} fusion(bf16[256,1024]{1,0:T(8,128)(2,1)S(1)} %collective-permute-done.21, bf16[8192,512]{1,0:T(8,128)(2,1)} %param.9, s32[]{:T(128)S(6)} %select_n.56), kind=kOutput, calls=%fused_computation.17 | convolution fusion | flops 268435456 | bytes 2097156 | tf_op jit(solution)/shard_map/dot_general | solution.py:190
  66.7 1.7 %fusion.17 = f32[256,512]{1,0:T(8,128)S(1)} fusion(bf16[256,1024]{1,0:T(8,128)(2,1)S(1)} %collective-permute-done.20, bf16[8192,512]{1,0:T(8,128)(2,1)} %param.9, s32[]{:T(128)S(6)} %select_n.54), kind=kOutput, calls=%fused_computation.19 | convolution fusion | flops 268435456 | bytes 2097156 | tf_op jit(solution)/shard_map/dot_general | solution.py:190
  68.4 1.7 %fusion.13 = f32[256,512]{1,0:T(8,128)S(1)} fusion(bf16[256,1024]{1,0:T(8,128)(2,1)S(1)} %collective-permute-done.22, bf16[8192,512]{1,0:T(8,128)(2,1)} %param.9, s32[]{:T(128)S(6)} %select_n.57), kind=kOutput, calls=%fused_computation.15 | convolution fusion | flops 268435456 | bytes 2097156 | tf_op jit(solution)/shard_map/dot_general | solution.py:190
  70.1 0.0 collective-permute-done.23.top_ref
  70.1 0.0 collective-permute-done.24.bottom_ref
  70.1 1.5 %collective-permute-start.27 = (bf16[256,1024]{1,0:T(8,128)(2,1)S(1)}, bf16[256,1024]{1,0:T(8,128)(2,1)S(1)}, u32[]{:S(2)}, u32[]{:S(2)}) collective-permute-start(bf16[256,1024]{1,0:T(8,128)(2,1)S(1)} %joined.1), channel_id=1, source_target_pairs={{0,1},{1,0},{2,3},{3,2},{4,5},{5,4},{6,7},{7,6},{8,9},{9,8},{10,11... | collective-permute-start | bytes 1572872 | tf_op jit(solution)/shard_map/ppermute | solution.py:157
  71.6 0.4 fusion.11
  72.1 0.5 fusion.4
  72.5 6.8 %collective-permute-done.26 = bf16[256,1024]{1,0:T(8,128)(2,1)S(1)} collective-permute-done((bf16[256,1024]{1,0:T(8,128)(2,1)S(1)}, bf16[256,1024]{1,0:T(8,128)(2,1)S(1)}, u32[]{:S(2)}, u32[]{:S(2)}) %collective-permute-start.26) | collective-permute-done | bytes 524320 | tf_op jit(solution)/shard_map/ppermute | solution.py:153
  79.3 0.4 fusion.8
  79.7 6.7 %collective-permute-done.27 = bf16[256,1024]{1,0:T(8,128)(2,1)S(1)} collective-permute-done((bf16[256,1024]{1,0:T(8,128)(2,1)S(1)}, bf16[256,1024]{1,0:T(8,128)(2,1)S(1)}, u32[]{:S(2)}, u32[]{:S(2)}) %collective-permute-start.27) | collective-permute-done | bytes 524320 | tf_op jit(solution)/shard_map/ppermute | solution.py:157
  86.4 0.4 fusion.6
  86.9 0.0 collective-permute-done.25
  86.9 1.2 %fusion.5 = bf16[256,512]{1,0:T(8,128)(2,1)} fusion(f32[256,512]{1,0:T(8,128)S(1)} %fusion.6, f32[256,512]{1,0:T(8,128)S(1)} %fusion.8, f32[256,512]{1,0:T(8,128)S(1)} %fusion.4, bf16[256,1024]{1,0:T(8,128)(2,1)S(1)} %collective-permute-done.25, bf16[8192,512]{1,0:T(8,128)(2,1)S(1)} %copy-done.1, s32[]{:T(128)S(6)} %select_n.60), kind=kOutput, calls=%fused_computation.7 | convolution fusion | flops 268959744 | bytes 3407876 | tf_op jit(solution)/shard_map/dot_general | solution.py:190
  (11 shorter events, 0.1 us)
Async XLA Ops:
  1.7 5.3 %collective-permute-start.3 = (bf16[256,256]{1,0:T(8,128)(2,1)S(1)}, bf16[256,256]{1,0:T(8,128)(2,1)S(1)}, u32[]{:S(2)}, u32[]{:S(2)}) collective-permute-start(bf16[256,256]{1,0:T(8,128)(2,1)S(1)} %constant_dynamic-update-slice_fusion.refs_0_), channel_id=1, source_target_pairs={{0,32},{8,40},{16,48},{24,56},{32,64},{40,72},{48,80},{56,88},{64,... | collective-permute-start | bytes 393224 | tf_op jit(solution)/shard_map/ppermute | solution.py:153
  2.8 7.5 %collective-permute-start.15 = (bf16[256,256]{1,0:T(8,128)(2,1)S(1)}, bf16[256,256]{1,0:T(8,128)(2,1)S(1)}, u32[]{:S(2)}, u32[]{:S(2)}) collective-permute-start(bf16[256,256]{1,0:T(8,128)(2,1)S(1)} %constant_dynamic-update-slice_fusion.refs_0_), channel_id=1, source_target_pairs={{0,192},{8,200},{16,208},{24,216},{32,224},{40,232},{48,240},{56,2... | collective-permute-start | bytes 393224 | tf_op jit(solution)/shard_map/ppermute | solution.py:153
  5.5 9.4 %collective-permute-start.1 = (bf16[256,256]{1,0:T(8,128)(2,1)S(1)}, bf16[256,256]{1,0:T(8,128)(2,1)S(1)}, u32[]{:S(2)}, u32[]{:S(2)}) collective-permute-start(bf16[256,256]{1,0:T(8,128)(2,1)S(1)} %constant_dynamic-update-slice_fusion.refs_0_), channel_id=1, source_target_pairs={{0,16},{8,24},{16,0},{24,8},{32,48},{40,56},{48,32},{56,40},{64,80... | collective-permute-start | bytes 393224 | tf_op jit(solution)/shard_map/ppermute | solution.py:157
  6.3 8.5 %collective-permute-start = (bf16[256,256]{1,0:T(8,128)(2,1)S(1)}, bf16[256,256]{1,0:T(8,128)(2,1)S(1)}, u32[]{:S(2)}, u32[]{:S(2)}) collective-permute-start(bf16[256,256]{1,0:T(8,128)(2,1)S(1)} %constant_dynamic-update-slice_fusion.refs_0_), channel_id=1, source_target_pairs={{0,8},{8,0},{16,24},{24,16},{32,40},{40,32},{48,56},{56,48},{64,72... | collective-permute-start | bytes 393224 | tf_op jit(solution)/shard_map/ppermute | solution.py:157
  7.0 8.3 %collective-permute-start.7 = (bf16[256,256]{1,0:T(8,128)(2,1)S(1)}, bf16[256,256]{1,0:T(8,128)(2,1)S(1)}, u32[]{:S(2)}, u32[]{:S(2)}) collective-permute-start(bf16[256,256]{1,0:T(8,128)(2,1)S(1)} %collective-permute-done.3.refs_4_), channel_id=1, source_target_pairs={{0,32},{8,40},{16,48},{24,56},{32,64},{40,72},{48,80},{56,88},{64,... | collective-permute-start | bytes 393224 | tf_op jit(solution)/shard_map/ppermute | solution.py:153
  8.1 7.3 %collective-permute-start.5 = (bf16[256,256]{1,0:T(8,128)(2,1)S(1)}, bf16[256,256]{1,0:T(8,128)(2,1)S(1)}, u32[]{:S(2)}, u32[]{:S(2)}) collective-permute-start(bf16[256,256]{1,0:T(8,128)(2,1)S(1)} %collective-permute-done.3.refs_4_), channel_id=1, source_target_pairs={{0,16},{8,24},{16,0},{24,8},{32,48},{40,56},{48,32},{56,40},{64,80... | collective-permute-start | bytes 393224 | tf_op jit(solution)/shard_map/ppermute | solution.py:157
  10.3 8.8 %collective-permute-start.16 = (bf16[256,256]{1,0:T(8,128)(2,1)S(1)}, bf16[256,256]{1,0:T(8,128)(2,1)S(1)}, u32[]{:S(2)}, u32[]{:S(2)}) collective-permute-start(bf16[256,256]{1,0:T(8,128)(2,1)S(1)} %collective-permute-done.15), channel_id=1, source_target_pairs={{0,192},{8,200},{16,208},{24,216},{32,224},{40,232},{48,240},{56,2... | collective-permute-start | bytes 393224 | tf_op jit(solution)/shard_map/ppermute | solution.py:153
  14.8 4.3 %collective-permute-start.4 = (bf16[256,256]{1,0:T(8,128)(2,1)S(1)}, bf16[256,256]{1,0:T(8,128)(2,1)S(1)}, u32[]{:S(2)}, u32[]{:S(2)}) collective-permute-start(bf16[256,256]{1,0:T(8,128)(2,1)S(1)} %collective-permute-done.3.refs_4_), channel_id=1, source_target_pairs={{0,8},{8,0},{16,24},{24,16},{32,40},{40,32},{48,56},{56,48},{64,72... | collective-permute-start | bytes 393224 | tf_op jit(solution)/shard_map/ppermute | solution.py:157
  14.9 4.8 %collective-permute-start.2 = (bf16[256,256]{1,0:T(8,128)(2,1)S(1)}, bf16[256,256]{1,0:T(8,128)(2,1)S(1)}, u32[]{:S(2)}, u32[]{:S(2)}) collective-permute-start(bf16[256,256]{1,0:T(8,128)(2,1)S(1)} %collective-permute-done.1.refs_2_), channel_id=1, source_target_pairs={{0,8},{8,0},{16,24},{24,16},{32,40},{40,32},{48,56},{56,48},{64,72... | collective-permute-start | bytes 393224 | tf_op jit(solution)/shard_map/ppermute | solution.py:157
  15.4 5.5 %collective-permute-start.11 = (bf16[256,256]{1,0:T(8,128)(2,1)S(1)}, bf16[256,256]{1,0:T(8,128)(2,1)S(1)}, u32[]{:S(2)}, u32[]{:S(2)}) collective-permute-start(bf16[256,256]{1,0:T(8,128)(2,1)S(1)} %collective-permute-done.7.refs_8_), channel_id=1, source_target_pairs={{0,32},{8,40},{16,48},{24,56},{32,64},{40,72},{48,80},{56,88},{64,... | collective-permute-start | bytes 393224 | tf_op jit(solution)/shard_map/ppermute | solution.py:153
  15.4 6.3 %collective-permute-start.9 = (bf16[256,256]{1,0:T(8,128)(2,1)S(1)}, bf16[256,256]{1,0:T(8,128)(2,1)S(1)}, u32[]{:S(2)}, u32[]{:S(2)}) collective-permute-start(bf16[256,256]{1,0:T(8,128)(2,1)S(1)} %collective-permute-done.7.refs_8_), channel_id=1, source_target_pairs={{0,16},{8,24},{16,0},{24,8},{32,48},{40,56},{48,32},{56,40},{64,80... | collective-permute-start | bytes 393224 | tf_op jit(solution)/shard_map/ppermute | solution.py:157
  19.1 2.6 %collective-permute-start.8 = (bf16[256,256]{1,0:T(8,128)(2,1)S(1)}, bf16[256,256]{1,0:T(8,128)(2,1)S(1)}, u32[]{:S(2)}, u32[]{:S(2)}) collective-permute-start(bf16[256,256]{1,0:T(8,128)(2,1)S(1)} %collective-permute-done.7.refs_8_), channel_id=1, source_target_pairs={{0,8},{8,0},{16,24},{24,16},{32,40},{40,32},{48,56},{56,48},{64,72... | collective-permute-start | bytes 393224 | tf_op jit(solution)/shard_map/ppermute | solution.py:157
  19.1 3.1 %collective-permute-start.6 = (bf16[256,256]{1,0:T(8,128)(2,1)S(1)}, bf16[256,256]{1,0:T(8,128)(2,1)S(1)}, u32[]{:S(2)}, u32[]{:S(2)}) collective-permute-start(bf16[256,256]{1,0:T(8,128)(2,1)S(1)} %collective-permute-done.5.refs_6_), channel_id=1, source_target_pairs={{0,8},{8,0},{16,24},{24,16},{32,40},{40,32},{48,56},{56,48},{64,72... | collective-permute-start | bytes 393224 | tf_op jit(solution)/shard_map/ppermute | solution.py:157
  19.6 6.3 %collective-permute-start.18 = (bf16[256,256]{1,0:T(8,128)(2,1)S(1)}, bf16[256,256]{1,0:T(8,128)(2,1)S(1)}, u32[]{:S(2)}, u32[]{:S(2)}) collective-permute-start(bf16[256,256]{1,0:T(8,128)(2,1)S(1)} %collective-permute-done.16.refs_16_), channel_id=1, source_target_pairs={{0,16},{8,24},{16,0},{24,8},{32,48},{40,56},{48,32},{56,40},{64,80... | collective-permute-start | bytes 393224 | tf_op jit(solution)/shard_map/ppermute | solution.py:157
  20.9 7.1 %collective-permute-start.13 = (bf16[256,256]{1,0:T(8,128)(2,1)S(1)}, bf16[256,256]{1,0:T(8,128)(2,1)S(1)}, u32[]{:S(2)}, u32[]{:S(2)}) collective-permute-start(bf16[256,256]{1,0:T(8,128)(2,1)S(1)} %collective-permute-done.11.refs_12_), channel_id=1, source_target_pairs={{0,16},{8,24},{16,0},{24,8},{32,48},{40,56},{48,32},{56,40},{64,80... | collective-permute-start | bytes 393224 | tf_op jit(solution)/shard_map/ppermute | solution.py:157
  21.7 7.0 %collective-permute-start.17 = (bf16[256,256]{1,0:T(8,128)(2,1)S(1)}, bf16[256,256]{1,0:T(8,128)(2,1)S(1)}, u32[]{:S(2)}, u32[]{:S(2)}) collective-permute-start(bf16[256,256]{1,0:T(8,128)(2,1)S(1)} %collective-permute-done.16.refs_16_), channel_id=1, source_target_pairs={{0,8},{8,0},{16,24},{24,16},{32,40},{40,32},{48,56},{56,48},{64,72... | collective-permute-start | bytes 393224 | tf_op jit(solution)/shard_map/ppermute | solution.py:157
  21.7 7.0 %collective-permute-start.12 = (bf16[256,256]{1,0:T(8,128)(2,1)S(1)}, bf16[256,256]{1,0:T(8,128)(2,1)S(1)}, u32[]{:S(2)}, u32[]{:S(2)}) collective-permute-start(bf16[256,256]{1,0:T(8,128)(2,1)S(1)} %collective-permute-done.11.refs_12_), channel_id=1, source_target_pairs={{0,8},{8,0},{16,24},{24,16},{32,40},{40,32},{48,56},{56,48},{64,72... | collective-permute-start | bytes 393224 | tf_op jit(solution)/shard_map/ppermute | solution.py:157
  22.2 6.5 %collective-permute-start.10 = (bf16[256,256]{1,0:T(8,128)(2,1)S(1)}, bf16[256,256]{1,0:T(8,128)(2,1)S(1)}, u32[]{:S(2)}, u32[]{:S(2)}) collective-permute-start(bf16[256,256]{1,0:T(8,128)(2,1)S(1)} %collective-permute-done.9.refs_10_), channel_id=1, source_target_pairs={{0,8},{8,0},{16,24},{24,16},{32,40},{40,32},{48,56},{56,48},{64,72... | collective-permute-start | bytes 393224 | tf_op jit(solution)/shard_map/ppermute | solution.py:157
  26.0 2.7 %collective-permute-start.19 = (bf16[256,256]{1,0:T(8,128)(2,1)S(1)}, bf16[256,256]{1,0:T(8,128)(2,1)S(1)}, u32[]{:S(2)}, u32[]{:S(2)}) collective-permute-start(bf16[256,256]{1,0:T(8,128)(2,1)S(1)} %collective-permute-done.18.refs_18_), channel_id=1, source_target_pairs={{0,8},{8,0},{16,24},{24,16},{32,40},{40,32},{48,56},{56,48},{64,72... | collective-permute-start | bytes 393224 | tf_op jit(solution)/shard_map/ppermute | solution.py:157
  28.0 1.3 %collective-permute-start.14 = (bf16[256,256]{1,0:T(8,128)(2,1)S(1)}, bf16[256,256]{1,0:T(8,128)(2,1)S(1)}, u32[]{:S(2)}, u32[]{:S(2)}) collective-permute-start(bf16[256,256]{1,0:T(8,128)(2,1)S(1)} %collective-permute-done.13.refs_14_), channel_id=1, source_target_pairs={{0,8},{8,0},{16,24},{24,16},{32,40},{40,32},{48,56},{56,48},{64,72... | collective-permute-start | bytes 393224 | tf_op jit(solution)/shard_map/ppermute | solution.py:157
  29.3 1.0 %copy-start = (bf16[256,1024]{1,0:T(8,128)(2,1)S(1)}, bf16[256,1024]{1,0:T(8,128)(2,1)}, u32[]{:S(2)}) copy-start(bf16[256,1024]{1,0:T(8,128)(2,1)} %q_ref.1) | copy-start | bytes 1572868
  45.2 13.9 %collective-permute-start.20 = (bf16[256,1024]{1,0:T(8,128)(2,1)S(1)}, bf16[256,1024]{1,0:T(8,128)(2,1)S(1)}, u32[]{:S(2)}, u32[]{:S(2)}) collective-permute-start(bf16[256,1024]{1,0:T(8,128)(2,1)S(1)} %attention.1), channel_id=1, source_target_pairs={{0,2},{1,3},{2,4},{3,5},{4,6},{5,7},{6,0},{7,1},{8,10},{9,11},{10,... | collective-permute-start | bytes 1572872 | tf_op jit(solution)/shard_map/ppermute | solution.py:153
  46.9 12.9 %collective-permute-start.21 = (bf16[256,1024]{1,0:T(8,128)(2,1)S(1)}, bf16[256,1024]{1,0:T(8,128)(2,1)S(1)}, u32[]{:S(2)}, u32[]{:S(2)}) collective-permute-start(bf16[256,1024]{1,0:T(8,128)(2,1)S(1)} %attention.1), channel_id=1, source_target_pairs={{0,6},{1,7},{2,0},{3,1},{4,2},{5,3},{6,4},{7,5},{8,14},{9,15},{10,... | collective-permute-start | bytes 1572872 | tf_op jit(solution)/shard_map/ppermute | solution.py:153
  48.5 14.5 %collective-permute-start.22 = (bf16[256,1024]{1,0:T(8,128)(2,1)S(1)}, bf16[256,1024]{1,0:T(8,128)(2,1)S(1)}, u32[]{:S(2)}, u32[]{:S(2)}) collective-permute-start(bf16[256,1024]{1,0:T(8,128)(2,1)S(1)} %attention.1), channel_id=1, source_target_pairs={{0,1},{1,0},{2,3},{3,2},{4,5},{5,4},{6,7},{7,6},{8,9},{9,8},{10,11... | collective-permute-start | bytes 1572872 | tf_op jit(solution)/shard_map/ppermute | solution.py:157
  49.9 21.7 %copy-start.1 = (bf16[8192,512]{1,0:T(8,128)(2,1)S(1)}, bf16[8192,512]{1,0:T(8,128)(2,1)}, u32[]{:S(2)}) copy-start(bf16[8192,512]{1,0:T(8,128)(2,1)} %param.9) | copy-start | bytes 25165828
  59.1 11.0 %collective-permute-start.23 = (bf16[128,1024]{1,0:T(8,128)(2,1)S(1)}, bf16[128,1024]{1,0:T(8,128)(2,1)S(1)}, u32[]{:S(2)}, u32[]{:S(2)}) collective-permute-start(bf16[128,1024]{1,0:T(8,128)(2,1)S(1)} %slice.8), channel_id=1, source_target_pairs={{0,2},{1,3},{2,4},{3,5},{4,6},{5,7},{6,0},{7,1},{8,10},{9,11},{10,... | collective-permute-start | bytes 786440 | tf_op jit(solution)/shard_map/ppermute | solution.py:153
  59.8 10.3 %collective-permute-start.24 = (bf16[128,1024]{1,0:T(8,128)(2,1)S(1)}, bf16[128,1024]{1,0:T(8,128)(2,1)S(1)}, u32[]{:S(2)}, u32[]{:S(2)}) collective-permute-start(bf16[128,1024]{1,0:T(8,128)(2,1)S(1)} %slice.9), channel_id=1, source_target_pairs={{0,6},{1,7},{2,0},{3,1},{4,2},{5,3},{6,4},{7,5},{8,14},{9,15},{10,... | collective-permute-start | bytes 786440 | tf_op jit(solution)/shard_map/ppermute | solution.py:153
  63.1 16.2 %collective-permute-start.26 = (bf16[256,1024]{1,0:T(8,128)(2,1)S(1)}, bf16[256,1024]{1,0:T(8,128)(2,1)S(1)}, u32[]{:S(2)}, u32[]{:S(2)}) collective-permute-start(bf16[256,1024]{1,0:T(8,128)(2,1)S(1)} %collective-permute-done.22), channel_id=1, source_target_pairs={{0,6},{1,7},{2,0},{3,1},{4,2},{5,3},{6,4},{7,5},{8,14},{9,15},{10,... | collective-permute-start | bytes 1572872 | tf_op jit(solution)/shard_map/ppermute | solution.py:153
  65.0 21.8 %collective-permute-start.25 = (bf16[256,1024]{1,0:T(8,128)(2,1)S(1)}, bf16[256,1024]{1,0:T(8,128)(2,1)S(1)}, u32[]{:S(2)}, u32[]{:S(2)}) collective-permute-start(bf16[256,1024]{1,0:T(8,128)(2,1)S(1)} %collective-permute-done.22), channel_id=1, source_target_pairs={{0,2},{1,3},{2,4},{3,5},{4,6},{5,7},{6,0},{7,1},{8,10},{9,11},{10,... | collective-permute-start | bytes 1572872 | tf_op jit(solution)/shard_map/ppermute | solution.py:153
  70.1 16.3 %collective-permute-start.27 = (bf16[256,1024]{1,0:T(8,128)(2,1)S(1)}, bf16[256,1024]{1,0:T(8,128)(2,1)S(1)}, u32[]{:S(2)}, u32[]{:S(2)}) collective-permute-start(bf16[256,1024]{1,0:T(8,128)(2,1)S(1)} %joined.1), channel_id=1, source_target_pairs={{0,1},{1,0},{2,3},{3,2},{4,5},{5,4},{6,7},{7,6},{8,9},{9,8},{10,11... | collective-permute-start | bytes 1572872 | tf_op jit(solution)/shard_map/ppermute | solution.py:157

commit v4 on v3

--- a/solution.py
+++ b/solution.py
@@ -128,24 +128,24 @@
     )(meta, queries, *pieces)
 
 
-def join_kernel(top_ref, bottom_ref, joined_ref):
+def join_kernel(top_ref, bottom_ref, below_ref, above_ref, joined_ref, below_out_ref, above_out_ref):
     half = top_ref.shape[0]
     joined_ref[:half] = top_ref[...]
     joined_ref[half:] = bottom_ref[...]
 
 
-def joined(top, bottom):
-    half, depth = top.shape
-    in_vmem = pl.BlockSpec(memory_space=pltpu.VMEM)
+def joined_before(top, bottom, below, above):
+    in_vmem, anywhere = pl.BlockSpec(memory_space=pltpu.VMEM), pl.BlockSpec(memory_space=pl.ANY)
     return pl.pallas_call(
         join_kernel,
-        out_shape=jax.ShapeDtypeStruct((2 * half, depth), top.dtype),
-        in_specs=[in_vmem, in_vmem],
-        out_specs=in_vmem,
+        out_shape=[jax.ShapeDtypeStruct(below.shape, below.dtype)] * 3,
+        in_specs=[in_vmem, in_vmem, anywhere, anywhere],
+        out_specs=[in_vmem, anywhere, anywhere],
+        input_output_aliases={2: 1, 3: 2},
         compiler_params=pltpu.CompilerParams(vmem_limit_bytes=40 * 1024 * 1024),
         cost_estimate=pl.CostEstimate(flops=0, bytes_accessed=2**20, transcendentals=0),
-        name="joined",
-    )(top, bottom)
+        name="joined_before",
+    )(top, bottom, below, above)
 
 
 def turned(value, axis, steps):
@@ -178,7 +178,7 @@
     half = rows // 2
     far_top = turned(below[:half], "head", 2)
     far_bottom = turned(above[half:], "head", -2)
-    far = joined(far_top, far_bottom)
+    far, below, above = joined_before(far_top, far_bottom, below, above)
     below_beside = turned(beside, "head", 2)
     above_beside = turned(beside, "head", -2)
     far_beside = swapped(far, "head", 1)

time: 88.8 us -> 88.6 us (level)
  the two profiles are of different devices: /device:TPU:166 before, /device:TPU:98 now
where the time goes in v4:
time: 88.6 us; the launch traced here: 87.7 us
  waiting for transfers between devices  31.8 us (36%)
  starting transfers between devices  27.9 us (31%)
  Pallas kernels  14.9 us (17%)
  matrix products  9.45 us (11%)
  local copies, waits for them, and re-layouts  2.79 us (3%)
    ppermute x11, waiting for transfers between devices, turned(): lax.ppermute(value, axis, [(source, (source + steps) % size) for source i...  23.1 us
    ppermute x11, starting transfers between devices, turned(): lax.ppermute(value, axis, [(source, (source + steps) % size) for source i...  18.4 us
    pallas_call x1, Pallas kernels, attention(): pl.pallas_call(attention_kernel, out_shape=jax.ShapeDtypeStruct(queries.s...  14.8 us
    ppermute x17, starting transfers between devices, swapped(): lax.ppermute(value, axis, [(source, source ^ flip) for source in range(la...  9.55 us
    dot_general x8, matrix products, term(): jnp.dot(piece, lax.dynamic_slice_in_dim(out_weight, source * depth, depth...  9.45 us
    ppermute x17, waiting for transfers between devices, swapped(): lax.ppermute(value, axis, [(source, source ^ flip) for source in range(la...  8.73 us
    unnamed x5, local copies, waits for them, and re-layouts  1.9 us
  transfers between devices with their start and end apart: 28, of which 10 were waited for; matrix products, arithmetic and copies ran while one was open for 10% of the time, Pallas kernels for 0%

profile of v4, /device:TPU:98, one launch (start us, length us, event | category | flops | bytes accessed | tf_op | source)
XLA Modules:
  0.0 87.7 jit_solution(8676299611390800671)
XLA Ops:
  0.0 0.9 constant_dynamic-update-slice_fusion.1
  0.9 0.9 constant_dynamic-update-slice_fusion.refs_0_
  1.7 3.2 %collective-permute-start.3 = (bf16[256,256]{1,0:T(8,128)(2,1)S(1)}, bf16[256,256]{1,0:T(8,128)(2,1)S(1)}, u32[]{:S(2)}, u32[]{:S(2)}) collective-permute-start(bf16[256,256]{1,0:T(8,128)(2,1)S(1)} %constant_dynamic-update-slice_fusion.refs_0_), channel_id=1, source_target_pairs={{0,32},{8,40},{16,48},{24,56},{32,64},{40,72},{48,80},{56,88},{64,... | collective-permute-start | bytes 393224 | tf_op jit(solution)/shard_map/ppermute | solution.py:153
  4.9 0.0 collective-permute-start.15
  4.9 0.5 collective-permute-start.1
  5.5 0.0 collective-permute-start
  5.5 2.2 %collective-permute-done.3.refs_4_ = bf16[256,256]{1,0:T(8,128)(2,1)S(1)} collective-permute-done((bf16[256,256]{1,0:T(8,128)(2,1)S(1)}, bf16[256,256]{1,0:T(8,128)(2,1)S(1)}, u32[]{:S(2)}, u32[]{:S(2)}) %collective-permute-start.3) | collective-permute-done | bytes 131104 | tf_op jit(solution)/shard_map/ppermute | solution.py:153
  7.7 3.7 %collective-permute-start.7 = (bf16[256,256]{1,0:T(8,128)(2,1)S(1)}, bf16[256,256]{1,0:T(8,128)(2,1)S(1)}, u32[]{:S(2)}, u32[]{:S(2)}) collective-permute-start(bf16[256,256]{1,0:T(8,128)(2,1)S(1)} %collective-permute-done.3.refs_4_), channel_id=1, source_target_pairs={{0,32},{8,40},{16,48},{24,56},{32,64},{40,72},{48,80},{56,88},{64,... | collective-permute-start | bytes 393224 | tf_op jit(solution)/shard_map/ppermute | solution.py:153
  11.4 0.5 collective-permute-start.5
  11.9 2.4 %collective-permute-done.15 = bf16[256,256]{1,0:T(8,128)(2,1)S(1)} collective-permute-done((bf16[256,256]{1,0:T(8,128)(2,1)S(1)}, bf16[256,256]{1,0:T(8,128)(2,1)S(1)}, u32[]{:S(2)}, u32[]{:S(2)}) %collective-permute-start.15) | collective-permute-done | bytes 131104 | tf_op jit(solution)/shard_map/ppermute | solution.py:153
  14.3 0.0 collective-permute-start.16
  14.3 0.0 collective-permute-done.1.refs_2_
  14.3 0.0 collective-permute-start.4
  14.3 0.0 collective-permute-done.refs_1_
  14.3 0.5 collective-permute-start.2
  14.8 0.0 collective-permute-done.7.refs_8_
  14.8 2.7 %collective-permute-start.11 = (bf16[256,256]{1,0:T(8,128)(2,1)S(1)}, bf16[256,256]{1,0:T(8,128)(2,1)S(1)}, u32[]{:S(2)}, u32[]{:S(2)}) collective-permute-start(bf16[256,256]{1,0:T(8,128)(2,1)S(1)} %collective-permute-done.7.refs_8_), channel_id=1, source_target_pairs={{0,32},{8,40},{16,48},{24,56},{32,64},{40,72},{48,80},{56,88},{64,... | collective-permute-start | bytes 393224 | tf_op jit(solution)/shard_map/ppermute | solution.py:153
  17.6 0.0 collective-permute-done.5.refs_6_
  17.6 0.5 collective-permute-start.9
  18.1 5.1 %collective-permute-done.16.refs_16_ = bf16[256,256]{1,0:T(8,128)(2,1)S(1)} collective-permute-done((bf16[256,256]{1,0:T(8,128)(2,1)S(1)}, bf16[256,256]{1,0:T(8,128)(2,1)S(1)}, u32[]{:S(2)}, u32[]{:S(2)}) %collective-permute-start.16) | collective-permute-done | bytes 131104 | tf_op jit(solution)/shard_map/ppermute | solution.py:153
  23.2 0.0 collective-permute-start.8
  23.2 0.0 collective-permute-done.4.refs_5_
  23.2 0.5 collective-permute-start.6
  23.7 0.0 collective-permute-done.2.refs_3_
  23.7 0.5 collective-permute-start.18
  24.2 0.0 collective-permute-done.11.refs_12_
  24.2 1.5 %collective-permute-start.13 = (bf16[256,256]{1,0:T(8,128)(2,1)S(1)}, bf16[256,256]{1,0:T(8,128)(2,1)S(1)}, u32[]{:S(2)}, u32[]{:S(2)}) collective-permute-start(bf16[256,256]{1,0:T(8,128)(2,1)S(1)} %collective-permute-done.11.refs_12_), channel_id=1, source_target_pairs={{0,16},{8,24},{16,0},{24,8},{32,48},{40,56},{48,32},{56,40},{64,80... | collective-permute-start | bytes 393224 | tf_op jit(solution)/shard_map/ppermute | solution.py:157
  25.7 0.0 collective-permute-done.9.refs_10_
  25.7 0.0 collective-permute-start.17
  25.7 0.5 collective-permute-start.12
  26.2 0.1 collective-permute-start.10
  26.3 3.7 %collective-permute-done.18.refs_18_ = bf16[256,256]{1,0:T(8,128)(2,1)S(1)} collective-permute-done((bf16[256,256]{1,0:T(8,128)(2,1)S(1)}, bf16[256,256]{1,0:T(8,128)(2,1)S(1)}, u32[]{:S(2)}, u32[]{:S(2)}) %collective-permute-start.18) | collective-permute-done | bytes 131104 | tf_op jit(solution)/shard_map/ppermute | solution.py:157
  30.0 0.0 collective-permute-start.19
  30.0 1.9 %collective-permute-done.13.refs_14_ = bf16[256,256]{1,0:T(8,128)(2,1)S(1)} collective-permute-done((bf16[256,256]{1,0:T(8,128)(2,1)S(1)}, bf16[256,256]{1,0:T(8,128)(2,1)S(1)}, u32[]{:S(2)}, u32[]{:S(2)}) %collective-permute-start.13) | collective-permute-done | bytes 131104 | tf_op jit(solution)/shard_map/ppermute | solution.py:157
  32.0 0.0 collective-permute-start.14
  32.0 0.7 pad_add_fusion.meta_ref
  32.7 0.0 collective-permute-done.12.refs_13_
  32.7 0.0 collective-permute-done.10.refs_11_
  32.7 0.6 collective-permute-done.14.refs_15_
  33.3 1.0 %copy-done = bf16[256,1024]{1,0:T(8,128)(2,1)S(1)} copy-done((bf16[256,1024]{1,0:T(8,128)(2,1)S(1)}, bf16[256,1024]{1,0:T(8,128)(2,1)}, u32[]{:S(2)}) %copy-start) | copy-done | bytes 524312
  34.4 14.8 %attention.1 = bf16[256,1024]{1,0:T(8,128)(2,1)S(1)} custom-call(s32[9]{0:T(128)S(1)} %pad_add_fusion.meta_ref, bf16[256,1024]{1,0:T(8,128)(2,1)S(1)} %copy-done, bf16[256,256]{1,0:T(8,128)(2,1)S(1)} %constant_dynamic-update-slice_fusion.refs_0_, bf16[256,256]{1,0:T(8,128)(2,1)S(1)} %collective-permute-done.refs_1_, ...), custom_call_target="tpu_custom_call" | custom-call | flops 5000000000 | bytes 4000000 | tf_op jit(solution)/shard_map/attention/pallas_call | solution.py:113
  49.2 1.6 %collective-permute-start.20 = (bf16[256,1024]{1,0:T(8,128)(2,1)S(1)}, bf16[256,1024]{1,0:T(8,128)(2,1)S(1)}, u32[]{:S(2)}, u32[]{:S(2)}) collective-permute-start(bf16[256,1024]{1,0:T(8,128)(2,1)S(1)} %attention.1), channel_id=1, source_target_pairs={{0,2},{1,3},{2,4},{3,5},{4,6},{5,7},{6,0},{7,1},{8,10},{9,11},{10,... | collective-permute-start | bytes 1572872 | tf_op jit(solution)/shard_map/ppermute | solution.py:153
  50.9 1.7 %collective-permute-start.22 = (bf16[256,1024]{1,0:T(8,128)(2,1)S(1)}, bf16[256,1024]{1,0:T(8,128)(2,1)S(1)}, u32[]{:S(2)}, u32[]{:S(2)}) collective-permute-start(bf16[256,1024]{1,0:T(8,128)(2,1)S(1)} %attention.1), channel_id=1, source_target_pairs={{0,6},{1,7},{2,0},{3,1},{4,2},{5,3},{6,4},{7,5},{8,14},{9,15},{10,... | collective-permute-start | bytes 1572872 | tf_op jit(solution)/shard_map/ppermute | solution.py:153
  52.6 2.1 %collective-permute-start.24 = (bf16[256,1024]{1,0:T(8,128)(2,1)S(1)}, bf16[256,1024]{1,0:T(8,128)(2,1)S(1)}, u32[]{:S(2)}, u32[]{:S(2)}) collective-permute-start(bf16[256,1024]{1,0:T(8,128)(2,1)S(1)} %attention.1), channel_id=1, source_target_pairs={{0,1},{1,0},{2,3},{3,2},{4,5},{5,4},{6,7},{7,6},{8,9},{9,8},{10,11... | collective-permute-start | bytes 1572872 | tf_op jit(solution)/shard_map/ppermute | solution.py:157
  54.7 9.5 %collective-permute-done.20.below_ref = bf16[256,1024]{1,0:T(8,128)(2,1)S(1)} collective-permute-done((bf16[256,1024]{1,0:T(8,128)(2,1)S(1)}, bf16[256,1024]{1,0:T(8,128)(2,1)S(1)}, u32[]{:S(2)}, u32[]{:S(2)}) %collective-permute-start.20) | collective-permute-done | bytes 524320 | tf_op jit(solution)/shard_map/ppermute | solution.py:153
  64.2 0.4 collective-permute-start.21
  64.6 0.0 collective-permute-done.22.above_ref
  64.6 3.0 %collective-permute-start.23 = (bf16[128,1024]{1,0:T(8,128)(2,1)S(1)}, bf16[128,1024]{1,0:T(8,128)(2,1)S(1)}, u32[]{:S(2)}, u32[]{:S(2)}) collective-permute-start(bf16[128,1024]{1,0:T(8,128)(2,1)S(1)} %slice.9), channel_id=1, source_target_pairs={{0,6},{1,7},{2,0},{3,1},{4,2},{5,3},{6,4},{7,5},{8,14},{9,15},{10,... | collective-permute-start | bytes 786440 | tf_op jit(solution)/shard_map/ppermute | solution.py:153
  67.6 1.3 %collective-permute-start.26 = (bf16[256,1024]{1,0:T(8,128)(2,1)S(1)}, bf16[256,1024]{1,0:T(8,128)(2,1)S(1)}, u32[]{:S(2)}, u32[]{:S(2)}) collective-permute-start(bf16[256,1024]{1,0:T(8,128)(2,1)S(1)} %collective-permute-done.24), channel_id=1, source_target_pairs={{0,6},{1,7},{2,0},{3,1},{4,2},{5,3},{6,4},{7,5},{8,14},{9,15},{10,... | collective-permute-start | bytes 1572872 | tf_op jit(solution)/shard_map/ppermute | solution.py:153
  68.9 0.8 collective-permute-start.25
  69.6 2.0 %fusion.13 = f32[256,512]{1,0:T(8,128)S(1)} fusion(bf16[256,1024]{1,0:T(8,128)(2,1)S(1)} %collective-permute-done.24, bf16[8192,512]{1,0:T(8,128)(2,1)} %param.9, s32[]{:T(128)S(6)} %select_n.57), kind=kOutput, calls=%fused_computation.15 | convolution fusion | flops 268435456 | bytes 2097156 | tf_op jit(solution)/shard_map/dot_general | solution.py:190
  71.7 2.9 %collective-permute-done.21.top_ref = bf16[128,1024]{1,0:T(8,128)(2,1)S(1)} collective-permute-done((bf16[128,1024]{1,0:T(8,128)(2,1)S(1)}, bf16[128,1024]{1,0:T(8,128)(2,1)S(1)}, u32[]{:S(2)}, u32[]{:S(2)}) %collective-permute-start.21) | collective-permute-done | bytes 262176 | tf_op jit(solution)/shard_map/ppermute | solution.py:153
  74.5 0.0 collective-permute-done.23.bottom_ref
  74.6 2.2 %collective-permute-start.27 = (bf16[256,1024]{1,0:T(8,128)(2,1)S(1)}, bf16[256,1024]{1,0:T(8,128)(2,1)S(1)}, u32[]{:S(2)}, u32[]{:S(2)}) collective-permute-start(bf16[256,1024]{1,0:T(8,128)(2,1)S(1)} %get-tuple-element.10), channel_id=1, source_target_pairs={{0,1},{1,0},{2,3},{3,2},{4,5},{5,4},{6,7},{7,6},{8,9},{9,8},{10,11... | collective-permute-start | bytes 1572872 | tf_op jit(solution)/shard_map/ppermute | solution.py:157
  76.8 1.7 %fusion.11 = f32[256,512]{1,0:T(8,128)S(1)} fusion(bf16[256,1024]{1,0:T(8,128)(2,1)S(1)} %get-tuple-element.10, bf16[8192,512]{1,0:T(8,128)(2,1)} %param.9, s32[]{:T(128)S(6)} %select_n.59), kind=kOutput, calls=%fused_computation.13 | convolution fusion | flops 268435456 | bytes 2097156 | tf_op jit(solution)/shard_map/dot_general | solution.py:190
  78.4 1.7 %fusion.15 = f32[256,512]{1,0:T(8,128)S(1)} fusion(bf16[256,1024]{1,0:T(8,128)(2,1)S(1)} %get-tuple-element.9, bf16[8192,512]{1,0:T(8,128)(2,1)} %param.9, s32[]{:T(128)S(6)} %select_n.56), kind=kOutput, calls=%fused_computation.17 | convolution fusion | flops 268435456 | bytes 2097156 | tf_op jit(solution)/shard_map/dot_general | solution.py:190
  80.1 1.7 %fusion.17 = f32[256,512]{1,0:T(8,128)S(1)} fusion(bf16[256,1024]{1,0:T(8,128)(2,1)S(1)} %get-tuple-element.8, bf16[8192,512]{1,0:T(8,128)(2,1)} %param.9, s32[]{:T(128)S(6)} %select_n.54), kind=kOutput, calls=%fused_computation.19 | convolution fusion | flops 268435456 | bytes 2097156 | tf_op jit(solution)/shard_map/dot_general | solution.py:190
  81.8 0.5 fusion.4
  82.2 1.0 %collective-permute-done.26 = bf16[256,1024]{1,0:T(8,128)(2,1)S(1)} collective-permute-done((bf16[256,1024]{1,0:T(8,128)(2,1)S(1)}, bf16[256,1024]{1,0:T(8,128)(2,1)S(1)}, u32[]{:S(2)}, u32[]{:S(2)}) %collective-permute-start.26) | collective-permute-done | bytes 524320 | tf_op jit(solution)/shard_map/ppermute | solution.py:153
  83.2 0.4 fusion.8
  83.7 2.4 %collective-permute-done.27 = bf16[256,1024]{1,0:T(8,128)(2,1)S(1)} collective-permute-done((bf16[256,1024]{1,0:T(8,128)(2,1)S(1)}, bf16[256,1024]{1,0:T(8,128)(2,1)S(1)}, u32[]{:S(2)}, u32[]{:S(2)}) %collective-permute-start.27) | collective-permute-done | bytes 524320 | tf_op jit(solution)/shard_map/ppermute | solution.py:157
  86.1 0.4 fusion.6
  86.6 0.0 collective-permute-done.25
  86.6 1.2 %fusion.5 = bf16[256,512]{1,0:T(8,128)(2,1)} fusion(f32[256,512]{1,0:T(8,128)S(1)} %fusion.6, f32[256,512]{1,0:T(8,128)S(1)} %fusion.8, f32[256,512]{1,0:T(8,128)S(1)} %fusion.4, bf16[256,1024]{1,0:T(8,128)(2,1)S(1)} %collective-permute-done.25, bf16[8192,512]{1,0:T(8,128)(2,1)S(1)} %copy-done.1, s32[]{:T(128)S(6)} %select_n.60), kind=kOutput, calls=%fused_computation.7 | convolution fusion | flops 268959744 | bytes 3407876 | tf_op jit(solution)/shard_map/dot_general | solution.py:190
  (11 shorter events, 0.1 us)
Async XLA Ops:
  1.7 6.0 %collective-permute-start.3 = (bf16[256,256]{1,0:T(8,128)(2,1)S(1)}, bf16[256,256]{1,0:T(8,128)(2,1)S(1)}, u32[]{:S(2)}, u32[]{:S(2)}) collective-permute-start(bf16[256,256]{1,0:T(8,128)(2,1)S(1)} %constant_dynamic-update-slice_fusion.refs_0_), channel_id=1, source_target_pairs={{0,32},{8,40},{16,48},{24,56},{32,64},{40,72},{48,80},{56,88},{64,... | collective-permute-start | bytes 393224 | tf_op jit(solution)/shard_map/ppermute | solution.py:153
  4.9 9.4 %collective-permute-start.15 = (bf16[256,256]{1,0:T(8,128)(2,1)S(1)}, bf16[256,256]{1,0:T(8,128)(2,1)S(1)}, u32[]{:S(2)}, u32[]{:S(2)}) collective-permute-start(bf16[256,256]{1,0:T(8,128)(2,1)S(1)} %constant_dynamic-update-slice_fusion.refs_0_), channel_id=1, source_target_pairs={{0,192},{8,200},{16,208},{24,216},{32,224},{40,232},{48,240},{56,2... | collective-permute-start | bytes 393224 | tf_op jit(solution)/shard_map/ppermute | solution.py:153
  4.9 9.4 %collective-permute-start.1 = (bf16[256,256]{1,0:T(8,128)(2,1)S(1)}, bf16[256,256]{1,0:T(8,128)(2,1)S(1)}, u32[]{:S(2)}, u32[]{:S(2)}) collective-permute-start(bf16[256,256]{1,0:T(8,128)(2,1)S(1)} %constant_dynamic-update-slice_fusion.refs_0_), channel_id=1, source_target_pairs={{0,16},{8,24},{16,0},{24,8},{32,48},{40,56},{48,32},{56,40},{64,80... | collective-permute-start | bytes 393224 | tf_op jit(solution)/shard_map/ppermute | solution.py:157
  5.5 8.8 %collective-permute-start = (bf16[256,256]{1,0:T(8,128)(2,1)S(1)}, bf16[256,256]{1,0:T(8,128)(2,1)S(1)}, u32[]{:S(2)}, u32[]{:S(2)}) collective-permute-start(bf16[256,256]{1,0:T(8,128)(2,1)S(1)} %constant_dynamic-update-slice_fusion.refs_0_), channel_id=1, source_target_pairs={{0,8},{8,0},{16,24},{24,16},{32,40},{40,32},{48,56},{56,48},{64,72... | collective-permute-start | bytes 393224 | tf_op jit(solution)/shard_map/ppermute | solution.py:157
  7.7 7.1 %collective-permute-start.7 = (bf16[256,256]{1,0:T(8,128)(2,1)S(1)}, bf16[256,256]{1,0:T(8,128)(2,1)S(1)}, u32[]{:S(2)}, u32[]{:S(2)}) collective-permute-start(bf16[256,256]{1,0:T(8,128)(2,1)S(1)} %collective-permute-done.3.refs_4_), channel_id=1, source_target_pairs={{0,32},{8,40},{16,48},{24,56},{32,64},{40,72},{48,80},{56,88},{64,... | collective-permute-start | bytes 393224 | tf_op jit(solution)/shard_map/ppermute | solution.py:153
  11.4 6.2 %collective-permute-start.5 = (bf16[256,256]{1,0:T(8,128)(2,1)S(1)}, bf16[256,256]{1,0:T(8,128)(2,1)S(1)}, u32[]{:S(2)}, u32[]{:S(2)}) collective-permute-start(bf16[256,256]{1,0:T(8,128)(2,1)S(1)} %collective-permute-done.3.refs_4_), channel_id=1, source_target_pairs={{0,16},{8,24},{16,0},{24,8},{32,48},{40,56},{48,32},{56,40},{64,80... | collective-permute-start | bytes 393224 | tf_op jit(solution)/shard_map/ppermute | solution.py:157
  14.3 8.9 %collective-permute-start.16 = (bf16[256,256]{1,0:T(8,128)(2,1)S(1)}, bf16[256,256]{1,0:T(8,128)(2,1)S(1)}, u32[]{:S(2)}, u32[]{:S(2)}) collective-permute-start(bf16[256,256]{1,0:T(8,128)(2,1)S(1)} %collective-permute-done.15), channel_id=1, source_target_pairs={{0,192},{8,200},{16,208},{24,216},{32,224},{40,232},{48,240},{56,2... | collective-permute-start | bytes 393224 | tf_op jit(solution)/shard_map/ppermute | solution.py:153
  14.3 8.9 %collective-permute-start.4 = (bf16[256,256]{1,0:T(8,128)(2,1)S(1)}, bf16[256,256]{1,0:T(8,128)(2,1)S(1)}, u32[]{:S(2)}, u32[]{:S(2)}) collective-permute-start(bf16[256,256]{1,0:T(8,128)(2,1)S(1)} %collective-permute-done.3.refs_4_), channel_id=1, source_target_pairs={{0,8},{8,0},{16,24},{24,16},{32,40},{40,32},{48,56},{56,48},{64,72... | collective-permute-start | bytes 393224 | tf_op jit(solution)/shard_map/ppermute | solution.py:157
  14.3 9.4 %collective-permute-start.2 = (bf16[256,256]{1,0:T(8,128)(2,1)S(1)}, bf16[256,256]{1,0:T(8,128)(2,1)S(1)}, u32[]{:S(2)}, u32[]{:S(2)}) collective-permute-start(bf16[256,256]{1,0:T(8,128)(2,1)S(1)} %collective-permute-done.1.refs_2_), channel_id=1, source_target_pairs={{0,8},{8,0},{16,24},{24,16},{32,40},{40,32},{48,56},{56,48},{64,72... | collective-permute-start | bytes 393224 | tf_op jit(solution)/shard_map/ppermute | solution.py:157
  14.8 9.4 %collective-permute-start.11 = (bf16[256,256]{1,0:T(8,128)(2,1)S(1)}, bf16[256,256]{1,0:T(8,128)(2,1)S(1)}, u32[]{:S(2)}, u32[]{:S(2)}) collective-permute-start(bf16[256,256]{1,0:T(8,128)(2,1)S(1)} %collective-permute-done.7.refs_8_), channel_id=1, source_target_pairs={{0,32},{8,40},{16,48},{24,56},{32,64},{40,72},{48,80},{56,88},{64,... | collective-permute-start | bytes 393224 | tf_op jit(solution)/shard_map/ppermute | solution.py:153
  17.6 8.2 %collective-permute-start.9 = (bf16[256,256]{1,0:T(8,128)(2,1)S(1)}, bf16[256,256]{1,0:T(8,128)(2,1)S(1)}, u32[]{:S(2)}, u32[]{:S(2)}) collective-permute-start(bf16[256,256]{1,0:T(8,128)(2,1)S(1)} %collective-permute-done.7.refs_8_), channel_id=1, source_target_pairs={{0,16},{8,24},{16,0},{24,8},{32,48},{40,56},{48,32},{56,40},{64,80... | collective-permute-start | bytes 393224 | tf_op jit(solution)/shard_map/ppermute | solution.py:157
  23.2 2.6 %collective-permute-start.8 = (bf16[256,256]{1,0:T(8,128)(2,1)S(1)}, bf16[256,256]{1,0:T(8,128)(2,1)S(1)}, u32[]{:S(2)}, u32[]{:S(2)}) collective-permute-start(bf16[256,256]{1,0:T(8,128)(2,1)S(1)} %collective-permute-done.7.refs_8_), channel_id=1, source_target_pairs={{0,8},{8,0},{16,24},{24,16},{32,40},{40,32},{48,56},{56,48},{64,72... | collective-permute-start | bytes 393224 | tf_op jit(solution)/shard_map/ppermute | solution.py:157
  23.2 3.1 %collective-permute-start.6 = (bf16[256,256]{1,0:T(8,128)(2,1)S(1)}, bf16[256,256]{1,0:T(8,128)(2,1)S(1)}, u32[]{:S(2)}, u32[]{:S(2)}) collective-permute-start(bf16[256,256]{1,0:T(8,128)(2,1)S(1)} %collective-permute-done.5.refs_6_), channel_id=1, source_target_pairs={{0,8},{8,0},{16,24},{24,16},{32,40},{40,32},{48,56},{56,48},{64,72... | collective-permute-start | bytes 393224 | tf_op jit(solution)/shard_map/ppermute | solution.py:157
  23.7 6.4 %collective-permute-start.18 = (bf16[256,256]{1,0:T(8,128)(2,1)S(1)}, bf16[256,256]{1,0:T(8,128)(2,1)S(1)}, u32[]{:S(2)}, u32[]{:S(2)}) collective-permute-start(bf16[256,256]{1,0:T(8,128)(2,1)S(1)} %collective-permute-done.16.refs_16_), channel_id=1, source_target_pairs={{0,16},{8,24},{16,0},{24,8},{32,48},{40,56},{48,32},{56,40},{64,80... | collective-permute-start | bytes 393224 | tf_op jit(solution)/shard_map/ppermute | solution.py:157
  24.2 7.8 %collective-permute-start.13 = (bf16[256,256]{1,0:T(8,128)(2,1)S(1)}, bf16[256,256]{1,0:T(8,128)(2,1)S(1)}, u32[]{:S(2)}, u32[]{:S(2)}) collective-permute-start(bf16[256,256]{1,0:T(8,128)(2,1)S(1)} %collective-permute-done.11.refs_12_), channel_id=1, source_target_pairs={{0,16},{8,24},{16,0},{24,8},{32,48},{40,56},{48,32},{56,40},{64,80... | collective-permute-start | bytes 393224 | tf_op jit(solution)/shard_map/ppermute | solution.py:157
  25.7 7.0 %collective-permute-start.17 = (bf16[256,256]{1,0:T(8,128)(2,1)S(1)}, bf16[256,256]{1,0:T(8,128)(2,1)S(1)}, u32[]{:S(2)}, u32[]{:S(2)}) collective-permute-start(bf16[256,256]{1,0:T(8,128)(2,1)S(1)} %collective-permute-done.16.refs_16_), channel_id=1, source_target_pairs={{0,8},{8,0},{16,24},{24,16},{32,40},{40,32},{48,56},{56,48},{64,72... | collective-permute-start | bytes 393224 | tf_op jit(solution)/shard_map/ppermute | solution.py:157
  25.7 7.0 %collective-permute-start.12 = (bf16[256,256]{1,0:T(8,128)(2,1)S(1)}, bf16[256,256]{1,0:T(8,128)(2,1)S(1)}, u32[]{:S(2)}, u32[]{:S(2)}) collective-permute-start(bf16[256,256]{1,0:T(8,128)(2,1)S(1)} %collective-permute-done.11.refs_12_), channel_id=1, source_target_pairs={{0,8},{8,0},{16,24},{24,16},{32,40},{40,32},{48,56},{56,48},{64,72... | collective-permute-start | bytes 393224 | tf_op jit(solution)/shard_map/ppermute | solution.py:157
  26.2 6.5 %collective-permute-start.10 = (bf16[256,256]{1,0:T(8,128)(2,1)S(1)}, bf16[256,256]{1,0:T(8,128)(2,1)S(1)}, u32[]{:S(2)}, u32[]{:S(2)}) collective-permute-start(bf16[256,256]{1,0:T(8,128)(2,1)S(1)} %collective-permute-done.9.refs_10_), channel_id=1, source_target_pairs={{0,8},{8,0},{16,24},{24,16},{32,40},{40,32},{48,56},{56,48},{64,72... | collective-permute-start | bytes 393224 | tf_op jit(solution)/shard_map/ppermute | solution.py:157
  30.0 2.7 %collective-permute-start.19 = (bf16[256,256]{1,0:T(8,128)(2,1)S(1)}, bf16[256,256]{1,0:T(8,128)(2,1)S(1)}, u32[]{:S(2)}, u32[]{:S(2)}) collective-permute-start(bf16[256,256]{1,0:T(8,128)(2,1)S(1)} %collective-permute-done.18.refs_18_), channel_id=1, source_target_pairs={{0,8},{8,0},{16,24},{24,16},{32,40},{40,32},{48,56},{56,48},{64,72... | collective-permute-start | bytes 393224 | tf_op jit(solution)/shard_map/ppermute | solution.py:157
  32.0 1.3 %collective-permute-start.14 = (bf16[256,256]{1,0:T(8,128)(2,1)S(1)}, bf16[256,256]{1,0:T(8,128)(2,1)S(1)}, u32[]{:S(2)}, u32[]{:S(2)}) collective-permute-start(bf16[256,256]{1,0:T(8,128)(2,1)S(1)} %collective-permute-done.13.refs_14_), channel_id=1, source_target_pairs={{0,8},{8,0},{16,24},{24,16},{32,40},{40,32},{48,56},{56,48},{64,72... | collective-permute-start | bytes 393224 | tf_op jit(solution)/shard_map/ppermute | solution.py:157
  33.3 1.0 %copy-start = (bf16[256,1024]{1,0:T(8,128)(2,1)S(1)}, bf16[256,1024]{1,0:T(8,128)(2,1)}, u32[]{:S(2)}) copy-start(bf16[256,1024]{1,0:T(8,128)(2,1)} %q_ref.1) | copy-start | bytes 1572868
  49.2 14.9 %collective-permute-start.20 = (bf16[256,1024]{1,0:T(8,128)(2,1)S(1)}, bf16[256,1024]{1,0:T(8,128)(2,1)S(1)}, u32[]{:S(2)}, u32[]{:S(2)}) collective-permute-start(bf16[256,1024]{1,0:T(8,128)(2,1)S(1)} %attention.1), channel_id=1, source_target_pairs={{0,2},{1,3},{2,4},{3,5},{4,6},{5,7},{6,0},{7,1},{8,10},{9,11},{10,... | collective-permute-start | bytes 1572872 | tf_op jit(solution)/shard_map/ppermute | solution.py:153
  50.9 13.7 %collective-permute-start.22 = (bf16[256,1024]{1,0:T(8,128)(2,1)S(1)}, bf16[256,1024]{1,0:T(8,128)(2,1)S(1)}, u32[]{:S(2)}, u32[]{:S(2)}) collective-permute-start(bf16[256,1024]{1,0:T(8,128)(2,1)S(1)} %attention.1), channel_id=1, source_target_pairs={{0,6},{1,7},{2,0},{3,1},{4,2},{5,3},{6,4},{7,5},{8,14},{9,15},{10,... | collective-permute-start | bytes 1572872 | tf_op jit(solution)/shard_map/ppermute | solution.py:153
  52.6 15.1 %collective-permute-start.24 = (bf16[256,1024]{1,0:T(8,128)(2,1)S(1)}, bf16[256,1024]{1,0:T(8,128)(2,1)S(1)}, u32[]{:S(2)}, u32[]{:S(2)}) collective-permute-start(bf16[256,1024]{1,0:T(8,128)(2,1)S(1)} %attention.1), channel_id=1, source_target_pairs={{0,1},{1,0},{2,3},{3,2},{4,5},{5,4},{6,7},{7,6},{8,9},{9,8},{10,11... | collective-permute-start | bytes 1572872 | tf_op jit(solution)/shard_map/ppermute | solution.py:157
  64.2 10.3 %collective-permute-start.21 = (bf16[128,1024]{1,0:T(8,128)(2,1)S(1)}, bf16[128,1024]{1,0:T(8,128)(2,1)S(1)}, u32[]{:S(2)}, u32[]{:S(2)}) collective-permute-start(bf16[128,1024]{1,0:T(8,128)(2,1)S(1)} %slice.8), channel_id=1, source_target_pairs={{0,2},{1,3},{2,4},{3,5},{4,6},{5,7},{6,0},{7,1},{8,10},{9,11},{10,... | collective-permute-start | bytes 786440 | tf_op jit(solution)/shard_map/ppermute | solution.py:153
  64.6 9.9 %collective-permute-start.23 = (bf16[128,1024]{1,0:T(8,128)(2,1)S(1)}, bf16[128,1024]{1,0:T(8,128)(2,1)S(1)}, u32[]{:S(2)}, u32[]{:S(2)}) collective-permute-start(bf16[128,1024]{1,0:T(8,128)(2,1)S(1)} %slice.9), channel_id=1, source_target_pairs={{0,6},{1,7},{2,0},{3,1},{4,2},{5,3},{6,4},{7,5},{8,14},{9,15},{10,... | collective-permute-start | bytes 786440 | tf_op jit(solution)/shard_map/ppermute | solution.py:153
  67.6 14.1 %copy-start.1 = (bf16[8192,512]{1,0:T(8,128)(2,1)S(1)}, bf16[8192,512]{1,0:T(8,128)(2,1)}, u32[]{:S(2)}) copy-start(bf16[8192,512]{1,0:T(8,128)(2,1)} %param.9) | copy-start | bytes 25165828
  67.6 15.6 %collective-permute-start.26 = (bf16[256,1024]{1,0:T(8,128)(2,1)S(1)}, bf16[256,1024]{1,0:T(8,128)(2,1)S(1)}, u32[]{:S(2)}, u32[]{:S(2)}) collective-permute-start(bf16[256,1024]{1,0:T(8,128)(2,1)S(1)} %collective-permute-done.24), channel_id=1, source_target_pairs={{0,6},{1,7},{2,0},{3,1},{4,2},{5,3},{6,4},{7,5},{8,14},{9,15},{10,... | collective-permute-start | bytes 1572872 | tf_op jit(solution)/shard_map/ppermute | solution.py:153
  68.9 17.7 %collective-permute-start.25 = (bf16[256,1024]{1,0:T(8,128)(2,1)S(1)}, bf16[256,1024]{1,0:T(8,128)(2,1)S(1)}, u32[]{:S(2)}, u32[]{:S(2)}) collective-permute-start(bf16[256,1024]{1,0:T(8,128)(2,1)S(1)} %collective-permute-done.24), channel_id=1, source_target_pairs={{0,2},{1,3},{2,4},{3,5},{4,6},{5,7},{6,0},{7,1},{8,10},{9,11},{10,... | collective-permute-start | bytes 1572872 | tf_op jit(solution)/shard_map/ppermute | solution.py:153
  74.6 11.6 %collective-permute-start.27 = (bf16[256,1024]{1,0:T(8,128)(2,1)S(1)}, bf16[256,1024]{1,0:T(8,128)(2,1)S(1)}, u32[]{:S(2)}, u32[]{:S(2)}) collective-permute-start(bf16[256,1024]{1,0:T(8,128)(2,1)S(1)} %get-tuple-element.10), channel_id=1, source_target_pairs={{0,1},{1,0},{2,3},{3,2},{4,5},{5,4},{6,7},{7,6},{8,9},{9,8},{10,11... | collective-permute-start | bytes 1572872 | tf_op jit(solution)/shard_map/ppermute | solution.py:157
